TPU v7x, 32 devices: a whole 2x2x4 slice. The times are simulated.
32 devices in a mesh: tm: 4 (over z), space: 8 (over y, x, core).
Axes of the slice: x: 2, y: 2, z: 4, core: 2. Of those that a mesh axis runs over, the one named last changes fastest.
Arguments:
- starts: float32 [4, 8, 256, 1024], P('tm', None, 'space'), may hold values from -3 to 3
- diffusivity: bfloat16 [8, 256, 1024], P(None, 'space'), may hold values from 0.25 to 1
- reaction: bfloat16 [8, 256, 1024], P(None, 'space'), may hold values from 0.5 to 2
Outputs:
- next_starts: float32 [4, 8, 256, 1024], P('tm', None, 'space')
All inputs are finite; a program needn't handle non-finite values.
Results may differ from a plain program's by a relative error of at most 0.0003.
Values sent between devices are 32-bit elements; how exact they have to be, the bound alone decides.
No kernel may reach another device: no remote copies, remote signals or barrier semaphores. Data moves between devices by JAX's collectives and lax.ppermute only.
A program may use at most 128 MiB of HBM per device.

v0:
```python
import jax
import jax.numpy as jnp
from jax import lax
from jax.sharding import PartitionSpec as P

FINE = 4
COARSE = 2


DT = 0.05
VEL = 0.5


def padded(block, sides, width):
    for axis, dim in sides:
        count = lax.axis_size(axis)
        forward = [(i, i + 1) for i in range(count - 1)]
        backward = [(target, source) for source, target in forward]
        low = lax.ppermute(
            lax.slice_in_dim(block, block.shape[dim] - width, None, axis=dim), axis, forward
        )
        high = lax.ppermute(lax.slice_in_dim(block, 0, width, axis=dim), axis, backward)
        block = jnp.concatenate([low, block, high], axis=dim)
    return block


def from_behind(value, axis, steps):
    count = lax.axis_size(axis)
    first, last = (max(0, -steps), min(count, count - steps))
    return lax.ppermute(value, axis, [(source, source + steps) for source in range(first, last)])


def restrict(values):
    layers, height, breadth = values.shape
    return values.reshape(layers, height // 4, 4, breadth // 4, 4).mean(axis=(2, 4))


def fine_update(values, rowed, diffusion, growth):
    upper_row = rowed[:, 2:, :]
    lower_row = rowed[:, :-2, :]
    z_padded = jnp.pad(values, ((1, 1), (0, 0), (0, 0)))
    x_padded = jnp.pad(values, ((0, 0), (0, 0), (1, 1)))
    z_above = z_padded[2:]
    z_below = z_padded[:-2]
    x_next = x_padded[:, :, 2:]
    x_prev = x_padded[:, :, :-2]
    laplace = z_above + z_below + upper_row + lower_row + x_next + x_prev - 6.0 * values
    drift = VEL * 0.5 * (upper_row - lower_row + (x_next - x_prev))
    return values + DT * (
        diffusion * laplace - drift + growth * (values - values * values * values / 3.0)
    )


def coarse_update(values, rowed, diffusion, growth):
    upper_row = rowed[:, 2:, :]
    lower_row = rowed[:, :-2, :]
    z_padded = jnp.pad(values, ((1, 1), (0, 0), (0, 0)))
    x_padded = jnp.pad(values, ((0, 0), (0, 0), (1, 1)))
    x_next = x_padded[:, :, 2:]
    x_prev = x_padded[:, :, :-2]
    vertical = z_padded[2:] + z_padded[:-2] - 2.0 * values
    level = (upper_row + lower_row + x_next + x_prev - 4.0 * values) / 16.0
    drift = VEL * (upper_row - lower_row + (x_next - x_prev)) / 8.0
    return values + 2.0 * DT * (
        diffusion * (vertical + level) - drift + growth * (values - values * values * values / 3.0)
    )


def per_device(starts, diffusivity, reaction):
    diffusion = diffusivity.astype(jnp.float32)
    growth = reaction.astype(jnp.float32)
    coarse_diff = restrict(diffusion)
    coarse_grow = restrict(growth)
    initial = starts[0]
    fine_end = initial
    for sweep in range(FINE):
        rowed = padded(fine_end, (("space", 1),), 1)
        fine_end = fine_update(fine_end, rowed, diffusion, growth)

    def advance(values):
        for sweep in range(COARSE):
            rowed = padded(values, (("space", 1),), 1)
            values = coarse_update(values, rowed, coarse_diff, coarse_grow)
        return values

    end_coarse = restrict(fine_end)
    slice_id = lax.axis_index("tm")
    jump_term = end_coarse - jnp.where(slice_id > 0, advance(restrict(initial)), 0.0)
    slices = lax.axis_size("tm")

    def relay(position, state_now):
        incoming = from_behind(state_now, "tm", 1)
        return jnp.where(slice_id > 0, advance(incoming), 0.0) + jump_term

    own_state = lax.fori_loop(0, slices - 1, relay, jump_term)
    correction = own_state - end_coarse
    prolonged = jnp.repeat(jnp.repeat(correction, 4, axis=1), 4, axis=2)
    return (fine_end + prolonged)[None]


def solution(mesh):
    in_specs = (P("tm", None, "space", None), P(None, "space", None), P(None, "space", None))
    out_specs = P("tm", None, "space", None)
    return jax.shard_map(
        per_device, mesh=mesh, in_specs=in_specs, out_specs=out_specs, check_vma=False
    )
```

profile of v0, /device:TPU:12, one launch (start us, length us, event | category | flops | bytes accessed | tf_op | source)
XLA Modules:
  0.0 195.8 jit_solution(7978799082765213457)
XLA Ops:
  1.1 2.8 %collective-permute-start.5 = (f32[8,1,1024]{2,0,1:T(8,128)S(1)}, f32[8,1,1024]{2,0,1:T(8,128)S(1)}, u32[]{:S(2)}, u32[]{:S(2)}) collective-permute-start(f32[8,1,1024]{2,0,1:T(8,128)S(1)} %copy.205), channel_id=1, source_target_pairs={{1,0},{2,1},{3,2},{4,3},{5,4},{6,5},{7,6},{9,8},{10,9},{11,10},{12... | collective-permute-start | bytes 98312 | tf_op jit(solution)/shard_map/ppermute | solution.py:22
  3.9 1.9 collective-permute-start.6
  5.8 9.8 %copy.223 = f32[1,8,32,1024]{1,3,2,0:T(8,128)} copy(f32[1,8,32,1024]{3,2,1,0:T(8,128)} %param.5) | data formatting | bytes 2097152 | tf_op args[0]
  15.7 10.1 %reduce_sum.37 = f32[8,8,256]{0,2,1:T(8,128)S(1)} reduce(f32[8,8,4,256,4]{0,4,3,2,1:T(4,128)} %bitcast.12, f32[]{:T(128)} %constant.106.clone.1), dimensions={2,4}, to_apply=%region_1.0 | reduce | flops 245760 | bytes 1114116 | tf_op jit(solution)/shard_map/reduce_sum | solution.py:35
  28.3 4.5 %collective-permute-start.7 = (f32[8,1,1024]{2,0,1:T(8,128)S(1)}, f32[8,1,1024]{2,0,1:T(8,128)S(1)}, u32[]{:S(2)}, u32[]{:S(2)}) collective-permute-start(f32[8,1,1024]{2,0,1:T(8,128)S(1)} %copy.209), channel_id=1, source_target_pairs={{1,0},{2,1},{3,2},{4,3},{5,4},{6,5},{7,6},{9,8},{10,9},{11,10},{12... | collective-permute-start | bytes 98312 | tf_op jit(solution)/shard_map/ppermute | solution.py:22
  32.8 1.9 collective-permute-start.8
  34.8 4.5 %collective-permute-start.13 = (f32[8,1,256]{2,1,0:T(1,128)S(1)}, f32[8,1,256]{2,1,0:T(1,128)}, u32[]{:S(2)}, u32[]{:S(2)}) collective-permute-start(f32[8,1,256]{2,1,0:T(1,128)S(1)} %get-tuple-element.156), channel_id=1, source_target_pairs={{1,0},{2,1},{3,2},{4,3},{5,4},{6,5},{7,6},{9,8},{10,9},{11,10},{12... | collective-permute-start | bytes 24584 | tf_op jit(solution)/shard_map/ppermute | solution.py:22
  39.3 1.9 collective-permute-start.14
  41.3 7.6 %copy.225 = f32[8,32,1024]{0,2,1:T(8,128)} copy(bf16[8,32,1024]{2,1,0:T(8,128)(2,1)S(1)} %copy-done.1) | data formatting | bytes 1572864 | tf_op jit(solution)/shard_map/convert_element_type | solution.py:70
  48.8 7.5 %copy.229 = f32[8,32,1024]{0,2,1:T(8,128)} copy(bf16[8,32,1024]{2,1,0:T(8,128)(2,1)S(1)} %copy-done) | data formatting | bytes 1572864 | tf_op jit(solution)/shard_map/convert_element_type | solution.py:71
  56.4 10.1 %reduce_sum.38 = f32[8,8,256]{0,2,1:T(8,128)S(1)} reduce(f32[8,8,4,256,4]{0,4,3,2,1:T(4,128)} %bitcast.10, f32[]{:T(128)} %constant.106.clone.1), dimensions={2,4}, to_apply=%region_2.3 | reduce | flops 245760 | bytes 1114116 | tf_op jit(solution)/shard_map/reduce_sum | solution.py:35
  66.7 10.1 %reduce_sum.39 = f32[8,8,256]{0,2,1:T(8,128)S(1)} reduce(f32[8,8,4,256,4]{0,4,3,2,1:T(4,128)} %bitcast.9, f32[]{:T(128)} %constant.106.clone.1), dimensions={2,4}, to_apply=%region_3.4 | reduce | flops 245760 | bytes 1114116 | tf_op jit(solution)/shard_map/reduce_sum | solution.py:35
  78.5 4.5 %collective-permute-start.9 = (f32[8,1,1024]{2,0,1:T(8,128)S(1)}, f32[8,1,1024]{2,0,1:T(8,128)S(1)}, u32[]{:S(2)}, u32[]{:S(2)}) collective-permute-start(f32[8,1,1024]{2,0,1:T(8,128)S(1)} %copy.213), channel_id=1, source_target_pairs={{1,0},{2,1},{3,2},{4,3},{5,4},{6,5},{7,6},{9,8},{10,9},{11,10},{12... | collective-permute-start | bytes 98312 | tf_op jit(solution)/shard_map/ppermute | solution.py:22
  83.0 1.9 collective-permute-start.10
  85.9 3.3 %collective-permute-done.10 = f32[8,1,1024]{2,0,1:T(8,128)S(1)} collective-permute-done((f32[8,1,1024]{2,0,1:T(8,128)S(1)}, f32[8,1,1024]{2,0,1:T(8,128)S(1)}, u32[]{:S(2)}, u32[]{:S(2)}) %collective-permute-start.10) | collective-permute-done | bytes 32800 | tf_op jit(solution)/shard_map/ppermute | solution.py:19
  90.4 1.9 collective-permute-start.11
  92.4 2.4 %collective-permute-start.12 = (f32[8,1,1024]{2,0,1:T(8,128)S(1)}, f32[8,1,1024]{2,0,1:T(8,128)S(1)}, u32[]{:S(2)}, u32[]{:S(2)}) collective-permute-start(f32[8,1,1024]{2,0,1:T(8,128)S(1)} %copy.219), channel_id=1, source_target_pairs={{0,1},{1,2},{2,3},{3,4},{4,5},{5,6},{6,7},{8,9},{9,10},{10,11},{11... | collective-permute-start | bytes 98312 | tf_op jit(solution)/shard_map/ppermute | solution.py:19
  94.8 4.1 %collective-permute-start.15 = (f32[8,1,256]{2,1,0:T(1,128)S(1)}, f32[8,1,256]{2,1,0:T(1,128)S(1)}, u32[]{:S(2)}, u32[]{:S(2)}) collective-permute-start(f32[8,1,256]{2,1,0:T(1,128)S(1)} %get-tuple-element.154), channel_id=1, source_target_pairs={{1,0},{2,1},{3,2},{4,3},{5,4},{6,5},{7,6},{9,8},{10,9},{11,10},{12... | collective-permute-start | bytes 24584 | tf_op jit(solution)/shard_map/ppermute | solution.py:22
  98.9 2.1 %collective-permute-start.16 = (f32[8,1,256]{2,1,0:T(1,128)S(1)}, f32[8,1,256]{2,1,0:T(1,128)S(1)}, u32[]{:S(2)}, u32[]{:S(2)}) collective-permute-start(f32[8,1,256]{2,1,0:T(1,128)S(1)} %get-tuple-element.153), channel_id=1, source_target_pairs={{0,1},{1,2},{2,3},{3,4},{4,5},{5,6},{6,7},{8,9},{9,10},{10,11},{11... | collective-permute-start | bytes 24584 | tf_op jit(solution)/shard_map/ppermute | solution.py:19
  102.3 8.6 %copy.221 = f32[8,32,1024]{0,2,1:T(8,128)} copy(f32[8,32,1024]{2,1,0:T(8,128)S(1)} %fusion.67) | data formatting | bytes 2097152 | tf_op jit(solution)/shard_map/add | solution.py:49
  110.9 10.1 %reduce_sum.36 = f32[8,8,256]{0,2,1:T(8,128)S(1)} reduce(f32[8,8,4,256,4]{0,4,3,2,1:T(4,128)} %bitcast.11, f32[]{:T(128)} %constant.106.clone.1), dimensions={2,4}, to_apply=%region_0.0 | reduce | flops 245760 | bytes 1114116 | tf_op jit(solution)/shard_map/reduce_sum | solution.py:35
  121.5 67.6 %while.13 = (s32[]{:T(128)}, f32[8,8,256]{2,1,0:T(8,128)S(1)}, pred[]{:T(512)}, f32[8,8,256]{2,1,0:T(8,128)S(1)}, f32[8,8,256]{2,1,0:T(8,128)S(1)}, /*index=5*/f32[8,8,256]{2,1,0:T(8,128)S(1)}, s32[]{:T(128)}) while((s32[]{:T(128)}, f32[8,8,256]{2,1,0:T(8,128)S(1)}, pred[]{:T(512)}, f32[8,8,256]{2,1,0:T(8,128)S(1)}, ...), condition=%wide.region_5.6_spmd, body=%wide.region_4.5_spmd.sunk | while | flops 884738 | bytes 1081622 | solution.py:95
  121.5 3.5 %collective-permute-start = (f32[8,8,256]{2,1,0:T(8,128)S(1)}, f32[8,8,256]{2,1,0:T(8,128)S(1)}, u32[]{:S(2)}, u32[]{:S(2)}) collective-permute-start(f32[8,8,256]{2,1,0:T(8,128)S(1)} %get-tuple-element.210), channel_id=1, source_target_pairs={{0,8},{8,16},{16,24},{1,9},{9,17},{17,25},{2,10},{10,18},{18,26},{... | collective-permute-start | bytes 196616 | tf_op jit(solution)/shard_map/while/body/eval_jaxpr/ppermute | solution.py:30
  125.0 2.7 %collective-permute-done = f32[8,8,256]{2,1,0:T(8,128)S(1)} collective-permute-done((f32[8,8,256]{2,1,0:T(8,128)S(1)}, f32[8,8,256]{2,1,0:T(8,128)S(1)}, u32[]{:S(2)}, u32[]{:S(2)}) %collective-permute-start) | collective-permute-done | bytes 65568 | tf_op jit(solution)/shard_map/while/body/eval_jaxpr/ppermute | solution.py:30
  127.6 3.4 %collective-permute-start.1 = (f32[8,1,256]{2,1,0:T(1,128)S(1)}, f32[8,1,256]{2,1,0:T(1,128)S(1)}, u32[]{:S(2)}, u32[]{:S(2)}) collective-permute-start(f32[8,1,256]{2,1,0:T(1,128)S(1)} %get-tuple-element.198), channel_id=1, source_target_pairs={{1,0},{2,1},{3,2},{4,3},{5,4},{6,5},{7,6},{9,8},{10,9},{11,10},{12... | collective-permute-start | bytes 24584 | tf_op jit(solution)/shard_map/while/body/eval_jaxpr/ppermute | solution.py:22
  131.0 1.9 collective-permute-start.2
  133.0 3.9 %collective-permute-done.2 = f32[8,1,256]{2,1,0:T(1,128)S(1)} collective-permute-done((f32[8,1,256]{2,1,0:T(1,128)S(1)}, f32[8,1,256]{2,1,0:T(1,128)S(1)}, u32[]{:S(2)}, u32[]{:S(2)}) %collective-permute-start.2) | collective-permute-done | bytes 8224 | tf_op jit(solution)/shard_map/while/body/eval_jaxpr/ppermute | solution.py:19
  137.1 1.9 collective-permute-start.3
  139.0 2.4 %collective-permute-start.4 = (f32[8,1,256]{2,1,0:T(1,128)S(1)}, f32[8,1,256]{2,1,0:T(1,128)S(1)}, u32[]{:S(2)}, u32[]{:S(2)}) collective-permute-start(f32[8,1,256]{2,1,0:T(1,128)S(1)} %get-tuple-element.201), channel_id=1, source_target_pairs={{0,1},{1,2},{2,3},{3,4},{4,5},{5,6},{6,7},{8,9},{9,10},{10,11},{11... | collective-permute-start | bytes 24584 | tf_op jit(solution)/shard_map/while/body/eval_jaxpr/ppermute | solution.py:19
  141.4 3.4 %collective-permute-done.4 = f32[8,1,256]{2,1,0:T(1,128)S(1)} collective-permute-done((f32[8,1,256]{2,1,0:T(1,128)S(1)}, f32[8,1,256]{2,1,0:T(1,128)S(1)}, u32[]{:S(2)}, u32[]{:S(2)}) %collective-permute-start.4) | collective-permute-done | bytes 8224 | tf_op jit(solution)/shard_map/while/body/eval_jaxpr/ppermute | solution.py:19
  145.0 3.5 %collective-permute-start = (f32[8,8,256]{2,1,0:T(8,128)S(1)}, f32[8,8,256]{2,1,0:T(8,128)S(1)}, u32[]{:S(2)}, u32[]{:S(2)}) collective-permute-start(f32[8,8,256]{2,1,0:T(8,128)S(1)} %get-tuple-element.210), channel_id=1, source_target_pairs={{0,8},{8,16},{16,24},{1,9},{9,17},{17,25},{2,10},{10,18},{18,26},{... | collective-permute-start | bytes 196616 | tf_op jit(solution)/shard_map/while/body/eval_jaxpr/ppermute | solution.py:30
  148.5 2.7 %collective-permute-done = f32[8,8,256]{2,1,0:T(8,128)S(1)} collective-permute-done((f32[8,8,256]{2,1,0:T(8,128)S(1)}, f32[8,8,256]{2,1,0:T(8,128)S(1)}, u32[]{:S(2)}, u32[]{:S(2)}) %collective-permute-start) | collective-permute-done | bytes 65568 | tf_op jit(solution)/shard_map/while/body/eval_jaxpr/ppermute | solution.py:30
  151.2 1.9 collective-permute-start.1
  153.1 2.4 %collective-permute-start.2 = (f32[8,1,256]{2,1,0:T(1,128)S(1)}, f32[8,1,256]{2,1,0:T(1,128)S(1)}, u32[]{:S(2)}, u32[]{:S(2)}) collective-permute-start(f32[8,1,256]{2,1,0:T(1,128)S(1)} %get-tuple-element.199), channel_id=1, source_target_pairs={{0,1},{1,2},{2,3},{3,4},{4,5},{5,6},{6,7},{8,9},{9,10},{10,11},{11... | collective-permute-start | bytes 24584 | tf_op jit(solution)/shard_map/while/body/eval_jaxpr/ppermute | solution.py:19
  155.5 3.4 %collective-permute-done.2 = f32[8,1,256]{2,1,0:T(1,128)S(1)} collective-permute-done((f32[8,1,256]{2,1,0:T(1,128)S(1)}, f32[8,1,256]{2,1,0:T(1,128)S(1)}, u32[]{:S(2)}, u32[]{:S(2)}) %collective-permute-start.2) | collective-permute-done | bytes 8224 | tf_op jit(solution)/shard_map/while/body/eval_jaxpr/ppermute | solution.py:19
  159.1 1.9 collective-permute-start.3
  161.0 2.4 %collective-permute-start.4 = (f32[8,1,256]{2,1,0:T(1,128)S(1)}, f32[8,1,256]{2,1,0:T(1,128)S(1)}, u32[]{:S(2)}, u32[]{:S(2)}) collective-permute-start(f32[8,1,256]{2,1,0:T(1,128)S(1)} %get-tuple-element.201), channel_id=1, source_target_pairs={{0,1},{1,2},{2,3},{3,4},{4,5},{5,6},{6,7},{8,9},{9,10},{10,11},{11... | collective-permute-start | bytes 24584 | tf_op jit(solution)/shard_map/while/body/eval_jaxpr/ppermute | solution.py:19
  163.5 3.4 %collective-permute-done.4 = f32[8,1,256]{2,1,0:T(1,128)S(1)} collective-permute-done((f32[8,1,256]{2,1,0:T(1,128)S(1)}, f32[8,1,256]{2,1,0:T(1,128)S(1)}, u32[]{:S(2)}, u32[]{:S(2)}) %collective-permute-start.4) | collective-permute-done | bytes 8224 | tf_op jit(solution)/shard_map/while/body/eval_jaxpr/ppermute | solution.py:19
  167.1 3.5 %collective-permute-start = (f32[8,8,256]{2,1,0:T(8,128)S(1)}, f32[8,8,256]{2,1,0:T(8,128)S(1)}, u32[]{:S(2)}, u32[]{:S(2)}) collective-permute-start(f32[8,8,256]{2,1,0:T(8,128)S(1)} %get-tuple-element.210), channel_id=1, source_target_pairs={{0,8},{8,16},{16,24},{1,9},{9,17},{17,25},{2,10},{10,18},{18,26},{... | collective-permute-start | bytes 196616 | tf_op jit(solution)/shard_map/while/body/eval_jaxpr/ppermute | solution.py:30
  170.5 2.7 %collective-permute-done = f32[8,8,256]{2,1,0:T(8,128)S(1)} collective-permute-done((f32[8,8,256]{2,1,0:T(8,128)S(1)}, f32[8,8,256]{2,1,0:T(8,128)S(1)}, u32[]{:S(2)}, u32[]{:S(2)}) %collective-permute-start) | collective-permute-done | bytes 65568 | tf_op jit(solution)/shard_map/while/body/eval_jaxpr/ppermute | solution.py:30
  173.2 1.9 collective-permute-start.1
  175.2 2.4 %collective-permute-start.2 = (f32[8,1,256]{2,1,0:T(1,128)S(1)}, f32[8,1,256]{2,1,0:T(1,128)S(1)}, u32[]{:S(2)}, u32[]{:S(2)}) collective-permute-start(f32[8,1,256]{2,1,0:T(1,128)S(1)} %get-tuple-element.199), channel_id=1, source_target_pairs={{0,1},{1,2},{2,3},{3,4},{4,5},{5,6},{6,7},{8,9},{9,10},{10,11},{11... | collective-permute-start | bytes 24584 | tf_op jit(solution)/shard_map/while/body/eval_jaxpr/ppermute | solution.py:19
  177.6 3.4 %collective-permute-done.2 = f32[8,1,256]{2,1,0:T(1,128)S(1)} collective-permute-done((f32[8,1,256]{2,1,0:T(1,128)S(1)}, f32[8,1,256]{2,1,0:T(1,128)S(1)}, u32[]{:S(2)}, u32[]{:S(2)}) %collective-permute-start.2) | collective-permute-done | bytes 8224 | tf_op jit(solution)/shard_map/while/body/eval_jaxpr/ppermute | solution.py:19
  181.2 1.9 collective-permute-start.3
  183.1 2.4 %collective-permute-start.4 = (f32[8,1,256]{2,1,0:T(1,128)S(1)}, f32[8,1,256]{2,1,0:T(1,128)S(1)}, u32[]{:S(2)}, u32[]{:S(2)}) collective-permute-start(f32[8,1,256]{2,1,0:T(1,128)S(1)} %get-tuple-element.201), channel_id=1, source_target_pairs={{0,1},{1,2},{2,3},{3,4},{4,5},{5,6},{6,7},{8,9},{9,10},{10,11},{11... | collective-permute-start | bytes 24584 | tf_op jit(solution)/shard_map/while/body/eval_jaxpr/ppermute | solution.py:19
  185.5 3.4 %collective-permute-done.4 = f32[8,1,256]{2,1,0:T(1,128)S(1)} collective-permute-done((f32[8,1,256]{2,1,0:T(1,128)S(1)}, f32[8,1,256]{2,1,0:T(1,128)S(1)}, u32[]{:S(2)}, u32[]{:S(2)}) %collective-permute-start.4) | collective-permute-done | bytes 8224 | tf_op jit(solution)/shard_map/while/body/eval_jaxpr/ppermute | solution.py:19
  189.6 2.2 %broadcast_in_dim.22 = f32[8,32,256,4]{1,0,3,2:T(8,128)} broadcast(f32[8,32,256]{1,0,2:T(8,128)S(1)} %copy.232), dimensions={0,1,2} | broadcast | bytes 1310720 | tf_op jit(solution)/shard_map/broadcast_in_dim | solution.py:97
  191.9 2.8 %copy.233 = f32[8,32,1024]{2,1,0:T(8,128)S(1)} copy(f32[8,32,1024]{1,0,2:T(8,128)} %bitcast.13) | data formatting | bytes 2097152 | tf_op jit(solution)/shard_map/reshape | solution.py:97
  (74 shorter events, 11.7 us)
Async XLA Ops:
  1.1 25.1 %collective-permute-start.5 = (f32[8,1,1024]{2,0,1:T(8,128)S(1)}, f32[8,1,1024]{2,0,1:T(8,128)S(1)}, u32[]{:S(2)}, u32[]{:S(2)}) collective-permute-start(f32[8,1,1024]{2,0,1:T(8,128)S(1)} %copy.205), channel_id=1, source_target_pairs={{1,0},{2,1},{3,2},{4,3},{5,4},{6,5},{7,6},{9,8},{10,9},{11,10},{12... | collective-permute-start | bytes 98312 | tf_op jit(solution)/shard_map/ppermute | solution.py:22
  3.9 22.3 %collective-permute-start.6 = (f32[8,1,1024]{2,0,1:T(8,128)S(1)}, f32[8,1,1024]{2,0,1:T(8,128)S(1)}, u32[]{:S(2)}, u32[]{:S(2)}) collective-permute-start(f32[8,1,1024]{2,0,1:T(8,128)S(1)} %copy.207), channel_id=1, source_target_pairs={{0,1},{1,2},{2,3},{3,4},{4,5},{5,6},{6,7},{8,9},{9,10},{10,11},{11... | collective-permute-start | bytes 98312 | tf_op jit(solution)/shard_map/ppermute | solution.py:19
  15.7 10.6 %copy-start.2 = (f32[1,8,32,1024]{3,2,1,0:T(8,128)S(1)}, f32[1,8,32,1024]{3,2,1,0:T(8,128)}, u32[]{:S(2)}) copy-start(f32[1,8,32,1024]{3,2,1,0:T(8,128)} %param.5) | copy-start | bytes 3145732
  25.8 1.0 copy-start
  25.8 1.2 copy-start.1
  28.3 48.9 %collective-permute-start.7 = (f32[8,1,1024]{2,0,1:T(8,128)S(1)}, f32[8,1,1024]{2,0,1:T(8,128)S(1)}, u32[]{:S(2)}, u32[]{:S(2)}) collective-permute-start(f32[8,1,1024]{2,0,1:T(8,128)S(1)} %copy.209), channel_id=1, source_target_pairs={{1,0},{2,1},{3,2},{4,3},{5,4},{6,5},{7,6},{9,8},{10,9},{11,10},{12... | collective-permute-start | bytes 98312 | tf_op jit(solution)/shard_map/ppermute | solution.py:22
  32.8 44.4 %collective-permute-start.8 = (f32[8,1,1024]{2,0,1:T(8,128)S(1)}, f32[8,1,1024]{2,0,1:T(8,128)S(1)}, u32[]{:S(2)}, u32[]{:S(2)}) collective-permute-start(f32[8,1,1024]{2,0,1:T(8,128)S(1)} %copy.211), channel_id=1, source_target_pairs={{0,1},{1,2},{2,3},{3,4},{4,5},{5,6},{6,7},{8,9},{9,10},{10,11},{11... | collective-permute-start | bytes 98312 | tf_op jit(solution)/shard_map/ppermute | solution.py:19
  34.8 50.2 %collective-permute-start.13 = (f32[8,1,256]{2,1,0:T(1,128)S(1)}, f32[8,1,256]{2,1,0:T(1,128)}, u32[]{:S(2)}, u32[]{:S(2)}) collective-permute-start(f32[8,1,256]{2,1,0:T(1,128)S(1)} %get-tuple-element.156), channel_id=1, source_target_pairs={{1,0},{2,1},{3,2},{4,3},{5,4},{6,5},{7,6},{9,8},{10,9},{11,10},{12... | collective-permute-start | bytes 24584 | tf_op jit(solution)/shard_map/ppermute | solution.py:22
  39.3 45.7 %collective-permute-start.14 = (f32[8,1,256]{2,1,0:T(1,128)S(1)}, f32[8,1,256]{2,1,0:T(1,128)}, u32[]{:S(2)}, u32[]{:S(2)}) collective-permute-start(f32[8,1,256]{2,1,0:T(1,128)S(1)} %get-tuple-element.155), channel_id=1, source_target_pairs={{0,1},{1,2},{2,3},{3,4},{4,5},{5,6},{6,7},{8,9},{9,10},{10,11},{11... | collective-permute-start | bytes 24584 | tf_op jit(solution)/shard_map/ppermute | solution.py:19
  78.5 7.4 %collective-permute-start.9 = (f32[8,1,1024]{2,0,1:T(8,128)S(1)}, f32[8,1,1024]{2,0,1:T(8,128)S(1)}, u32[]{:S(2)}, u32[]{:S(2)}) collective-permute-start(f32[8,1,1024]{2,0,1:T(8,128)S(1)} %copy.213), channel_id=1, source_target_pairs={{1,0},{2,1},{3,2},{4,3},{5,4},{6,5},{7,6},{9,8},{10,9},{11,10},{12... | collective-permute-start | bytes 98312 | tf_op jit(solution)/shard_map/ppermute | solution.py:22
  83.0 6.1 %collective-permute-start.10 = (f32[8,1,1024]{2,0,1:T(8,128)S(1)}, f32[8,1,1024]{2,0,1:T(8,128)S(1)}, u32[]{:S(2)}, u32[]{:S(2)}) collective-permute-start(f32[8,1,1024]{2,0,1:T(8,128)S(1)} %copy.215), channel_id=1, source_target_pairs={{0,1},{1,2},{2,3},{3,4},{4,5},{5,6},{6,7},{8,9},{9,10},{10,11},{11... | collective-permute-start | bytes 98312 | tf_op jit(solution)/shard_map/ppermute | solution.py:19
  90.4 10.6 %collective-permute-start.11 = (f32[8,1,1024]{2,0,1:T(8,128)S(1)}, f32[8,1,1024]{2,0,1:T(8,128)S(1)}, u32[]{:S(2)}, u32[]{:S(2)}) collective-permute-start(f32[8,1,1024]{2,0,1:T(8,128)S(1)} %copy.217), channel_id=1, source_target_pairs={{1,0},{2,1},{3,2},{4,3},{5,4},{6,5},{7,6},{9,8},{10,9},{11,10},{12... | collective-permute-start | bytes 98312 | tf_op jit(solution)/shard_map/ppermute | solution.py:22
  92.4 8.7 %collective-permute-start.12 = (f32[8,1,1024]{2,0,1:T(8,128)S(1)}, f32[8,1,1024]{2,0,1:T(8,128)S(1)}, u32[]{:S(2)}, u32[]{:S(2)}) collective-permute-start(f32[8,1,1024]{2,0,1:T(8,128)S(1)} %copy.219), channel_id=1, source_target_pairs={{0,1},{1,2},{2,3},{3,4},{4,5},{5,6},{6,7},{8,9},{9,10},{10,11},{11... | collective-permute-start | bytes 98312 | tf_op jit(solution)/shard_map/ppermute | solution.py:19
  94.8 26.5 %collective-permute-start.15 = (f32[8,1,256]{2,1,0:T(1,128)S(1)}, f32[8,1,256]{2,1,0:T(1,128)S(1)}, u32[]{:S(2)}, u32[]{:S(2)}) collective-permute-start(f32[8,1,256]{2,1,0:T(1,128)S(1)} %get-tuple-element.154), channel_id=1, source_target_pairs={{1,0},{2,1},{3,2},{4,3},{5,4},{6,5},{7,6},{9,8},{10,9},{11,10},{12... | collective-permute-start | bytes 24584 | tf_op jit(solution)/shard_map/ppermute | solution.py:22
  98.9 22.4 %collective-permute-start.16 = (f32[8,1,256]{2,1,0:T(1,128)S(1)}, f32[8,1,256]{2,1,0:T(1,128)S(1)}, u32[]{:S(2)}, u32[]{:S(2)}) collective-permute-start(f32[8,1,256]{2,1,0:T(1,128)S(1)} %get-tuple-element.153), channel_id=1, source_target_pairs={{0,1},{1,2},{2,3},{3,4},{4,5},{5,6},{6,7},{8,9},{9,10},{10,11},{11... | collective-permute-start | bytes 24584 | tf_op jit(solution)/shard_map/ppermute | solution.py:19
  121.5 6.2 %collective-permute-start = (f32[8,8,256]{2,1,0:T(8,128)S(1)}, f32[8,8,256]{2,1,0:T(8,128)S(1)}, u32[]{:S(2)}, u32[]{:S(2)}) collective-permute-start(f32[8,8,256]{2,1,0:T(8,128)S(1)} %get-tuple-element.210), channel_id=1, source_target_pairs={{0,8},{8,16},{16,24},{1,9},{9,17},{17,25},{2,10},{10,18},{18,26},{... | collective-permute-start | bytes 196616 | tf_op jit(solution)/shard_map/while/body/eval_jaxpr/ppermute | solution.py:30
  127.6 5.3 %collective-permute-start.1 = (f32[8,1,256]{2,1,0:T(1,128)S(1)}, f32[8,1,256]{2,1,0:T(1,128)S(1)}, u32[]{:S(2)}, u32[]{:S(2)}) collective-permute-start(f32[8,1,256]{2,1,0:T(1,128)S(1)} %get-tuple-element.198), channel_id=1, source_target_pairs={{1,0},{2,1},{3,2},{4,3},{5,4},{6,5},{7,6},{9,8},{10,9},{11,10},{12... | collective-permute-start | bytes 24584 | tf_op jit(solution)/shard_map/while/body/eval_jaxpr/ppermute | solution.py:22
  131.0 5.9 %collective-permute-start.2 = (f32[8,1,256]{2,1,0:T(1,128)S(1)}, f32[8,1,256]{2,1,0:T(1,128)S(1)}, u32[]{:S(2)}, u32[]{:S(2)}) collective-permute-start(f32[8,1,256]{2,1,0:T(1,128)S(1)} %get-tuple-element.199), channel_id=1, source_target_pairs={{0,1},{1,2},{2,3},{3,4},{4,5},{5,6},{6,7},{8,9},{9,10},{10,11},{11... | collective-permute-start | bytes 24584 | tf_op jit(solution)/shard_map/while/body/eval_jaxpr/ppermute | solution.py:19
  137.1 4.3 %collective-permute-start.3 = (f32[8,1,256]{2,1,0:T(1,128)S(1)}, f32[8,1,256]{2,1,0:T(1,128)S(1)}, u32[]{:S(2)}, u32[]{:S(2)}) collective-permute-start(f32[8,1,256]{2,1,0:T(1,128)S(1)} %get-tuple-element.200), channel_id=1, source_target_pairs={{1,0},{2,1},{3,2},{4,3},{5,4},{6,5},{7,6},{9,8},{10,9},{11,10},{12... | collective-permute-start | bytes 24584 | tf_op jit(solution)/shard_map/while/body/eval_jaxpr/ppermute | solution.py:22
  139.0 5.9 %collective-permute-start.4 = (f32[8,1,256]{2,1,0:T(1,128)S(1)}, f32[8,1,256]{2,1,0:T(1,128)S(1)}, u32[]{:S(2)}, u32[]{:S(2)}) collective-permute-start(f32[8,1,256]{2,1,0:T(1,128)S(1)} %get-tuple-element.201), channel_id=1, source_target_pairs={{0,1},{1,2},{2,3},{3,4},{4,5},{5,6},{6,7},{8,9},{9,10},{10,11},{11... | collective-permute-start | bytes 24584 | tf_op jit(solution)/shard_map/while/body/eval_jaxpr/ppermute | solution.py:19
  145.0 6.2 %collective-permute-start = (f32[8,8,256]{2,1,0:T(8,128)S(1)}, f32[8,8,256]{2,1,0:T(8,128)S(1)}, u32[]{:S(2)}, u32[]{:S(2)}) collective-permute-start(f32[8,8,256]{2,1,0:T(8,128)S(1)} %get-tuple-element.210), channel_id=1, source_target_pairs={{0,8},{8,16},{16,24},{1,9},{9,17},{17,25},{2,10},{10,18},{18,26},{... | collective-permute-start | bytes 196616 | tf_op jit(solution)/shard_map/while/body/eval_jaxpr/ppermute | solution.py:30
  151.2 4.3 %collective-permute-start.1 = (f32[8,1,256]{2,1,0:T(1,128)S(1)}, f32[8,1,256]{2,1,0:T(1,128)S(1)}, u32[]{:S(2)}, u32[]{:S(2)}) collective-permute-start(f32[8,1,256]{2,1,0:T(1,128)S(1)} %get-tuple-element.198), channel_id=1, source_target_pairs={{1,0},{2,1},{3,2},{4,3},{5,4},{6,5},{7,6},{9,8},{10,9},{11,10},{12... | collective-permute-start | bytes 24584 | tf_op jit(solution)/shard_map/while/body/eval_jaxpr/ppermute | solution.py:22
  153.1 5.9 %collective-permute-start.2 = (f32[8,1,256]{2,1,0:T(1,128)S(1)}, f32[8,1,256]{2,1,0:T(1,128)S(1)}, u32[]{:S(2)}, u32[]{:S(2)}) collective-permute-start(f32[8,1,256]{2,1,0:T(1,128)S(1)} %get-tuple-element.199), channel_id=1, source_target_pairs={{0,1},{1,2},{2,3},{3,4},{4,5},{5,6},{6,7},{8,9},{9,10},{10,11},{11... | collective-permute-start | bytes 24584 | tf_op jit(solution)/shard_map/while/body/eval_jaxpr/ppermute | solution.py:19
  159.1 4.3 %collective-permute-start.3 = (f32[8,1,256]{2,1,0:T(1,128)S(1)}, f32[8,1,256]{2,1,0:T(1,128)S(1)}, u32[]{:S(2)}, u32[]{:S(2)}) collective-permute-start(f32[8,1,256]{2,1,0:T(1,128)S(1)} %get-tuple-element.200), channel_id=1, source_target_pairs={{1,0},{2,1},{3,2},{4,3},{5,4},{6,5},{7,6},{9,8},{10,9},{11,10},{12... | collective-permute-start | bytes 24584 | tf_op jit(solution)/shard_map/while/body/eval_jaxpr/ppermute | solution.py:22
  161.0 5.9 %collective-permute-start.4 = (f32[8,1,256]{2,1,0:T(1,128)S(1)}, f32[8,1,256]{2,1,0:T(1,128)S(1)}, u32[]{:S(2)}, u32[]{:S(2)}) collective-permute-start(f32[8,1,256]{2,1,0:T(1,128)S(1)} %get-tuple-element.201), channel_id=1, source_target_pairs={{0,1},{1,2},{2,3},{3,4},{4,5},{5,6},{6,7},{8,9},{9,10},{10,11},{11... | collective-permute-start | bytes 24584 | tf_op jit(solution)/shard_map/while/body/eval_jaxpr/ppermute | solution.py:19
  167.1 6.2 %collective-permute-start = (f32[8,8,256]{2,1,0:T(8,128)S(1)}, f32[8,8,256]{2,1,0:T(8,128)S(1)}, u32[]{:S(2)}, u32[]{:S(2)}) collective-permute-start(f32[8,8,256]{2,1,0:T(8,128)S(1)} %get-tuple-element.210), channel_id=1, source_target_pairs={{0,8},{8,16},{16,24},{1,9},{9,17},{17,25},{2,10},{10,18},{18,26},{... | collective-permute-start | bytes 196616 | tf_op jit(solution)/shard_map/while/body/eval_jaxpr/ppermute | solution.py:30
  173.2 4.3 %collective-permute-start.1 = (f32[8,1,256]{2,1,0:T(1,128)S(1)}, f32[8,1,256]{2,1,0:T(1,128)S(1)}, u32[]{:S(2)}, u32[]{:S(2)}) collective-permute-start(f32[8,1,256]{2,1,0:T(1,128)S(1)} %get-tuple-element.198), channel_id=1, source_target_pairs={{1,0},{2,1},{3,2},{4,3},{5,4},{6,5},{7,6},{9,8},{10,9},{11,10},{12... | collective-permute-start | bytes 24584 | tf_op jit(solution)/shard_map/while/body/eval_jaxpr/ppermute | solution.py:22
  175.2 5.9 %collective-permute-start.2 = (f32[8,1,256]{2,1,0:T(1,128)S(1)}, f32[8,1,256]{2,1,0:T(1,128)S(1)}, u32[]{:S(2)}, u32[]{:S(2)}) collective-permute-start(f32[8,1,256]{2,1,0:T(1,128)S(1)} %get-tuple-element.199), channel_id=1, source_target_pairs={{0,1},{1,2},{2,3},{3,4},{4,5},{5,6},{6,7},{8,9},{9,10},{10,11},{11... | collective-permute-start | bytes 24584 | tf_op jit(solution)/shard_map/while/body/eval_jaxpr/ppermute | solution.py:19
  181.2 4.3 %collective-permute-start.3 = (f32[8,1,256]{2,1,0:T(1,128)S(1)}, f32[8,1,256]{2,1,0:T(1,128)S(1)}, u32[]{:S(2)}, u32[]{:S(2)}) collective-permute-start(f32[8,1,256]{2,1,0:T(1,128)S(1)} %get-tuple-element.200), channel_id=1, source_target_pairs={{1,0},{2,1},{3,2},{4,3},{5,4},{6,5},{7,6},{9,8},{10,9},{11,10},{12... | collective-permute-start | bytes 24584 | tf_op jit(solution)/shard_map/while/body/eval_jaxpr/ppermute | solution.py:22
  183.1 5.9 %collective-permute-start.4 = (f32[8,1,256]{2,1,0:T(1,128)S(1)}, f32[8,1,256]{2,1,0:T(1,128)S(1)}, u32[]{:S(2)}, u32[]{:S(2)}) collective-permute-start(f32[8,1,256]{2,1,0:T(1,128)S(1)} %get-tuple-element.201), channel_id=1, source_target_pairs={{0,1},{1,2},{2,3},{3,4},{4,5},{5,6},{6,7},{8,9},{9,10},{10,11},{11... | collective-permute-start | bytes 24584 | tf_op jit(solution)/shard_map/while/body/eval_jaxpr/ppermute | solution.py:19
where the time goes:
time: 197 us; the launch traced here: 196 us
  starting transfers between devices  72 us (37%)
  other arithmetic  47.9 us (24%)
  local copies, waits for them, and re-layouts  42.6 us (22%)
  waiting for transfers between devices  32.5 us (16%)
    reduce_sum x4, other arithmetic, restrict(): values.reshape(layers, height // 4, 4, breadth // 4, 4).mean(axis=(2, 4))  40.4 us
    ppermute x12, starting transfers between devices, padded(): lax.ppermute(lax.slice_in_dim(block, 0, width, axis=dim), axis, backward)  35.4 us
    ppermute x12, starting transfers between devices, padded(): lax.ppermute(lax.slice_in_dim(block, block.shape[dim] - width, None, axis...  26.1 us
    ppermute x12, waiting for transfers between devices, padded(): lax.ppermute(lax.slice_in_dim(block, block.shape[dim] - width, None, axis...  24.5 us
    unnamed x8, local copies, waits for them, and re-layouts  10.6 us
    ppermute x3, starting transfers between devices, from_behind(): lax.ppermute(value, axis, [(source, source + steps) for source in range(f...  10.5 us
    add x1, local copies, waits for them, and re-layouts, fine_update(): values + DT * (diffusion * laplace - drift + growth * (values - values *...  8.6 us
    ppermute x3, waiting for transfers between devices, from_behind(): lax.ppermute(value, axis, [(source, source + steps) for source in range(f...  8 us
  transfers between devices with their start and end apart: 27, of which 10 were waited for; matrix products, arithmetic and copies ran while one was open for 40% of the time, Pallas kernels for 0%

commit v1 on v0

v1 whole, which is shorter than its diff:
```python
import functools

import jax
import jax.numpy as jnp
from jax import lax
from jax.experimental import pallas as pl
from jax.experimental.pallas import tpu as pltpu
from jax.sharding import PartitionSpec as P

FINE = 4
COARSE = 2
DT = 0.05
VEL = 0.5
LANES = 128
F32 = jnp.float32
BF16 = jnp.bfloat16

VMEM = pl.BlockSpec(memory_space=pltpu.VMEM)
ANY = pl.BlockSpec(memory_space=pl.ANY)


def params(mib):
    return pltpu.CompilerParams(vmem_limit_bytes=mib * 2**20)


def struct(*shape):
    return jax.ShapeDtypeStruct(shape, F32)


def parity():
    return lax.rem(lax.axis_index("space"), 2)


def tiles_of(ref, row, breadth):
    return [ref[row, :, i : i + LANES] for i in range(0, breadth, LANES)]


def put_tiles(ref, row, tiles):
    for i, tile in enumerate(tiles):
        ref[row, :, i * LANES : (i + 1) * LANES] = tile


def masks():
    lane = lax.broadcasted_iota(jnp.int32, (8, LANES), 1)
    level = lax.broadcasted_iota(jnp.int32, (8, LANES), 0)
    return lane == 0, lane == LANES - 1, level == 0, level == 7


def neighbours(tiles, edges):
    first, last, bottom, top = edges
    back = [pltpu.roll(t, LANES - 1, 1) for t in tiles]
    forth = [pltpu.roll(t, 1, 1) for t in tiles]
    zero = jnp.zeros_like(tiles[0])
    x_next = [jnp.where(last, b, a) for a, b in zip(back, back[1:] + [zero])]
    x_prev = [jnp.where(first, b, a) for a, b in zip(forth, [zero] + forth[:-1])]
    levels = [
        jnp.where(top, 0.0, pltpu.roll(t, 7, 0)) + jnp.where(bottom, 0.0, pltpu.roll(t, 1, 0))
        for t in tiles
    ]
    return x_next, x_prev, levels


def fine_row(state, row, coef_a, coef_b, coef_k, coef_row, breadth, edges):
    tiles = tiles_of(state, row, breadth)
    x_next, x_prev, levels = neighbours(tiles, edges)
    out = []
    for i, u in enumerate(tiles):
        span = slice(i * LANES, (i + 1) * LANES)
        plus = state[row + 1, :, span] + x_next[i]
        minus = state[row - 1, :, span] + x_prev[i]
        own = u * (coef_a[coef_row, :, span] - coef_b[coef_row, :, span] * (u * u))
        spread = coef_k[coef_row, :, span] * ((plus + minus) + levels[i])
        out.append((own + spread) - (0.5 * VEL * DT) * (plus - minus))
    return out


def coarse_row(state, row, coef_k, coef_g, coef_row, breadth, edges):
    tiles = tiles_of(state, row, breadth)
    x_next, x_prev, levels = neighbours(tiles, edges)
    out = []
    for i, c in enumerate(tiles):
        span = slice(i * LANES, (i + 1) * LANES)
        plus = state[row + 1, :, span] + x_next[i]
        minus = state[row - 1, :, span] + x_prev[i]
        k = coef_k[coef_row, :, span]
        g = coef_g[coef_row, :, span]
        bend = (levels[i] - 2.0 * c) + ((plus + minus) - 4.0 * c) * (1.0 / 16.0)
        drift = (VEL / 8.0) * (plus - minus)
        out.append(c + (2.0 * DT) * (k * bend - drift + g * (c - c * c * c * (1.0 / 3.0))))
    return out


def split_dot(values, matrix):
    high = values.astype(BF16)
    rest = values - high.astype(F32)
    mid = rest.astype(BF16)
    low = (rest - mid.astype(F32)).astype(BF16)
    dot = functools.partial(jnp.dot, preferred_element_type=F32)
    return dot(high, matrix) + (dot(mid, matrix) + dot(low, matrix))


def pool_matrix(breadth, value):
    fine = lax.broadcasted_iota(jnp.int32, (breadth, breadth // 4), 0)
    coarse = lax.broadcasted_iota(jnp.int32, (breadth, breadth // 4), 1)
    return jnp.where(fine // 4 == coarse, value, 0.0).astype(BF16)


def spread_matrix(breadth):
    coarse = lax.broadcasted_iota(jnp.int32, (breadth // 4, breadth), 0)
    fine = lax.broadcasted_iota(jnp.int32, (breadth // 4, breadth), 1)
    return jnp.where(fine // 4 == coarse, 1.0, 0.0).astype(BF16)


def pooled(ref, first_row, coarse_rows, pool):
    sums = []
    for c in range(coarse_rows):
        r = first_row + 4 * c
        sums.append((ref[r] + ref[r + 1]) + (ref[r + 2] + ref[r + 3]))
    return split_dot(jnp.concatenate(sums, axis=0), pool)


def pack_kernel(u_hbm, k_hbm, g_hbm, even_ref, odd_ref, u_nat, k_nat, g_nat, k_wide, g_wide, sems):
    height = u_hbm.shape[2]
    copies = []
    for side, (low, low16) in enumerate(((0, 0), (height - 8, height - 16))):
        copies.append(pltpu.make_async_copy(u_hbm.at[0, :, pl.ds(low, 8), :], u_nat.at[side], sems.at[0, side]))
        copies.append(pltpu.make_async_copy(k_hbm.at[:, pl.ds(low16, 16), :], k_nat.at[side], sems.at[1, side]))
        copies.append(pltpu.make_async_copy(g_hbm.at[:, pl.ds(low16, 16), :], g_nat.at[side], sems.at[2, side]))
    for copy in copies:
        copy.start()
    for copy in copies:
        copy.wait()

    def fill(side, ref):
        k_wide[...] = k_nat[side].astype(F32)
        g_wide[...] = g_nat[side].astype(F32)
        for i in range(4):
            ref[i] = u_nat[side, :, (4 if side else 0) + i, :]
        for i in range(3):
            ref[4 + i] = k_wide[:, (13 if side else 0) + i, :]
            ref[7 + i] = g_wide[:, (13 if side else 0) + i, :]

    even_device = parity() == 0

    @pl.when(even_device)
    def _():
        fill(0, odd_ref)
        fill(1, even_ref)

    @pl.when(jnp.logical_not(even_device))
    def _():
        fill(1, odd_ref)
        fill(0, even_ref)


def pack(starts, diffusivity, reaction):
    breadth = starts.shape[3]
    return pl.pallas_call(
        pack_kernel,
        out_shape=[struct(10, 8, breadth)] * 2,
        in_specs=[ANY] * 3,
        out_specs=[VMEM] * 2,
        scratch_shapes=[
            pltpu.VMEM((2, 8, 8, breadth), F32),
            pltpu.VMEM((2, 8, 16, breadth), BF16),
            pltpu.VMEM((2, 8, 16, breadth), BF16),
            pltpu.VMEM((8, 16, breadth), F32),
            pltpu.VMEM((8, 16, breadth), F32),
            pltpu.SemaphoreType.DMA((3, 2)),
        ],
        compiler_params=params(16),
        name="pack_rows",
    )(starts, diffusivity, reaction)


def set_coefs(k, g, a_ref, b_ref, k_ref, row):
    k = DT * k
    g = DT * g
    k_ref[row] = k
    b_ref[row] = g * (1.0 / 3.0)
    a_ref[row] = 1.0 + (g - 6.0 * k)


def inner_kernel(
    u_hbm, k_hbm, g_hbm, got_ref, fine_ref, edge_ref, coarse_ref, end_ref,
    one, two, coef_a, coef_b, coef_k, k_nat, g_nat, k_wide, g_wide, sems,
):
    height, breadth = u_hbm.shape[2:]
    small = height // 4
    even_side = parity() == 0
    u_copies = [
        pltpu.make_async_copy(u_hbm.at[0, z], one.at[pl.ds(4, height), z, :], sems.at[z]) for z in range(8)
    ]
    k_copy = pltpu.make_async_copy(k_hbm, k_nat, sems.at[8])
    g_copy = pltpu.make_async_copy(g_hbm, g_nat, sems.at[9])
    for copy in [k_copy, g_copy] + u_copies:
        copy.start()
    got = jnp.where(even_side, 4 + height, 0)
    lost = jnp.where(even_side, 0, 4 + height)
    zeros = jnp.zeros((8, breadth), F32)
    for i in range(4):
        one[got + i] = got_ref[i]
        one[lost + i] = zeros
    got_c = jnp.where(even_side, 4 + height, 1)
    lost_c = jnp.where(even_side, 1, 4 + height)
    for i in range(3):
        set_coefs(got_ref[4 + i], got_ref[7 + i], coef_a, coef_b, coef_k, got_c + i)
        coef_a[lost_c + i] = zeros
        coef_b[lost_c + i] = zeros
        coef_k[lost_c + i] = zeros
    pool = pool_matrix(breadth, 1.0 / 16.0)
    k_copy.wait()
    k_wide[...] = k_nat[...].astype(F32)
    g_copy.wait()
    g_wide[...] = g_nat[...].astype(F32)
    sums_k = []
    sums_g = []
    for c in range(small):
        k_rows = [k_wide[:, 4 * c + i, :] for i in range(4)]
        g_rows = [g_wide[:, 4 * c + i, :] for i in range(4)]
        for i in range(4):
            set_coefs(k_rows[i], g_rows[i], coef_a, coef_b, coef_k, 4 + 4 * c + i)
        sums_k.append((k_rows[0] + k_rows[1]) + (k_rows[2] + k_rows[3]))
        sums_g.append((g_rows[0] + g_rows[1]) + (g_rows[2] + g_rows[3]))
    coarse_ref[1] = split_dot(jnp.concatenate(sums_k, axis=0), pool).reshape(small, 8, breadth // 4)
    coarse_ref[2] = split_dot(jnp.concatenate(sums_g, axis=0), pool).reshape(small, 8, breadth // 4)
    for copy in u_copies:
        copy.wait()
    coarse_ref[0] = pooled(one, 4, small, pool).reshape(small, 8, breadth // 4)

    base = jnp.where(even_side, 4, height - 4)
    for i in range(8):
        edge_ref[0, i] = one[base + i]
        edge_ref[1, i] = coef_a[base + i]
        edge_ref[2, i] = coef_b[base + i]
        edge_ref[3, i] = coef_k[base + i]

    edges = masks()

    def sweep(source, target, low, high, shift):
        def body(row, carry):
            put_tiles(target, row - shift, fine_row(source, row, coef_a, coef_b, coef_k, row, breadth, edges))
            return carry

        lax.fori_loop(low, high, body, 0, unroll=2)

    sweep(one, two, 1, height + 7, 0)
    sweep(two, one, 2, height + 6, 0)
    sweep(one, two, 3, height + 5, 0)
    sweep(two, fine_ref, 4, height + 4, 4)
    end_ref[...] = pooled(fine_ref, 0, small, pool).reshape(small, 8, breadth // 4)


def inner(starts, diffusivity, reaction, got):
    height, breadth = starts.shape[2:]
    small = height // 4
    wide = pltpu.VMEM((height + 8, 8, breadth), F32)
    return pl.pallas_call(
        inner_kernel,
        out_shape=[
            struct(height, 8, breadth),
            struct(4, 8, 8, breadth),
            struct(3, small, 8, breadth // 4),
            struct(small, 8, breadth // 4),
        ],
        in_specs=[ANY] * 3 + [VMEM],
        out_specs=[VMEM] * 4,
        scratch_shapes=[wide] * 5
        + [
            pltpu.VMEM((8, height, breadth), BF16),
            pltpu.VMEM((8, height, breadth), BF16),
            pltpu.VMEM((8, height, breadth), F32),
            pltpu.VMEM((8, height, breadth), F32),
            pltpu.SemaphoreType.DMA((10,)),
        ],
        compiler_params=params(24),
        cost_estimate=pl.CostEstimate(flops=30_000_000, bytes_accessed=4_000_000, transcendentals=0),
        name="inner_updates",
    )(starts, diffusivity, reaction, got)


def rows_for(array, low_side, reach):
    start = jnp.where(low_side, 0, array.shape[1] - reach)
    return lax.dynamic_slice_in_dim(array, start, reach, axis=1)


def exchanges(count):
    even = [(i, i ^ 1) for i in range(count)]
    odd = [(i, (i - 1 if i % 2 == 0 else i + 1) % count) for i in range(count)]
    return even, odd


def alive():
    place = lax.axis_index("space")
    last = lax.axis_size("space") - 1
    return jnp.where(jnp.logical_or(place == 0, place == last), 0.0, 1.0).astype(F32)


def edge_kernel(
    edge_ref, got_ref, end_in, coarse_ref, even_c, odd_c, rows_ref, end_ref, jump_ref,
    one, two, coef_a, coef_b, coef_k, seen, half, coarse_k, coarse_g,
):
    breadth = edge_ref.shape[3]
    small = end_ref.shape[0]
    low_side = parity() == 0
    live = alive()
    edges = masks()
    own_u = jnp.where(low_side, 4, 0)
    own_c = jnp.where(low_side, 4, 0)
    got_u = jnp.where(low_side, 0, 8)
    got_c = jnp.where(low_side, 1, 8)
    for i in range(8):
        one[own_u + i] = edge_ref[0, i]
        coef_a[own_c + i] = edge_ref[1, i]
        coef_b[own_c + i] = edge_ref[2, i]
        coef_k[own_c + i] = edge_ref[3, i]
    for i in range(4):
        one[got_u + i] = got_ref[i] * live
    for i in range(3):
        set_coefs(got_ref[4 + i], got_ref[7 + i], coef_a, coef_b, coef_k, got_c + i)

    def sweep(source, target, low, high, shift):
        def body(row, carry):
            outside = jnp.where(low_side, row < 4, row >= 8)
            factor = jnp.where(outside, live, 1.0)
            tiles = fine_row(source, row, coef_a, coef_b, coef_k, row, breadth, edges)
            put_tiles(target, row - shift, [t * factor for t in tiles])
            return carry

        lax.fori_loop(low, high, body, 0, unroll=2)

    sweep(one, two, 1, 11, 0)
    sweep(two, one, 2, 10, 0)
    sweep(one, two, 3, 9, 0)
    sweep(two, rows_ref, 4, 8, 4)
    pool = pool_matrix(breadth, 1.0 / 16.0)
    end_ref[...] = end_in[...]
    end_ref[jnp.where(low_side, 0, small - 1)] = pooled(rows_ref, 0, 1, pool)

    fill_coarse(seen, coarse_ref.at[0], even_c.at[0], odd_c.at[0], 2, low_side, live)
    fill_coarse(coarse_k, coarse_ref.at[1], even_c.at[1], odd_c.at[1], 2, low_side, live)
    fill_coarse(coarse_g, coarse_ref.at[2], even_c.at[2], odd_c.at[2], 2, low_side, live)
    coarse_sweep(seen, half, coarse_k, coarse_g, 1, small + 3, 2, small, low_side, live, edges)
    first = lax.axis_index("tm") == 0
    for r in range(small):
        tiles = coarse_row(half, 2 + r, coarse_k, coarse_g, 2 + r, breadth // 4, edges)
        for i, tile in enumerate(tiles):
            span = slice(i * LANES, (i + 1) * LANES)
            jump_ref[r, :, span] = end_ref[r, :, span] - jnp.where(first, 0.0, tile)


def fill_coarse(wide, own, even_part, odd_part, reach, low_side, live):
    rows = own.shape[0]
    count = even_part.shape[0]
    for r in range(rows):
        wide[reach + r] = own[r]
    odd_at = jnp.where(low_side, 0, reach + rows)
    even_at = jnp.where(low_side, reach + rows, 0)
    odd_from = jnp.where(low_side, count - reach, 0)
    even_from = jnp.where(low_side, 0, count - reach)
    for i in range(reach):
        wide[odd_at + i] = odd_part[odd_from + i] * live
        wide[even_at + i] = even_part[even_from + i]


def coarse_sweep(source, target, coef_k, coef_g, low, high, reach, rows, low_side, live, edges, shift=0):
    breadth = source.shape[2]
    for row in range(low, high):
        tiles = coarse_row(source, row, coef_k, coef_g, row + shift, breadth, edges)
        if row < reach:
            factor = jnp.where(low_side, live, 1.0)
            tiles = [t * factor for t in tiles]
        elif row >= reach + rows:
            factor = jnp.where(low_side, 1.0, live)
            tiles = [t * factor for t in tiles]
        put_tiles(target, row, tiles)


def edge(edge_rows, got, end, coarse, even_c, odd_c):
    breadth = edge_rows.shape[3]
    small = end.shape[0]
    wide = pltpu.VMEM((12, 8, breadth), F32)
    thin = pltpu.VMEM((small + 4, 8, breadth // 4), F32)
    return pl.pallas_call(
        edge_kernel,
        out_shape=[
            struct(4, 8, breadth),
            struct(small, 8, breadth // 4),
            struct(small, 8, breadth // 4),
        ],
        in_specs=[VMEM] * 6,
        out_specs=[VMEM] * 3,
        scratch_shapes=[wide] * 5 + [thin] * 4,
        compiler_params=params(16),
        name="edge_updates",
    )(edge_rows, got, end, coarse, even_c, odd_c)


def last_kernel(
    fine_hbm, rows_ref, end_ref, jump_ref, before_ref, even_j, odd_j, coarse_ref, even_c, odd_c, out_ref,
    fine_ref, one, two, coarse_k, coarse_g, added, sem,
):
    behind = before_ref.shape[0]
    reach = COARSE * behind
    height, _, breadth = fine_hbm.shape
    small = height // 4
    fetch = pltpu.make_async_copy(fine_hbm, fine_ref, sem.at[0])
    fetch.start()
    low_side = parity() == 0
    live = alive()
    edges = masks()
    slice_id = lax.axis_index("tm")
    fill_coarse(coarse_k, coarse_ref.at[1], even_c.at[1], odd_c.at[1], reach, low_side, live)
    fill_coarse(coarse_g, coarse_ref.at[2], even_c.at[2], odd_c.at[2], reach, low_side, live)
    at = 0
    for j in range(behind):
        width = reach - COARSE * j
        ok = jnp.where(slice_id >= behind - j, 1.0, 0.0).astype(F32)
        target = one if j == 0 else added
        base = reach - width
        for r in range(small):
            target[reach + r] = before_ref[j, r] * ok
        odd_at = jnp.where(low_side, base, reach + small)
        even_at = jnp.where(low_side, reach + small, base)
        for i in range(width):
            target[odd_at + i] = odd_j[at + i] * (ok * live)
            target[even_at + i] = even_j[at + i] * ok
        at += width
        if j > 0:
            for r in range(base, reach + small + width):
                one[r] = one[r] + added[r]
        coarse_sweep(one, two, coarse_k, coarse_g, base + 1, reach + small + width - 1, reach, small, low_side, live, edges)
        coarse_sweep(two, one, coarse_k, coarse_g, base + 2, reach + small + width - 2, reach, small, low_side, live, edges)
    spread = spread_matrix(breadth)
    change = jnp.concatenate(
        [(one[reach + r] + jump_ref[r]) - end_ref[r] for r in range(small)], axis=0
    )
    moved = split_dot(change, spread)
    fetch.wait()
    fixed = jnp.where(low_side, 0, height - 4)
    for i in range(4):
        fine_ref[fixed + i] = rows_ref[i]
    for y in range(height):
        c = y // 4
        out_ref[0, :, y, :] = fine_ref[y] + moved[8 * c : 8 * c + 8]


def last(fine, rows, end, jump, before, even_j, odd_j, coarse, even_c, odd_c):
    height, _, breadth = fine.shape
    small = height // 4
    reach = COARSE * before.shape[0]
    thin = pltpu.VMEM((small + 2 * reach, 8, breadth // 4), F32)
    return pl.pallas_call(
        last_kernel,
        out_shape=struct(1, 8, height, breadth),
        in_specs=[ANY] + [VMEM] * 9,
        out_specs=VMEM,
        scratch_shapes=[pltpu.VMEM((height, 8, breadth), F32)] + [thin] * 5 + [pltpu.SemaphoreType.DMA((1,))],
        compiler_params=params(16),
        name="chain_and_spread",
    )(fine, rows, end, jump, before, even_j, odd_j, coarse, even_c, odd_c)


def relay(jump, coarse, even_c, odd_c, even, odd):
    low_side = parity() == 0
    live = alive()
    small = jump.shape[0]

    def widened(own, even_part, odd_part):
        even_part, odd_part = even_part[:, -2:], odd_part[:, -2:] * live
        low = jnp.where(low_side, odd_part, even_part)
        high = jnp.where(low_side, even_part, odd_part)
        return jnp.concatenate([low, own, high], axis=1)

    def update(values, k, g):
        rows = values.shape[0] - 2
        middle = values[1:-1]
        plus = values[2:] + jnp.pad(middle, ((0, 0), (0, 0), (0, 1)))[:, :, 1:]
        minus = values[:-2] + jnp.pad(middle, ((0, 0), (0, 0), (1, 0)))[:, :, :-1]
        levels = jnp.pad(middle, ((0, 0), (0, 1), (0, 0)))[:, 1:] + jnp.pad(middle, ((0, 0), (1, 0), (0, 0)))[:, :-1]
        bend = levels - 2.0 * middle + (plus + minus - 4.0 * middle) / 16.0
        drift = VEL * (plus - minus) / 8.0
        return middle + 2.0 * DT * (k * bend - drift + g * (middle - middle * middle * middle / 3.0))

    side_e = coarse_halo(coarse, even_c, 2, jnp.logical_not(low_side))
    side_o = coarse_halo(coarse, odd_c, 2, low_side)
    coefs = widened(coarse, side_e, side_o)
    place = lax.axis_index("space")
    start = jnp.where(place == 0, 1, 0)
    stop = jnp.where(place == lax.axis_size("space") - 1, small + 1, small + 2)
    row = jnp.arange(small + 2)[:, None, None]
    inside = jnp.logical_and(row >= start, row < stop)

    def advance(values):
        block = values[None]
        even_v = lax.ppermute(rows_for(block, jnp.logical_not(low_side), 2), "space", even)
        odd_v = lax.ppermute(rows_for(block, low_side, 2), "space", odd)
        wide = widened(block, even_v, odd_v)[0]
        wide = jnp.where(inside, update(wide, coefs[1, 1:-1], coefs[2, 1:-1]), 0.0)
        return update(wide, coarse[1], coarse[2])

    slice_id = lax.axis_index("tm")
    slices = lax.axis_size("tm")
    onward = [(i, i + 1) for i in range(slices - 1)]

    def link(position, state):
        incoming = lax.ppermute(state, "tm", onward)
        return jnp.where(slice_id > 0, advance(incoming), 0.0) + jump

    return lax.fori_loop(0, slices - 1, link, jump)


def coarse_halo(coarse, part, reach, low_side):
    start = jnp.where(low_side, part.shape[1] - reach, 0)
    return lax.dynamic_slice_in_dim(part, start, reach, axis=1)


def per_device(starts, diffusivity, reaction):
    height, breadth = starts.shape[2:]
    small = height // 4
    slices = lax.axis_size("tm")
    behind = slices - 1
    reach = COARSE * behind
    at_once = 0 < behind and reach <= small
    even, odd = exchanges(lax.axis_size("space"))
    low_side = parity() == 0
    high_side = jnp.logical_not(low_side)

    even_rows, odd_rows = pack(starts, diffusivity, reaction)
    odd_got = lax.ppermute(odd_rows, "space", odd)
    even_got = lax.ppermute(even_rows, "space", even)
    fine, edge_rows, coarse, end = inner(starts, diffusivity, reaction, even_got)
    width = reach if at_once else COARSE
    odd_c = lax.ppermute(rows_for(coarse, low_side, width), "space", odd)
    even_c = lax.ppermute(rows_for(coarse, high_side, width), "space", even)
    rows, end, jump = edge(edge_rows, odd_got, end, coarse, even_c, odd_c)
    if at_once:
        before = [
            lax.ppermute(jump, "tm", [(i, (i + k) % slices) for i in range(slices)])
            for k in range(behind, 0, -1)
        ]
        before = jnp.stack(before)

        def outer(low):
            return jnp.concatenate(
                [rows_for(before[j][None], low, reach - COARSE * j)[0] for j in range(behind)], axis=0
            )

        odd_j = lax.ppermute(outer(low_side), "space", odd)
        even_j = lax.ppermute(outer(high_side), "space", even)
        return last(fine, rows, end, jump, before, even_j, odd_j, coarse, even_c, odd_c)
    chained = relay(jump, coarse, even_c, odd_c, even, odd)
    change = jnp.repeat(jnp.repeat(chained - end, 4, axis=0), 4, axis=2)
    fixed = jnp.where(low_side, 0, height - 4)
    fine = lax.dynamic_update_slice_in_dim(fine, rows, fixed, axis=0)
    return jnp.transpose(fine + change, (1, 0, 2))[None]


def solution(mesh):
    in_specs = (P("tm", None, "space", None), P(None, "space", None), P(None, "space", None))
    out_specs = P("tm", None, "space", None)
    return jax.shard_map(per_device, mesh=mesh, in_specs=in_specs, out_specs=out_specs, check_vma=False)
```

time: 197 us -> 51.4 us (0.26)
  the two profiles are of different devices: /device:TPU:12 before, /device:TPU:0 now
where the time goes in v1:
time: 51.4 us; the launch traced here: 51.1 us
  Pallas kernels  18 us (35%)
  waiting for transfers between devices  16.1 us (31%)
  starting transfers between devices  11.8 us (23%)
  local copies, waits for them, and re-layouts  5.07 us (10%)
    pallas_call x1, Pallas kernels, inner(): pl.pallas_call(inner_kernel, out_shape=[struct(height, 8, breadth), struc...  11.5 us
    ppermute x3, waiting for transfers between devices, per_device(): lax.ppermute(jump, 'tm', [(i, (i + k) % slices) for i in range(slices)])  6.16 us
    ppermute x1, waiting for transfers between devices, per_device(): odd_c = lax.ppermute(rows_for(coarse, low_side, width), 'space', odd)  5.23 us
    unnamed x16, local copies, waits for them, and re-layouts  5.03 us
    ppermute x1, waiting for transfers between devices, per_device(): odd_j = lax.ppermute(outer(low_side), 'space', odd)  4.69 us
    ppermute x3, starting transfers between devices, per_device(): lax.ppermute(jump, 'tm', [(i, (i + k) % slices) for i in range(slices)])  4.66 us
    ppermute x1, starting transfers between devices, per_device(): odd_got = lax.ppermute(odd_rows, 'space', odd)  3.56 us
    pallas_call x1, Pallas kernels, edge(): pl.pallas_call(edge_kernel, out_shape=[struct(4, 8, breadth), struct(smal...  2.98 us
  transfers between devices with their start and end apart: 9, of which 5 were waited for; matrix products, arithmetic and copies ran while one was open for 0% of the time, Pallas kernels for 23%

profile of v1, /device:TPU:0, one launch (start us, length us, event | category | flops | bytes accessed | tf_op | source)
XLA Modules:
  0.0 51.1 jit_solution(2924031386585553461)
XLA Ops:
  0.0 0.0 copy-start
  0.0 1.2 %copy-done = f32[1,8,32,1024]{3,2,1,0:T(8,128)S(1)} copy-done((f32[1,8,32,1024]{3,2,1,0:T(8,128)S(1)}, f32[1,8,32,1024]{3,2,1,0:T(8,128)}, u32[]{:S(2)}) %copy-start) | copy-done | bytes 1048600
  1.2 0.0 copy-start.2
  1.2 1.0 %copy-done.2 = bf16[8,32,1024]{2,1,0:T(8,128)(2,1)S(1)} copy-done((bf16[8,32,1024]{2,1,0:T(8,128)(2,1)S(1)}, bf16[8,32,1024]{2,1,0:T(8,128)(2,1)}, u32[]{:S(2)}) %copy-start.2) | copy-done | bytes 524312
  2.3 0.0 copy-start.4
  2.3 1.0 %copy-done.4 = bf16[8,32,1024]{2,1,0:T(8,128)(2,1)S(1)} copy-done((bf16[8,32,1024]{2,1,0:T(8,128)(2,1)S(1)}, bf16[8,32,1024]{2,1,0:T(8,128)(2,1)}, u32[]{:S(2)}) %copy-start.4) | copy-done | bytes 524312
  3.3 0.0 copy-start.1
  3.3 0.0 copy-start.3
  3.3 0.0 copy-start.5
  3.3 1.1 %pack_rows.1 = (f32[10,8,1024]{2,1,0:T(8,128)S(1)}, f32[10,8,1024]{2,1,0:T(8,128)}) custom-call(f32[1,8,32,1024]{3,2,1,0:T(8,128)S(1)} %copy-done, bf16[8,32,1024]{2,1,0:T(8,128)(2,1)S(1)} %copy-done.2, bf16[8,32,1024]{2,1,0:T(8,128)(2,1)S(1)} %copy-done.4), custom_call_target="tpu_custom_call" | custom-call | tf_op jit(solution)/shard_map/pack_rows/pallas_call | solution.py:158
  4.5 0.5 %collective-permute-start = (f32[10,8,1024]{2,1,0:T(8,128)S(1)}, f32[10,8,1024]{2,1,0:T(8,128)S(1)}, u32[]{:S(2)}, u32[]{:S(2)}) collective-permute-start(f32[10,8,1024]{2,1,0:T(8,128)S(1)} %get-tuple-element.14), channel_id=1, source_target_pairs={{0,1},{1,0},{2,3},{3,2},{4,5},{5,4},{6,7},{7,6},{8,9},{9,8},{10,11... | collective-permute-start | bytes 983048 | tf_op jit(solution)/shard_map/ppermute | solution.py:531
  5.0 3.6 %collective-permute-start.1 = (f32[10,8,1024]{2,1,0:T(8,128)}, f32[10,8,1024]{2,1,0:T(8,128)}, u32[]{:S(2)}, u32[]{:S(2)}) collective-permute-start(f32[10,8,1024]{2,1,0:T(8,128)} %get-tuple-element.17), channel_id=1, source_target_pairs={{0,7},{1,2},{2,1},{3,4},{4,3},{5,6},{6,5},{7,0},{8,15},{9,10},{10,... | collective-permute-start | bytes 983048 | tf_op jit(solution)/shard_map/ppermute | solution.py:530
  8.5 0.0 collective-permute-done.got_ref
  8.5 0.0 copy-start.6
  8.5 0.7 %copy-done.6 = f32[10,8,1024]{2,1,0:T(8,128)} copy-done((f32[10,8,1024]{2,1,0:T(8,128)}, f32[10,8,1024]{2,1,0:T(8,128)S(1)}, u32[]{:S(2)}) %copy-start.6) | copy-done | bytes 327704
  9.3 0.0 copy-done.1
  9.3 0.0 copy-done.3
  9.3 0.0 copy-done.5
  9.3 0.0 copy-start.7
  9.3 1.0 %copy-done.7 = f32[10,8,1024]{2,1,0:T(8,128)S(1)} copy-done((f32[10,8,1024]{2,1,0:T(8,128)S(1)}, f32[10,8,1024]{2,1,0:T(8,128)}, u32[]{:S(2)}) %copy-start.7) | copy-done | bytes 327704
  10.3 11.5 %inner_updates.1 = (f32[32,8,1024]{2,1,0:T(8,128)S(1)}, f32[4,8,8,1024]{3,2,1,0:T(8,128)S(1)}, f32[3,8,8,256]{3,2,1,0:T(8,128)S(1)}, f32[8,8,256]{2,1,0:T(8,128)S(1)}) custom-call(f32[1,8,32,1024]{3,2,1,0:T(8,128)S(1)} %copy-done.1, bf16[8,32,1024]{2,1,0:T(8,128)(2,1)S(1)} %copy-done.3, bf16[8,32,1024]{2,1,0:T(8,128)(2,1)S(1)} %copy-done.5, ...), custom_call_target="tpu_custom_call" | custom-call | flops 30000000 | bytes 4000000 | tf_op jit(solution)/shard_map/inner_updates/pallas_call | solution.py:258
  21.9 0.1 collective-permute-start.2
  21.9 1.6 %collective-permute-start.3 = (f32[3,6,8,256]{3,2,1,0:T(8,128)S(1)}, f32[3,6,8,256]{3,2,1,0:T(8,128)S(1)}, u32[]{:S(2)}, u32[]{:S(2)}) collective-permute-start(f32[3,6,8,256]{3,2,1,0:T(8,128)S(1)} %get-tuple-element.23), channel_id=1, source_target_pairs={{0,7},{1,2},{2,1},{3,4},{4,3},{5,6},{6,5},{7,0},{8,15},{9,10},{10,... | collective-permute-start | bytes 442376 | tf_op jit(solution)/shard_map/ppermute | solution.py:534
  23.5 0.0 collective-permute-done.1.got_ref
  23.5 0.0 collective-permute-done.2.even_c
  23.6 5.2 %collective-permute-done.3.odd_c = f32[3,6,8,256]{3,2,1,0:T(8,128)S(1)} collective-permute-done((f32[3,6,8,256]{3,2,1,0:T(8,128)S(1)}, f32[3,6,8,256]{3,2,1,0:T(8,128)S(1)}, u32[]{:S(2)}, u32[]{:S(2)}) %collective-permute-start.3) | collective-permute-done | bytes 147488 | tf_op jit(solution)/shard_map/ppermute | solution.py:534
  28.8 3.0 %edge_updates.1 = (f32[4,8,1024]{2,1,0:T(8,128)S(1)}, f32[8,8,256]{2,1,0:T(8,128)S(1)}, f32[8,8,256]{2,1,0:T(8,128)S(1)}) custom-call(f32[4,8,8,1024]{3,2,1,0:T(8,128)S(1)} %get-tuple-element.16.edge_ref, f32[10,8,1024]{2,1,0:T(8,128)} %collective-permute-done.1.got_ref, f32[8,8,256]{2,1,0:T(8,128)S(1)} %get-tuple-element.18.end_in, ...), custom_call_target="tpu_custom_call" | custom-call | tf_op jit(solution)/shard_map/edge_updates/pallas_call | solution.py:384
  31.8 3.6 %collective-permute-start.4 = (f32[8,8,256]{2,1,0:T(8,128)S(1)}, f32[8,8,256]{2,1,0:T(8,128)S(1)}, u32[]{:S(2)}, u32[]{:S(2)}) collective-permute-start(f32[8,8,256]{2,1,0:T(8,128)S(1)} %get-tuple-element.22.jump_ref), channel_id=1, source_target_pairs={{0,24},{8,0},{16,8},{24,16},{1,25},{9,1},{17,9},{25,17},{2,26},{10... | collective-permute-start | bytes 196616 | tf_op jit(solution)/shard_map/ppermute | solution.py:539
  35.4 0.0 collective-permute-start.6
  35.4 1.0 %collective-permute-start.5 = (f32[8,8,256]{2,1,0:T(8,128)S(1)}, f32[8,8,256]{2,1,0:T(8,128)S(1)}, u32[]{:S(2)}, u32[]{:S(2)}) collective-permute-start(f32[8,8,256]{2,1,0:T(8,128)S(1)} %get-tuple-element.22.jump_ref), channel_id=1, source_target_pairs={{0,16},{8,24},{16,0},{24,8},{1,17},{9,25},{17,1},{25,9},{2,18},{10... | collective-permute-start | bytes 196616 | tf_op jit(solution)/shard_map/ppermute | solution.py:539
  36.4 1.5 %collective-permute-done.4 = f32[8,8,256]{2,1,0:T(8,128)S(1)} collective-permute-done((f32[8,8,256]{2,1,0:T(8,128)S(1)}, f32[8,8,256]{2,1,0:T(8,128)S(1)}, u32[]{:S(2)}, u32[]{:S(2)}) %collective-permute-start.4) | collective-permute-done | bytes 65568 | tf_op jit(solution)/shard_map/ppermute | solution.py:539
  37.9 3.5 %collective-permute-done.6 = f32[8,8,256]{2,1,0:T(8,128)S(1)} collective-permute-done((f32[8,8,256]{2,1,0:T(8,128)S(1)}, f32[8,8,256]{2,1,0:T(8,128)S(1)}, u32[]{:S(2)}, u32[]{:S(2)}) %collective-permute-start.6) | collective-permute-done | bytes 65568 | tf_op jit(solution)/shard_map/ppermute | solution.py:539
  41.5 1.1 %collective-permute-done.5 = f32[8,8,256]{2,1,0:T(8,128)S(1)} collective-permute-done((f32[8,8,256]{2,1,0:T(8,128)S(1)}, f32[8,8,256]{2,1,0:T(8,128)S(1)}, u32[]{:S(2)}, u32[]{:S(2)}) %collective-permute-start.5) | collective-permute-done | bytes 65568 | tf_op jit(solution)/shard_map/ppermute | solution.py:539
  42.6 0.1 collective-permute-start.7
  42.7 1.3 %collective-permute-start.8 = (f32[12,8,256]{2,1,0:T(8,128)S(1)}, f32[12,8,256]{2,1,0:T(8,128)S(1)}, u32[]{:S(2)}, u32[]{:S(2)}) collective-permute-start(f32[12,8,256]{2,1,0:T(8,128)S(1)} %pad_maximum_fusion.2), channel_id=1, source_target_pairs={{0,7},{1,2},{2,1},{3,4},{4,3},{5,6},{6,5},{7,0},{8,15},{9,10},{10,... | collective-permute-start | bytes 294920 | tf_op jit(solution)/shard_map/ppermute | solution.py:549
  44.0 0.0 collective-permute-done.7.even_j
  44.0 4.7 %collective-permute-done.8.odd_j = f32[12,8,256]{2,1,0:T(8,128)S(1)} collective-permute-done((f32[12,8,256]{2,1,0:T(8,128)S(1)}, f32[12,8,256]{2,1,0:T(8,128)S(1)}, u32[]{:S(2)}, u32[]{:S(2)}) %collective-permute-start.8) | collective-permute-done | bytes 98336 | tf_op jit(solution)/shard_map/ppermute | solution.py:549
  48.7 2.3 %chain_and_spread.1 = f32[1,8,32,1024]{3,2,1,0:T(8,128)} custom-call(f32[32,8,1024]{2,1,0:T(8,128)S(1)} %get-tuple-element.15.fine_hbm, f32[4,8,1024]{2,1,0:T(8,128)S(1)} %get-tuple-element.20.rows_ref, f32[8,8,256]{2,1,0:T(8,128)S(1)} %get-tuple-element.21.end_ref, f32[8,8,256]{2,1,0:T(8,128)S(1)} %get-tuple-element.22.jump_ref, ...), custom_call_target="tpu_custom_call" | custom-call | tf_op jit(solution)/shard_map/chain_and_spread/pallas_call | solution.py:453
  (7 shorter events, 0.1 us)
Async XLA Ops:
  0.0 1.2 %copy-start = (f32[1,8,32,1024]{3,2,1,0:T(8,128)S(1)}, f32[1,8,32,1024]{3,2,1,0:T(8,128)}, u32[]{:S(2)}) copy-start(f32[1,8,32,1024]{3,2,1,0:T(8,128)} %u_hbm.3) | copy-start | bytes 3145732
  1.2 1.0 %copy-start.2 = (bf16[8,32,1024]{2,1,0:T(8,128)(2,1)S(1)}, bf16[8,32,1024]{2,1,0:T(8,128)(2,1)}, u32[]{:S(2)}) copy-start(bf16[8,32,1024]{2,1,0:T(8,128)(2,1)} %k_hbm.3) | copy-start | bytes 1572868
  2.3 1.0 %copy-start.4 = (bf16[8,32,1024]{2,1,0:T(8,128)(2,1)S(1)}, bf16[8,32,1024]{2,1,0:T(8,128)(2,1)}, u32[]{:S(2)}) copy-start(bf16[8,32,1024]{2,1,0:T(8,128)(2,1)} %g_hbm.3) | copy-start | bytes 1572868
  3.3 6.0 %copy-start.1 = (f32[1,8,32,1024]{3,2,1,0:T(8,128)S(1)}, f32[1,8,32,1024]{3,2,1,0:T(8,128)}, u32[]{:S(2)}) copy-start(f32[1,8,32,1024]{3,2,1,0:T(8,128)} %u_hbm.3) | copy-start | bytes 3145732
  3.3 6.0 %copy-start.3 = (bf16[8,32,1024]{2,1,0:T(8,128)(2,1)S(1)}, bf16[8,32,1024]{2,1,0:T(8,128)(2,1)}, u32[]{:S(2)}) copy-start(bf16[8,32,1024]{2,1,0:T(8,128)(2,1)} %k_hbm.3) | copy-start | bytes 1572868
  3.3 6.0 %copy-start.5 = (bf16[8,32,1024]{2,1,0:T(8,128)(2,1)S(1)}, bf16[8,32,1024]{2,1,0:T(8,128)(2,1)}, u32[]{:S(2)}) copy-start(bf16[8,32,1024]{2,1,0:T(8,128)(2,1)} %g_hbm.3) | copy-start | bytes 1572868
  4.5 4.1 %collective-permute-start = (f32[10,8,1024]{2,1,0:T(8,128)S(1)}, f32[10,8,1024]{2,1,0:T(8,128)S(1)}, u32[]{:S(2)}, u32[]{:S(2)}) collective-permute-start(f32[10,8,1024]{2,1,0:T(8,128)S(1)} %get-tuple-element.14), channel_id=1, source_target_pairs={{0,1},{1,0},{2,3},{3,2},{4,5},{5,4},{6,7},{7,6},{8,9},{9,8},{10,11... | collective-permute-start | bytes 983048 | tf_op jit(solution)/shard_map/ppermute | solution.py:531
  5.0 18.6 %collective-permute-start.1 = (f32[10,8,1024]{2,1,0:T(8,128)}, f32[10,8,1024]{2,1,0:T(8,128)}, u32[]{:S(2)}, u32[]{:S(2)}) collective-permute-start(f32[10,8,1024]{2,1,0:T(8,128)} %get-tuple-element.17), channel_id=1, source_target_pairs={{0,7},{1,2},{2,1},{3,4},{4,3},{5,6},{6,5},{7,0},{8,15},{9,10},{10,... | collective-permute-start | bytes 983048 | tf_op jit(solution)/shard_map/ppermute | solution.py:530
  8.5 0.7 %copy-start.6 = (f32[10,8,1024]{2,1,0:T(8,128)}, f32[10,8,1024]{2,1,0:T(8,128)S(1)}, u32[]{:S(2)}) copy-start(f32[10,8,1024]{2,1,0:T(8,128)S(1)} %collective-permute-done.got_ref) | copy-start | bytes 983044
  9.3 1.0 %copy-start.7 = (f32[10,8,1024]{2,1,0:T(8,128)S(1)}, f32[10,8,1024]{2,1,0:T(8,128)}, u32[]{:S(2)}) copy-start(f32[10,8,1024]{2,1,0:T(8,128)} %copy-done.6) | copy-start | bytes 983044
  21.9 1.7 %collective-permute-start.2 = (f32[3,6,8,256]{3,2,1,0:T(8,128)S(1)}, f32[3,6,8,256]{3,2,1,0:T(8,128)S(1)}, u32[]{:S(2)}, u32[]{:S(2)}) collective-permute-start(f32[3,6,8,256]{3,2,1,0:T(8,128)S(1)} %get-tuple-element.24), channel_id=1, source_target_pairs={{0,1},{1,0},{2,3},{3,2},{4,5},{5,4},{6,7},{7,6},{8,9},{9,8},{10,11... | collective-permute-start | bytes 442376 | tf_op jit(solution)/shard_map/ppermute | solution.py:535
  21.9 6.8 %collective-permute-start.3 = (f32[3,6,8,256]{3,2,1,0:T(8,128)S(1)}, f32[3,6,8,256]{3,2,1,0:T(8,128)S(1)}, u32[]{:S(2)}, u32[]{:S(2)}) collective-permute-start(f32[3,6,8,256]{3,2,1,0:T(8,128)S(1)} %get-tuple-element.23), channel_id=1, source_target_pairs={{0,7},{1,2},{2,1},{3,4},{4,3},{5,6},{6,5},{7,0},{8,15},{9,10},{10,... | collective-permute-start | bytes 442376 | tf_op jit(solution)/shard_map/ppermute | solution.py:534
  31.8 6.2 %collective-permute-start.4 = (f32[8,8,256]{2,1,0:T(8,128)S(1)}, f32[8,8,256]{2,1,0:T(8,128)S(1)}, u32[]{:S(2)}, u32[]{:S(2)}) collective-permute-start(f32[8,8,256]{2,1,0:T(8,128)S(1)} %get-tuple-element.22.jump_ref), channel_id=1, source_target_pairs={{0,24},{8,0},{16,8},{24,16},{1,25},{9,1},{17,9},{25,17},{2,26},{10... | collective-permute-start | bytes 196616 | tf_op jit(solution)/shard_map/ppermute | solution.py:539
  35.4 6.1 %collective-permute-start.6 = (f32[8,8,256]{2,1,0:T(8,128)S(1)}, f32[8,8,256]{2,1,0:T(8,128)S(1)}, u32[]{:S(2)}, u32[]{:S(2)}) collective-permute-start(f32[8,8,256]{2,1,0:T(8,128)S(1)} %get-tuple-element.22.jump_ref), channel_id=1, source_target_pairs={{0,8},{8,16},{16,24},{24,0},{1,9},{9,17},{17,25},{25,1},{2,10},{10... | collective-permute-start | bytes 196616 | tf_op jit(solution)/shard_map/ppermute | solution.py:539
  35.4 7.2 %collective-permute-start.5 = (f32[8,8,256]{2,1,0:T(8,128)S(1)}, f32[8,8,256]{2,1,0:T(8,128)S(1)}, u32[]{:S(2)}, u32[]{:S(2)}) collective-permute-start(f32[8,8,256]{2,1,0:T(8,128)S(1)} %get-tuple-element.22.jump_ref), channel_id=1, source_target_pairs={{0,16},{8,24},{16,0},{24,8},{1,17},{9,25},{17,1},{25,9},{2,18},{10... | collective-permute-start | bytes 196616 | tf_op jit(solution)/shard_map/ppermute | solution.py:539
  42.6 1.4 %collective-permute-start.7 = (f32[12,8,256]{2,1,0:T(8,128)S(1)}, f32[12,8,256]{2,1,0:T(8,128)S(1)}, u32[]{:S(2)}, u32[]{:S(2)}) collective-permute-start(f32[12,8,256]{2,1,0:T(8,128)S(1)} %pad_maximum_fusion.1), channel_id=1, source_target_pairs={{0,1},{1,0},{2,3},{3,2},{4,5},{5,4},{6,7},{7,6},{8,9},{9,8},{10,11... | collective-permute-start | bytes 294920 | tf_op jit(solution)/shard_map/ppermute | solution.py:550
  42.7 6.0 %collective-permute-start.8 = (f32[12,8,256]{2,1,0:T(8,128)S(1)}, f32[12,8,256]{2,1,0:T(8,128)S(1)}, u32[]{:S(2)}, u32[]{:S(2)}) collective-permute-start(f32[12,8,256]{2,1,0:T(8,128)S(1)} %pad_maximum_fusion.2), channel_id=1, source_target_pairs={{0,7},{1,2},{2,1},{3,4},{4,3},{5,6},{6,5},{7,0},{8,15},{9,10},{10,... | collective-permute-start | bytes 294920 | tf_op jit(solution)/shard_map/ppermute | solution.py:549

commit v2 on v1

v2 whole, which is shorter than its diff:
```python
import functools

import jax
import jax.numpy as jnp
from jax import lax
from jax.experimental import pallas as pl
from jax.experimental.pallas import tpu as pltpu
from jax.sharding import PartitionSpec as P

FINE = 4
COARSE = 2
DT = 0.05
VEL = 0.5
LANES = 128
F32 = jnp.float32
BF16 = jnp.bfloat16

VMEM = pl.BlockSpec(memory_space=pltpu.VMEM)
ANY = pl.BlockSpec(memory_space=pl.ANY)
HBM = pl.BlockSpec(memory_space=pltpu.HBM)


def params(mib):
    return pltpu.CompilerParams(vmem_limit_bytes=mib * 2**20)


def struct(*shape):
    return jax.ShapeDtypeStruct(shape, F32)


def parity():
    return lax.rem(lax.axis_index("space"), 2)


def tiles_of(ref, row, breadth):
    return [ref[row, :, i : i + LANES] for i in range(0, breadth, LANES)]


def put_tiles(ref, row, tiles):
    for i, tile in enumerate(tiles):
        ref[row, :, i * LANES : (i + 1) * LANES] = tile


def masks():
    lane = lax.broadcasted_iota(jnp.int32, (8, LANES), 1)
    level = lax.broadcasted_iota(jnp.int32, (8, LANES), 0)
    return lane == 0, lane == LANES - 1, level == 0, level == 7


def neighbours(tiles, edges):
    first, last, bottom, top = edges
    back = [pltpu.roll(t, LANES - 1, 1) for t in tiles]
    forth = [pltpu.roll(t, 1, 1) for t in tiles]
    zero = jnp.zeros_like(tiles[0])
    x_next = [jnp.where(last, b, a) for a, b in zip(back, back[1:] + [zero])]
    x_prev = [jnp.where(first, b, a) for a, b in zip(forth, [zero] + forth[:-1])]
    levels = [
        jnp.where(top, 0.0, pltpu.roll(t, 7, 0)) + jnp.where(bottom, 0.0, pltpu.roll(t, 1, 0))
        for t in tiles
    ]
    return x_next, x_prev, levels


def fine_row(state, row, coef_a, coef_b, coef_k, coef_row, breadth, edges):
    tiles = tiles_of(state, row, breadth)
    x_next, x_prev, levels = neighbours(tiles, edges)
    out = []
    for i, u in enumerate(tiles):
        span = slice(i * LANES, (i + 1) * LANES)
        plus = state[row + 1, :, span] + x_next[i]
        minus = state[row - 1, :, span] + x_prev[i]
        own = u * (coef_a[coef_row, :, span] - coef_b[coef_row, :, span] * (u * u))
        spread = coef_k[coef_row, :, span] * ((plus + minus) + levels[i])
        out.append((own + spread) - (0.5 * VEL * DT) * (plus - minus))
    return out


def coarse_row(state, row, coef_k, coef_g, coef_row, breadth, edges):
    tiles = tiles_of(state, row, breadth)
    x_next, x_prev, levels = neighbours(tiles, edges)
    out = []
    for i, c in enumerate(tiles):
        span = slice(i * LANES, (i + 1) * LANES)
        plus = state[row + 1, :, span] + x_next[i]
        minus = state[row - 1, :, span] + x_prev[i]
        k = coef_k[coef_row, :, span]
        g = coef_g[coef_row, :, span]
        bend = (levels[i] - 2.0 * c) + ((plus + minus) - 4.0 * c) * (1.0 / 16.0)
        drift = (2.0 * DT * VEL / 8.0) * (plus - minus)
        out.append(c + ((k * bend - drift) + g * (c - c * c * c * (1.0 / 3.0))))
    return out


def split_dot(values, matrix):
    high = values.astype(BF16)
    rest = values - high.astype(F32)
    mid = rest.astype(BF16)
    low = (rest - mid.astype(F32)).astype(BF16)
    dot = functools.partial(jnp.dot, preferred_element_type=F32)
    return dot(high, matrix) + (dot(mid, matrix) + dot(low, matrix))


def pool_matrix(breadth, value):
    fine = lax.broadcasted_iota(jnp.int32, (breadth, breadth // 4), 0)
    coarse = lax.broadcasted_iota(jnp.int32, (breadth, breadth // 4), 1)
    return jnp.where(fine // 4 == coarse, value, 0.0).astype(BF16)


def spread_matrix(breadth):
    coarse = lax.broadcasted_iota(jnp.int32, (breadth // 4, breadth), 0)
    fine = lax.broadcasted_iota(jnp.int32, (breadth // 4, breadth), 1)
    return jnp.where(fine // 4 == coarse, 1.0, 0.0).astype(BF16)


def pooled(ref, first_row, coarse_rows, pool):
    sums = []
    for c in range(coarse_rows):
        r = first_row + 4 * c
        sums.append((ref[r] + ref[r + 1]) + (ref[r + 2] + ref[r + 3]))
    return split_dot(jnp.concatenate(sums, axis=0), pool)


def set_coefs(k, g, a_ref, b_ref, k_ref, row):
    k = DT * k
    g = DT * g
    k_ref[row] = k
    b_ref[row] = g * (1.0 / 3.0)
    a_ref[row] = 1.0 + (g - 6.0 * k)


def pack_kernel(u_hbm, k_hbm, g_hbm, even_ref, odd_ref, u_nat, k_nat, g_nat, k_wide, g_wide, sems):
    height, breadth = u_hbm.shape[2:]
    copies = []
    for side, (low, low16) in enumerate(((0, 0), (height - 8, height - 16))):
        copies.append(pltpu.make_async_copy(u_hbm.at[0, :, pl.ds(low, 8), :], u_nat.at[side], sems.at[0, side]))
        copies.append(pltpu.make_async_copy(k_hbm.at[:, pl.ds(low16, 16), :], k_nat.at[side], sems.at[1, side]))
        copies.append(pltpu.make_async_copy(g_hbm.at[:, pl.ds(low16, 16), :], g_nat.at[side], sems.at[2, side]))
    for copy in copies:
        copy.start()
    pool = pool_matrix(breadth, 1.0 / 16.0)
    for copy in copies:
        copy.wait()

    def fill(side, ref):
        k_wide[side] = k_nat[side].astype(F32)
        g_wide[side] = g_nat[side].astype(F32)
        u_rows = [u_nat[side, :, i, :] for i in range(8)]
        low = 12 if side else 0
        k_rows = [k_wide[side, :, low + i, :] for i in range(4)]
        g_rows = [g_wide[side, :, low + i, :] for i in range(4)]
        for i in range(4):
            ref[i] = u_rows[(4 if side else 0) + i]
        for i in range(3):
            ref[4 + i] = k_rows[(1 if side else 0) + i]
            ref[7 + i] = g_rows[(1 if side else 0) + i]
        return [(r[0] + r[1]) + (r[2] + r[3]) for r in (u_rows[:4], u_rows[4:], k_rows, g_rows)]

    def both(first, second):
        sums = fill(first, odd_ref) + fill(second, even_ref)
        small = split_dot(jnp.concatenate(sums, axis=0), pool)
        for j, ref in enumerate((odd_ref, even_ref)):
            for i in range(4):
                scale = 1.0 if i < 2 else 2.0 * DT
                row = small[32 * j + 8 * i : 32 * j + 8 * i + 8]
                ref[10, :, i * (breadth // 4) : (i + 1) * (breadth // 4)] = row * scale

    even_device = parity() == 0

    @pl.when(even_device)
    def _():
        both(0, 1)

    @pl.when(jnp.logical_not(even_device))
    def _():
        both(1, 0)


def pack(starts, diffusivity, reaction):
    breadth = starts.shape[3]
    return pl.pallas_call(
        pack_kernel,
        out_shape=[struct(11, 8, breadth)] * 2,
        in_specs=[HBM] * 3,
        out_specs=[VMEM] * 2,
        scratch_shapes=[
            pltpu.VMEM((2, 8, 8, breadth), F32),
            pltpu.VMEM((2, 8, 16, breadth), BF16),
            pltpu.VMEM((2, 8, 16, breadth), BF16),
            pltpu.VMEM((2, 8, 16, breadth), F32),
            pltpu.VMEM((2, 8, 16, breadth), F32),
            pltpu.SemaphoreType.DMA((3, 2)),
        ],
        compiler_params=params(16),
        name="pack_rows",
    )(starts, diffusivity, reaction)


def inner_kernel(
    u_hbm, k_hbm, g_hbm, got_ref, fine_ref, steps_ref, coefs_ref, coarse_ref, end_ref,
    one, two, coef_a, coef_b, coef_k, k_nat, g_nat, flat, sems,
):
    height, breadth = u_hbm.shape[2:]
    columns = breadth // LANES
    small = height // 4
    thin = breadth // 4
    spans = [slice(x * LANES, (x + 1) * LANES) for x in range(columns)]
    above = parity() == 0
    own = pl.multiple_of(jnp.where(above, 0, 8), 8)
    copies = [
        pltpu.make_async_copy(
            u_hbm.at[0, :, :, pl.ds(x * LANES, LANES)], one.at[pl.ds(1, 8), x, pl.ds(8 + own, height), :], sems.at[x]
        )
        for x in range(columns)
    ]
    k_copy = pltpu.make_async_copy(k_hbm, k_nat, sems.at[columns])
    g_copy = pltpu.make_async_copy(g_hbm, g_nat, sems.at[columns + 1])
    for copy in [k_copy, g_copy] + copies:
        copy.start()
    blank = jnp.zeros((8, LANES), F32)
    top = height + 16

    def clear(z, carry):
        for ref in (one, two):
            for x in range(columns):
                ref[z, x, 0:8, :] = blank
                ref[z, x, top : top + 8, :] = blank
        return carry

    lax.fori_loop(0, 10, clear, 0)
    for ref in (one, two):
        for z in (0, 9):
            for x in range(columns):
                ref[z, x, 8:top, :] = jnp.zeros((height + 8, LANES), F32)

    def place(u_row, c_row, tile):
        for x in range(columns):
            for z in range(8):
                one[1 + z, x, 8 + tile : 16 + tile, :] = blank
                coef_a[z, x, tile : tile + 8, :] = blank
                coef_b[z, x, tile : tile + 8, :] = blank
                coef_k[z, x, tile : tile + 8, :] = blank
        for x, span in enumerate(spans):
            for i in range(4):
                one[1:9, x, u_row + i, :] = got_ref[i, :, span]
            for i in range(3):
                k = DT * got_ref[4 + i, :, span]
                g = DT * got_ref[7 + i, :, span]
                coef_k[:, x, c_row + i, :] = k
                coef_b[:, x, c_row + i, :] = g * (1.0 / 3.0)
                coef_a[:, x, c_row + i, :] = 1.0 + (g - 6.0 * k)

    @pl.when(above)
    def _():
        place(8 + height, height, height)

    @pl.when(jnp.logical_not(above))
    def _():
        place(12, 5, 0)

    k_copy.wait()
    g_copy.wait()

    def widen(z, carry):
        for x, span in enumerate(spans):
            for r in range(0, height, 16):
                k = DT * k_nat[z, r : r + 16, span].astype(F32)
                g = DT * g_nat[z, r : r + 16, span].astype(F32)
                rows = pl.ds(own + r, 16)
                coef_k[z, x, rows, :] = k
                coef_b[z, x, rows, :] = g * (1.0 / 3.0)
                coef_a[z, x, rows, :] = 1.0 + (g - 6.0 * k)
        return carry

    lax.fori_loop(0, 8, widen, 0)
    for copy in copies:
        copy.wait()

    lane = lax.broadcasted_iota(jnp.int32, (8, LANES), 1)
    first, final = lane == 0, lane == LANES - 1

    def sweep(source, target, level, shift):
        def body(z, carry):
            for row in range(8, top, 8):
                tiles = [source[z + 1, x, row : row + 8, :] for x in range(columns)]
                back = [pltpu.roll(t, LANES - 1, 1) for t in tiles] + [blank]
                forth = [blank] + [pltpu.roll(t, 1, 1) for t in tiles]
                for x, u in enumerate(tiles):
                    x_next = jnp.where(final, back[x + 1], back[x])
                    x_prev = jnp.where(first, forth[x], forth[x + 1])
                    plus = source[z + 1, x, row + 1 : row + 9, :] + x_next
                    minus = source[z + 1, x, row - 1 : row + 7, :] + x_prev
                    levels = source[z, x, row : row + 8, :] + source[z + 2, x, row : row + 8, :]
                    rows = slice(row - 8, row)
                    own_part = u * (coef_a[z, x, rows, :] - coef_b[z, x, rows, :] * (u * u))
                    spread = coef_k[z, x, rows, :] * ((plus + minus) + levels)
                    out = (own_part + spread) - (0.5 * VEL * DT) * (plus - minus)
                    if shift is None:
                        target[z + level, x, row : row + 8, :] = out
                    else:
                        target[z + level, x, pl.ds(pl.multiple_of(row + shift, 8), 8), :] = out
            return carry

        lax.fori_loop(0, 8, body, 0, unroll=2)

    def keep(step, source):
        def write(row):
            for x, span in enumerate(spans):
                for i in range(2):
                    steps_ref[2 * step + i, :, span] = source[1:9, x, row + i, :]

        @pl.when(above)
        def _():
            write(8 + step)

        @pl.when(jnp.logical_not(above))
        def _():
            write(16 + height - 2 - step)

    def keep_coefs(row):
        for x, span in enumerate(spans):
            for i in range(4):
                coefs_ref[0, i, :, span] = coef_a[:, x, row + i, :]
                coefs_ref[1, i, :, span] = coef_b[:, x, row + i, :]
                coefs_ref[2, i, :, span] = coef_k[:, x, row + i, :]

    @pl.when(above)
    def _():
        keep_coefs(0)

    @pl.when(jnp.logical_not(above))
    def _():
        keep_coefs(8 + height - 4)

    pool = pool_matrix(breadth, 1.0 / 16.0)

    def sums_of(ref, level, start):
        def body(z, carry):
            for x, span in enumerate(spans):
                parts = [ref[z + level, x, pl.ds(start + i, small, stride=4), :] for i in range(4)]
                flat[z, :, span] = (parts[0] + parts[1]) + (parts[2] + parts[3])
            return carry

        lax.fori_loop(0, 8, body, 0)

    def pooled_into(ref, level, start, target, scale):
        sums_of(ref, level, start)
        mean = split_dot(flat[...].reshape(8 * small, breadth), pool) * scale
        flat[:, :, 0:thin] = mean.reshape(8, small, thin)
        for r in range(small):
            target[r] = flat[:, r, 0:thin]

    pooled_into(one, 1, 8 + own, coarse_ref.at[0], 1.0)
    pooled_into(coef_k, 0, own, coarse_ref.at[1], 2.0)
    pooled_into(coef_b, 0, own, coarse_ref.at[2], 6.0)
    keep(0, one)
    sweep(one, two, 1, None)
    keep(1, two)
    sweep(two, one, 1, None)
    keep(2, one)
    sweep(one, two, 1, None)
    keep(3, two)
    sweep(two, fine_ref, 0, jnp.where(above, 0, -8))
    pooled_into(fine_ref, 0, 8, end_ref, 1.0)


def inner(starts, diffusivity, reaction, got):
    height, breadth = starts.shape[2:]
    small = height // 4
    columns = breadth // LANES
    wide = pltpu.VMEM((10, columns, height + 24, LANES), F32)
    coef = pltpu.VMEM((8, columns, height + 8, LANES), F32)
    return pl.pallas_call(
        inner_kernel,
        out_shape=[
            struct(8, columns, height + 16, LANES),
            struct(8, 8, breadth),
            struct(3, 4, 8, breadth),
            struct(3, small, 8, breadth // 4),
            struct(small, 8, breadth // 4),
        ],
        in_specs=[ANY] * 3 + [VMEM],
        out_specs=[VMEM] * 5,
        scratch_shapes=[wide, wide, coef, coef, coef]
        + [
            pltpu.VMEM((8, height, breadth), BF16),
            pltpu.VMEM((8, height, breadth), BF16),
            pltpu.VMEM((8, small, breadth), F32),
            pltpu.SemaphoreType.DMA((columns + 2,)),
        ],
        compiler_params=params(28),
        cost_estimate=pl.CostEstimate(flops=30_000_000, bytes_accessed=4_000_000, transcendentals=0),
        name="inner_updates",
    )(starts, diffusivity, reaction, got)


def rows_for(array, low_side, reach):
    start = jnp.where(low_side, 0, array.shape[1] - reach)
    return lax.dynamic_slice_in_dim(array, start, reach, axis=1)


def exchanges(count):
    even = [(i, i ^ 1) for i in range(count)]
    odd = [(i, (i - 1 if i % 2 == 0 else i + 1) % count) for i in range(count)]
    return even, odd


def alive():
    place = lax.axis_index("space")
    last = lax.axis_size("space") - 1
    return jnp.where(jnp.logical_or(place == 0, place == last), 0.0, 1.0).astype(F32)


def edge_kernel(
    steps_ref, coefs_ref, got_ref, even_ref, end_in, coarse_ref, rows_ref, end_ref, jump_ref,
    zero, one, two, three, coef_a, coef_b, coef_k, seen, half, coarse_k, coarse_g,
):
    breadth = got_ref.shape[2]
    small = end_ref.shape[0]
    low_side = parity() == 0
    live = alive()
    edges = masks()
    states = (zero, one, two, three, rows_ref)
    got_u = jnp.where(low_side, 0, 8)
    got_c = jnp.where(low_side, 1, 8)
    for i in range(4):
        zero[got_u + i] = got_ref[i] * live
        coef_a[4 + i] = coefs_ref[0, i]
        coef_b[4 + i] = coefs_ref[1, i]
        coef_k[4 + i] = coefs_ref[2, i]
    for i in range(3):
        set_coefs(got_ref[4 + i], got_ref[7 + i], coef_a, coef_b, coef_k, got_c + i)
    for step in range(4):
        at = jnp.where(low_side, 4 + step, 6 - step)
        for i in range(2):
            states[step][at + i] = steps_ref[2 * step + i]
    for step in range(1, 5):
        at = jnp.where(low_side, step, 8 - step)
        for i in range(4):
            tiles = fine_row(states[step - 1], at + i, coef_a, coef_b, coef_k, at + i, breadth, edges)
            outside = jnp.logical_or(
                jnp.logical_and(low_side, i < 4 - step), jnp.logical_and(jnp.logical_not(low_side), i >= step)
            )
            if step < 4:
                factor = jnp.where(outside, live, 1.0)
                put_tiles(states[step], at + i, [t * factor for t in tiles])
            else:
                put_tiles(rows_ref, i, tiles)
    pool = pool_matrix(breadth, 1.0 / 16.0)
    end_ref[...] = end_in[...]
    end_ref[jnp.where(low_side, 0, small - 1)] = pooled(rows_ref, 0, 1, pool)

    thin = breadth // 4
    odd_at = jnp.where(low_side, 0, 2 + small)
    even_at = jnp.where(low_side, 2 + small, 0)
    near = jnp.where(low_side, 1, 2 + small)
    far = jnp.where(low_side, 2 + small, 1)
    for r in range(small):
        seen[2 + r] = coarse_ref[0, r]
        coarse_k[2 + r] = coarse_ref[1, r]
        coarse_g[2 + r] = coarse_ref[2, r]
    for i in range(2):
        span = slice(i * thin, (i + 1) * thin)
        seen[odd_at + i] = got_ref[10, :, span] * live
        seen[even_at + i] = even_ref[10, :, span]
    for i, ref in ((2, coarse_k), (3, coarse_g)):
        span = slice(i * thin, (i + 1) * thin)
        ref[near] = got_ref[10, :, span]
        ref[far] = even_ref[10, :, span]
    coarse_sweep(seen, half, coarse_k, coarse_g, 1, small + 3, 2, small, low_side, live, edges)
    first = lax.axis_index("tm") == 0
    for r in range(small):
        tiles = coarse_row(half, 2 + r, coarse_k, coarse_g, 2 + r, thin, edges)
        for i, tile in enumerate(tiles):
            span = slice(i * LANES, (i + 1) * LANES)
            jump_ref[r, :, span] = end_ref[r, :, span] - jnp.where(first, 0.0, tile)


def fill_coarse(wide, own, even_part, odd_part, reach, low_side, live):
    rows = own.shape[0]
    count = even_part.shape[0]
    for r in range(rows):
        wide[reach + r] = own[r]
    odd_at = jnp.where(low_side, 0, reach + rows)
    even_at = jnp.where(low_side, reach + rows, 0)
    odd_from = jnp.where(low_side, count - reach, 0)
    even_from = jnp.where(low_side, 0, count - reach)
    for i in range(reach):
        wide[odd_at + i] = odd_part[odd_from + i] * live
        wide[even_at + i] = even_part[even_from + i]


def coarse_sweep(source, target, coef_k, coef_g, low, high, reach, rows, low_side, live, edges, shift=0):
    breadth = source.shape[2]
    for row in range(low, high):
        tiles = coarse_row(source, row, coef_k, coef_g, row + shift, breadth, edges)
        if row < reach:
            factor = jnp.where(low_side, live, 1.0)
            tiles = [t * factor for t in tiles]
        elif row >= reach + rows:
            factor = jnp.where(low_side, 1.0, live)
            tiles = [t * factor for t in tiles]
        put_tiles(target, row, tiles)


def edge(steps, coefs, got, even_got, end, coarse):
    breadth = got.shape[2]
    small = end.shape[0]
    wide = pltpu.VMEM((12, 8, breadth), F32)
    thin = pltpu.VMEM((small + 4, 8, breadth // 4), F32)
    return pl.pallas_call(
        edge_kernel,
        out_shape=[
            struct(4, 8, breadth),
            struct(small, 8, breadth // 4),
            struct(small, 8, breadth // 4),
        ],
        in_specs=[VMEM] * 6,
        out_specs=[VMEM] * 3,
        scratch_shapes=[wide] * 7 + [thin] * 4,
        compiler_params=params(16),
        name="edge_updates",
    )(steps, coefs, got, even_got, end, coarse)


def last_kernel(
    fine_hbm, rows_ref, end_ref, jump_ref, before_ref, even_j, odd_j, coarse_ref, even_c, odd_c, out_hbm,
    fine_ref, out_ref, one, two, coarse_k, coarse_g, added, change, moved, sems,
):
    behind = before_ref.shape[0]
    reach = COARSE * behind
    height, breadth = out_hbm.shape[2:]
    columns = breadth // LANES
    small = height // 4
    fetch = pltpu.make_async_copy(fine_hbm, fine_ref, sems.at[8])
    fetch.start()
    low_side = parity() == 0
    live = alive()
    edges = masks()
    slice_id = lax.axis_index("tm")
    fill_coarse(coarse_k, coarse_ref.at[1], even_c.at[0], odd_c.at[0], reach, low_side, live)
    fill_coarse(coarse_g, coarse_ref.at[2], even_c.at[1], odd_c.at[1], reach, low_side, live)
    at = 0
    for j in range(behind):
        width = reach - COARSE * j
        ok = jnp.where(slice_id >= behind - j, 1.0, 0.0).astype(F32)
        target = one if j == 0 else added
        base = reach - width
        for r in range(small):
            target[reach + r] = before_ref[j, r] * ok
        odd_at = jnp.where(low_side, base, reach + small)
        even_at = jnp.where(low_side, reach + small, base)
        for i in range(width):
            target[odd_at + i] = odd_j[at + i] * (ok * live)
            target[even_at + i] = even_j[at + i] * ok
        at += width
        if j > 0:
            for r in range(base, reach + small + width):
                one[r] = one[r] + added[r]
        coarse_sweep(one, two, coarse_k, coarse_g, base + 1, reach + small + width - 1, reach, small, low_side, live, edges)
        coarse_sweep(two, one, coarse_k, coarse_g, base + 2, reach + small + width - 2, reach, small, low_side, live, edges)
    for r in range(small):
        change[:, r, :] = (one[reach + r] + jump_ref[r]) - end_ref[r]
    spread = spread_matrix(breadth)
    moved[...] = split_dot(change[...].reshape(8 * small, breadth // 4), spread).reshape(8, small, breadth)
    fetch.wait()

    def fix(row):
        for x in range(columns):
            for i in range(4):
                fine_ref[:, x, row + i, :] = rows_ref[i, :, x * LANES : (x + 1) * LANES]

    @pl.when(low_side)
    def _():
        fix(8)

    @pl.when(jnp.logical_not(low_side))
    def _():
        fix(8 + height - 4)

    lower = lax.broadcasted_iota(jnp.int32, (8, LANES), 0) < 4

    def body(z, carry):
        for x in range(columns):
            span = slice(x * LANES, (x + 1) * LANES)
            for row in range(0, height, 8):
                c = row // 4
                step = jnp.where(lower, moved[z, c : c + 1, span], moved[z, c + 1 : c + 2, span])
                out_ref[z, row : row + 8, span] = fine_ref[z, x, 8 + row : 16 + row, :] + step
        pltpu.make_async_copy(out_ref.at[z], out_hbm.at[0, z], sems.at[z]).start()
        return carry

    lax.fori_loop(0, 8, body, 0)
    for z in range(8):
        pltpu.make_async_copy(out_ref.at[z], out_hbm.at[0, z], sems.at[z]).wait()


def last(fine, rows, end, jump, before, even_j, odd_j, coarse, even_c, odd_c, height):
    breadth = rows.shape[2]
    small = height // 4
    reach = COARSE * before.shape[0]
    thin = pltpu.VMEM((small + 2 * reach, 8, breadth // 4), F32)
    return pl.pallas_call(
        last_kernel,
        out_shape=struct(1, 8, height, breadth),
        in_specs=[ANY] + [VMEM] * 9,
        out_specs=HBM,
        scratch_shapes=[pltpu.VMEM(fine.shape, F32), pltpu.VMEM((8, height, breadth), F32)]
        + [thin] * 5
        + [
            pltpu.VMEM((8, small, breadth // 4), F32),
            pltpu.VMEM((8, small, breadth), F32),
            pltpu.SemaphoreType.DMA((9,)),
        ],
        compiler_params=params(16),
        name="chain_and_spread",
    )(fine, rows, end, jump, before, even_j, odd_j, coarse, even_c, odd_c)


def relay(jump, coarse, even_c, odd_c, even, odd):
    low_side = parity() == 0
    live = alive()
    small = jump.shape[0]

    def widened(own, even_part, odd_part):
        odd_part = odd_part * live
        low = jnp.where(low_side, odd_part, even_part)
        high = jnp.where(low_side, even_part, odd_part)
        return jnp.concatenate([low, own, high], axis=1)

    def update(values, k, g):
        rows = values.shape[0] - 2
        middle = values[1:-1]
        plus = values[2:] + jnp.pad(middle, ((0, 0), (0, 0), (0, 1)))[:, :, 1:]
        minus = values[:-2] + jnp.pad(middle, ((0, 0), (0, 0), (1, 0)))[:, :, :-1]
        levels = jnp.pad(middle, ((0, 0), (0, 1), (0, 0)))[:, 1:] + jnp.pad(middle, ((0, 0), (1, 0), (0, 0)))[:, :-1]
        bend = levels - 2.0 * middle + (plus + minus - 4.0 * middle) / 16.0
        drift = VEL * (plus - minus) / 8.0
        return middle + (k * bend - 2.0 * DT * drift + g * (middle - middle * middle * middle / 3.0))

    coefs = widened(coarse[1:], even_c, odd_c)
    place = lax.axis_index("space")
    start = jnp.where(place == 0, 1, 0)
    stop = jnp.where(place == lax.axis_size("space") - 1, small + 1, small + 2)
    row = jnp.arange(small + 2)[:, None, None]
    inside = jnp.logical_and(row >= start, row < stop)

    def advance(values):
        block = values[None]
        even_v = lax.ppermute(rows_for(block, jnp.logical_not(low_side), 2), "space", even)
        odd_v = lax.ppermute(rows_for(block, low_side, 2), "space", odd)
        wide = widened(block, even_v, odd_v)[0]
        wide = jnp.where(inside, update(wide, coefs[0, 1:-1], coefs[1, 1:-1]), 0.0)
        return update(wide, coarse[1], coarse[2])

    slice_id = lax.axis_index("tm")
    slices = lax.axis_size("tm")
    onward = [(i, i + 1) for i in range(slices - 1)]

    def link(position, state):
        incoming = lax.ppermute(state, "tm", onward)
        return jnp.where(slice_id > 0, advance(incoming), 0.0) + jump

    return lax.fori_loop(0, slices - 1, link, jump)


def per_device(starts, diffusivity, reaction):
    height, breadth = starts.shape[2:]
    small = height // 4
    slices = lax.axis_size("tm")
    behind = slices - 1
    reach = COARSE * behind
    at_once = 0 < behind and reach <= small
    even, odd = exchanges(lax.axis_size("space"))
    low_side = parity() == 0
    high_side = jnp.logical_not(low_side)

    even_rows, odd_rows = pack(starts, diffusivity, reaction)
    odd_got = lax.ppermute(odd_rows, "space", odd)
    even_got = lax.ppermute(even_rows, "space", even)
    fine, steps, coefs, coarse, end = inner(starts, diffusivity, reaction, even_got)
    rows, end, jump = edge(steps, coefs, odd_got, even_got, end, coarse)
    width = reach if at_once else COARSE
    later, jump = lax.optimization_barrier((coarse[1:], jump))
    odd_c = lax.ppermute(rows_for(later, low_side, width), "space", odd)
    even_c = lax.ppermute(rows_for(later, high_side, width), "space", even)
    if at_once:
        before = [
            lax.ppermute(jump, "tm", [(i, (i + k) % slices) for i in range(slices)])
            for k in range(behind, 0, -1)
        ]
        before = jnp.stack(before)

        def outer(low):
            return jnp.concatenate(
                [rows_for(before[j][None], low, reach - COARSE * j)[0] for j in range(behind)], axis=0
            )

        odd_j = lax.ppermute(outer(low_side), "space", odd)
        even_j = lax.ppermute(outer(high_side), "space", even)
        return last(fine, rows, end, jump, before, even_j, odd_j, coarse, even_c, odd_c, height)
    chained = relay(jump, coarse, even_c, odd_c, even, odd)
    change = jnp.repeat(jnp.repeat(jnp.transpose(chained - end, (1, 0, 2)), 4, axis=1), 4, axis=2)
    fixed = jnp.where(low_side, 0, height - 4)
    fine = jnp.transpose(fine[:, :, 8 : 8 + height], (0, 2, 1, 3)).reshape(8, height, breadth)
    fine = lax.dynamic_update_slice_in_dim(fine, jnp.transpose(rows, (1, 0, 2)), fixed, axis=1)
    return (fine + change)[None]


def solution(mesh):
    in_specs = (P("tm", None, "space", None), P(None, "space", None), P(None, "space", None))
    out_specs = P("tm", None, "space", None)
    return jax.shard_map(per_device, mesh=mesh, in_specs=in_specs, out_specs=out_specs, check_vma=False)
```

time: 51.4 us -> 35 us (0.68)
  waiting for transfers between devices: 16.1 us -> 6.43 us
  Pallas kernels: 18 us -> 12 us
  local copies, waits for them, and re-layouts: 5.07 us -> 3.38 us
  starting transfers between devices: 11.8 us -> 12.8 us
    ppermute x2, waiting for transfers between devices: 5.23 us -> 0.01 us  [the longest x1 0.01 us: per_device(): even_c = lax.ppermute(rows_for(later, high_side, width), 'space', even)]
    pallas_call x2, Pallas kernels: 12.7 us -> 8.89 us  [the longest x1 7.96 us: inner(): pl.pallas_call(inner_kernel, out_shape=[struct(8, columns, height + 16, L...]
    ppermute x3, waiting for transfers between devices: 6.16 us -> 2.82 us  [per_device(): lax.ppermute(jump, 'tm', [(i, (i + k) % slices) for i in range(slices)])]
    pallas_call x1, Pallas kernels: 2.98 us -> 0.87 us  [edge(): pl.pallas_call(edge_kernel, out_shape=[struct(4, 8, breadth), struct(smal...]
    unnamed x16 -> x12, local copies, waits for them, and re-layouts: 5.03 us -> 3.32 us
    ppermute x1, waiting for transfers between devices: 4.69 us -> 3.44 us  [per_device(): odd_j = lax.ppermute(outer(low_side), 'space', odd)]
    ppermute x3, starting transfers between devices: 4.66 us -> 5.91 us  [per_device(): lax.ppermute(jump, 'tm', [(i, (i + k) % slices) for i in range(slices)])]
    ppermute x2, starting transfers between devices: 1.68 us -> 0.76 us  [the longest x1 0.76 us: per_device(): odd_c = lax.ppermute(rows_for(later, low_side, width), 'space', odd)]
  transfers between devices with their start and end apart: 9 -> 9, of which waited for: 5 -> 3; matrix products, arithmetic and copies ran while one was open for 0% -> 0% of each run, Pallas kernels for 23% -> 23%
where the time goes in v2:
time: 35 us; the launch traced here: 34.7 us
  starting transfers between devices  12.8 us (37%)
  Pallas kernels  12 us (34%)
  waiting for transfers between devices  6.43 us (18%)
  local copies, waits for them, and re-layouts  3.38 us (10%)
    pallas_call x1, Pallas kernels, inner(): pl.pallas_call(inner_kernel, out_shape=[struct(8, columns, height + 16, L...  7.96 us
    ppermute x3, starting transfers between devices, per_device(): lax.ppermute(jump, 'tm', [(i, (i + k) % slices) for i in range(slices)])  5.91 us
    ppermute x1, starting transfers between devices, per_device(): odd_got = lax.ppermute(odd_rows, 'space', odd)  3.54 us
    ppermute x1, waiting for transfers between devices, per_device(): odd_j = lax.ppermute(outer(low_side), 'space', odd)  3.44 us
    unnamed x12, local copies, waits for them, and re-layouts  3.32 us
    ppermute x3, waiting for transfers between devices, per_device(): lax.ppermute(jump, 'tm', [(i, (i + k) % slices) for i in range(slices)])  2.82 us
    pallas_call x1, Pallas kernels, last(): pl.pallas_call(last_kernel, out_shape=struct(1, 8, height, breadth), in_s...  2.2 us
    ppermute x1, starting transfers between devices, per_device(): odd_j = lax.ppermute(outer(low_side), 'space', odd)  1.98 us
  transfers between devices with their start and end apart: 9, of which 3 were waited for; matrix products, arithmetic and copies ran while one was open for 0% of the time, Pallas kernels for 23%

profile of v2, /device:TPU:0, one launch (start us, length us, event | category | flops | bytes accessed | tf_op | source)
XLA Modules:
  0.0 34.7 jit_solution(1736662670479898864)
XLA Ops:
  0.0 0.0 copy-start
  0.0 1.2 %copy-done = f32[1,8,32,1024]{3,2,1,0:T(8,128)S(1)} copy-done((f32[1,8,32,1024]{3,2,1,0:T(8,128)S(1)}, f32[1,8,32,1024]{3,2,1,0:T(8,128)}, u32[]{:S(2)}) %copy-start) | copy-done | bytes 1048600
  1.2 0.0 copy-start.2
  1.2 1.0 %copy-done.2 = bf16[8,32,1024]{2,1,0:T(8,128)(2,1)S(1)} copy-done((bf16[8,32,1024]{2,1,0:T(8,128)(2,1)S(1)}, bf16[8,32,1024]{2,1,0:T(8,128)(2,1)}, u32[]{:S(2)}) %copy-start.2) | copy-done | bytes 524312
  2.3 0.0 copy-start.4
  2.3 1.0 %copy-done.4 = bf16[8,32,1024]{2,1,0:T(8,128)(2,1)S(1)} copy-done((bf16[8,32,1024]{2,1,0:T(8,128)(2,1)S(1)}, bf16[8,32,1024]{2,1,0:T(8,128)(2,1)}, u32[]{:S(2)}) %copy-start.4) | copy-done | bytes 524312
  3.3 0.0 copy-start.1
  3.3 0.0 copy-start.3
  3.3 0.0 copy-start.5
  3.3 0.9 %pack_rows.1 = (f32[11,8,1024]{2,1,0:T(8,128)S(1)}, f32[11,8,1024]{2,1,0:T(8,128)S(1)}) custom-call(f32[1,8,32,1024]{3,2,1,0:T(8,128)S(1)} %copy-done, bf16[8,32,1024]{2,1,0:T(8,128)(2,1)S(1)} %copy-done.2, bf16[8,32,1024]{2,1,0:T(8,128)(2,1)S(1)} %copy-done.4), custom_call_target="tpu_custom_call" | custom-call | tf_op jit(solution)/shard_map/pack_rows/pallas_call | solution.py:180
  4.3 0.5 %collective-permute-start = (f32[11,8,1024]{2,1,0:T(8,128)S(1)}, f32[11,8,1024]{2,1,0:T(8,128)S(1)}, u32[]{:S(2)}, u32[]{:S(2)}) collective-permute-start(f32[11,8,1024]{2,1,0:T(8,128)S(1)} %get-tuple-element.17), channel_id=1, source_target_pairs={{0,1},{1,0},{2,3},{3,2},{4,5},{5,4},{6,7},{7,6},{8,9},{9,8},{10,11... | collective-permute-start | bytes 1081352 | tf_op jit(solution)/shard_map/ppermute | solution.py:679
  4.8 3.5 %collective-permute-start.1 = (f32[11,8,1024]{2,1,0:T(8,128)S(1)}, f32[11,8,1024]{2,1,0:T(8,128)S(1)}, u32[]{:S(2)}, u32[]{:S(2)}) collective-permute-start(f32[11,8,1024]{2,1,0:T(8,128)S(1)} %get-tuple-element.21), channel_id=1, source_target_pairs={{0,7},{1,2},{2,1},{3,4},{4,3},{5,6},{6,5},{7,0},{8,15},{9,10},{10,... | collective-permute-start | bytes 1081352 | tf_op jit(solution)/shard_map/ppermute | solution.py:678
  8.3 0.0 collective-permute-done.got_ref.even_ref
  8.3 0.0 copy-done.1
  8.3 0.0 copy-done.3
  8.3 0.0 copy-done.5
  8.3 8.0 %inner_updates.1 = (f32[8,8,48,128]{3,2,1,0:T(8,128)S(1)}, f32[8,8,1024]{2,1,0:T(8,128)S(1)}, f32[3,4,8,1024]{3,2,1,0:T(8,128)S(1)}, f32[3,8,8,256]{3,2,1,0:T(8,128)S(1)}, f32[8,8,256]{2,1,0:T(8,128)S(1)}) custom-call(f32[1,8,32,1024]{3,2,1,0:T(8,128)S(1)} %copy-done.1, bf16[8,32,1024]{2,1,0:T(8,128)(2,1)S(1)} %copy-done.3, ...), custom_call_target="tpu_custom_call" | custom-call | flops 30000000 | bytes 4000000 | tf_op jit(solution)/shard_map/inner_updates/pallas_call | solution.py:372
  16.3 0.2 collective-permute-done.1.got_ref
  16.5 0.9 %edge_updates.1 = (f32[4,8,1024]{2,1,0:T(8,128)S(1)}, f32[8,8,256]{2,1,0:T(8,128)S(1)}, f32[8,8,256]{2,1,0:T(8,128)S(1)}) custom-call(f32[8,8,1024]{2,1,0:T(8,128)S(1)} %get-tuple-element.19.steps_ref, f32[3,4,8,1024]{3,2,1,0:T(8,128)S(1)} %get-tuple-element.20.coefs_ref, f32[11,8,1024]{2,1,0:T(8,128)S(1)} %collective-permute-done.1.got_ref, ...), custom_call_target="tpu_custom_call" | custom-call | tf_op jit(solution)/shard_map/edge_updates/pallas_call | solution.py:510
  17.4 2.0 %collective-permute-start.4 = (f32[8,8,256]{2,1,0:T(8,128)S(1)}, f32[8,8,256]{2,1,0:T(8,128)S(1)}, u32[]{:S(2)}, u32[]{:S(2)}) collective-permute-start(f32[8,8,256]{2,1,0:T(8,128)S(1)} %get-tuple-element.27.jump_ref), channel_id=1, source_target_pairs={{0,8},{8,16},{16,24},{24,0},{1,9},{9,17},{17,25},{25,1},{2,10},{10... | collective-permute-start | bytes 196616 | tf_op jit(solution)/shard_map/ppermute | solution.py:688
  19.3 2.6 %collective-permute-start.3 = (f32[8,8,256]{2,1,0:T(8,128)S(1)}, f32[8,8,256]{2,1,0:T(8,128)S(1)}, u32[]{:S(2)}, u32[]{:S(2)}) collective-permute-start(f32[8,8,256]{2,1,0:T(8,128)S(1)} %get-tuple-element.27.jump_ref), channel_id=1, source_target_pairs={{0,16},{8,24},{16,0},{24,8},{1,17},{9,25},{17,1},{25,9},{2,18},{10... | collective-permute-start | bytes 196616 | tf_op jit(solution)/shard_map/ppermute | solution.py:688
  21.9 1.3 %collective-permute-start.2 = (f32[8,8,256]{2,1,0:T(8,128)S(1)}, f32[8,8,256]{2,1,0:T(8,128)S(1)}, u32[]{:S(2)}, u32[]{:S(2)}) collective-permute-start(f32[8,8,256]{2,1,0:T(8,128)S(1)} %get-tuple-element.27.jump_ref), channel_id=1, source_target_pairs={{0,24},{8,0},{16,8},{24,16},{1,25},{9,1},{17,9},{25,17},{2,26},{10... | collective-permute-start | bytes 196616 | tf_op jit(solution)/shard_map/ppermute | solution.py:688
  23.3 0.8 %collective-permute-start.8 = (f32[2,6,8,256]{3,2,1,0:T(8,128)S(1)}, f32[2,6,8,256]{3,2,1,0:T(8,128)S(1)}, u32[]{:S(2)}, u32[]{:S(2)}) collective-permute-start(f32[2,6,8,256]{3,2,1,0:T(8,128)S(1)} %get-tuple-element.29), channel_id=1, source_target_pairs={{0,7},{1,2},{2,1},{3,4},{4,3},{5,6},{6,5},{7,0},{8,15},{9,10},{10,... | collective-permute-start | bytes 294920 | tf_op jit(solution)/shard_map/ppermute | solution.py:684
  24.1 0.0 collective-permute-start.7
  24.1 2.8 %collective-permute-done.2 = f32[8,8,256]{2,1,0:T(8,128)S(1)} collective-permute-done((f32[8,8,256]{2,1,0:T(8,128)S(1)}, f32[8,8,256]{2,1,0:T(8,128)S(1)}, u32[]{:S(2)}, u32[]{:S(2)}) %collective-permute-start.2) | collective-permute-done | bytes 65568 | tf_op jit(solution)/shard_map/ppermute | solution.py:688
  26.9 0.0 collective-permute-done.4
  26.9 0.0 collective-permute-done.3
  27.0 0.1 collective-permute-start.5
  27.1 2.0 %collective-permute-start.6 = (f32[12,8,256]{2,1,0:T(8,128)S(1)}, f32[12,8,256]{2,1,0:T(8,128)S(1)}, u32[]{:S(2)}, u32[]{:S(2)}) collective-permute-start(f32[12,8,256]{2,1,0:T(8,128)S(1)} %pad_maximum_fusion.2), channel_id=1, source_target_pairs={{0,7},{1,2},{2,1},{3,4},{4,3},{5,6},{6,5},{7,0},{8,15},{9,10},{10,... | collective-permute-start | bytes 294920 | tf_op jit(solution)/shard_map/ppermute | solution.py:698
  29.1 0.0 collective-permute-done.8.odd_c
  29.1 0.0 collective-permute-done.7.even_c
  29.1 0.0 collective-permute-done.5.even_j
  29.1 3.4 %collective-permute-done.6.odd_j = f32[12,8,256]{2,1,0:T(8,128)S(1)} collective-permute-done((f32[12,8,256]{2,1,0:T(8,128)S(1)}, f32[12,8,256]{2,1,0:T(8,128)S(1)}, u32[]{:S(2)}, u32[]{:S(2)}) %collective-permute-start.6) | collective-permute-done | bytes 98336 | tf_op jit(solution)/shard_map/ppermute | solution.py:698
  32.5 2.2 %chain_and_spread.1 = f32[1,8,32,1024]{3,2,1,0:T(8,128)} custom-call(f32[8,8,48,128]{3,2,1,0:T(8,128)S(1)} %get-tuple-element.18.fine_hbm, f32[4,8,1024]{2,1,0:T(8,128)S(1)} %get-tuple-element.24.rows_ref, f32[8,8,256]{2,1,0:T(8,128)S(1)} %get-tuple-element.25.end_ref, f32[8,8,256]{2,1,0:T(8,128)S(1)} %get-tuple-element.27.jump_ref, ...), custom_call_target="tpu_custom_call" | custom-call | tf_op jit(solution)/shard_map/chain_and_spread/pallas_call | solution.py:602
  (8 shorter events, 0.1 us)
Async XLA Ops:
  0.0 1.2 %copy-start = (f32[1,8,32,1024]{3,2,1,0:T(8,128)S(1)}, f32[1,8,32,1024]{3,2,1,0:T(8,128)}, u32[]{:S(2)}) copy-start(f32[1,8,32,1024]{3,2,1,0:T(8,128)} %u_hbm.3) | copy-start | bytes 3145732
  1.2 1.0 %copy-start.2 = (bf16[8,32,1024]{2,1,0:T(8,128)(2,1)S(1)}, bf16[8,32,1024]{2,1,0:T(8,128)(2,1)}, u32[]{:S(2)}) copy-start(bf16[8,32,1024]{2,1,0:T(8,128)(2,1)} %k_hbm.3) | copy-start | bytes 1572868
  2.3 1.0 %copy-start.4 = (bf16[8,32,1024]{2,1,0:T(8,128)(2,1)S(1)}, bf16[8,32,1024]{2,1,0:T(8,128)(2,1)}, u32[]{:S(2)}) copy-start(bf16[8,32,1024]{2,1,0:T(8,128)(2,1)} %g_hbm.3) | copy-start | bytes 1572868
  3.3 5.0 %copy-start.1 = (f32[1,8,32,1024]{3,2,1,0:T(8,128)S(1)}, f32[1,8,32,1024]{3,2,1,0:T(8,128)}, u32[]{:S(2)}) copy-start(f32[1,8,32,1024]{3,2,1,0:T(8,128)} %u_hbm.3) | copy-start | bytes 3145732
  3.3 5.0 %copy-start.3 = (bf16[8,32,1024]{2,1,0:T(8,128)(2,1)S(1)}, bf16[8,32,1024]{2,1,0:T(8,128)(2,1)}, u32[]{:S(2)}) copy-start(bf16[8,32,1024]{2,1,0:T(8,128)(2,1)} %k_hbm.3) | copy-start | bytes 1572868
  3.3 5.0 %copy-start.5 = (bf16[8,32,1024]{2,1,0:T(8,128)(2,1)S(1)}, bf16[8,32,1024]{2,1,0:T(8,128)(2,1)}, u32[]{:S(2)}) copy-start(bf16[8,32,1024]{2,1,0:T(8,128)(2,1)} %g_hbm.3) | copy-start | bytes 1572868
  4.3 4.1 %collective-permute-start = (f32[11,8,1024]{2,1,0:T(8,128)S(1)}, f32[11,8,1024]{2,1,0:T(8,128)S(1)}, u32[]{:S(2)}, u32[]{:S(2)}) collective-permute-start(f32[11,8,1024]{2,1,0:T(8,128)S(1)} %get-tuple-element.17), channel_id=1, source_target_pairs={{0,1},{1,0},{2,3},{3,2},{4,5},{5,4},{6,7},{7,6},{8,9},{9,8},{10,11... | collective-permute-start | bytes 1081352 | tf_op jit(solution)/shard_map/ppermute | solution.py:679
  4.8 11.7 %collective-permute-start.1 = (f32[11,8,1024]{2,1,0:T(8,128)S(1)}, f32[11,8,1024]{2,1,0:T(8,128)S(1)}, u32[]{:S(2)}, u32[]{:S(2)}) collective-permute-start(f32[11,8,1024]{2,1,0:T(8,128)S(1)} %get-tuple-element.21), channel_id=1, source_target_pairs={{0,7},{1,2},{2,1},{3,4},{4,3},{5,6},{6,5},{7,0},{8,15},{9,10},{10,... | collective-permute-start | bytes 1081352 | tf_op jit(solution)/shard_map/ppermute | solution.py:678
  17.4 9.5 %collective-permute-start.4 = (f32[8,8,256]{2,1,0:T(8,128)S(1)}, f32[8,8,256]{2,1,0:T(8,128)S(1)}, u32[]{:S(2)}, u32[]{:S(2)}) collective-permute-start(f32[8,8,256]{2,1,0:T(8,128)S(1)} %get-tuple-element.27.jump_ref), channel_id=1, source_target_pairs={{0,8},{8,16},{16,24},{24,0},{1,9},{9,17},{17,25},{25,1},{2,10},{10... | collective-permute-start | bytes 196616 | tf_op jit(solution)/shard_map/ppermute | solution.py:688
  19.3 7.6 %collective-permute-start.3 = (f32[8,8,256]{2,1,0:T(8,128)S(1)}, f32[8,8,256]{2,1,0:T(8,128)S(1)}, u32[]{:S(2)}, u32[]{:S(2)}) collective-permute-start(f32[8,8,256]{2,1,0:T(8,128)S(1)} %get-tuple-element.27.jump_ref), channel_id=1, source_target_pairs={{0,16},{8,24},{16,0},{24,8},{1,17},{9,25},{17,1},{25,9},{2,18},{10... | collective-permute-start | bytes 196616 | tf_op jit(solution)/shard_map/ppermute | solution.py:688
  21.9 4.9 %collective-permute-start.2 = (f32[8,8,256]{2,1,0:T(8,128)S(1)}, f32[8,8,256]{2,1,0:T(8,128)S(1)}, u32[]{:S(2)}, u32[]{:S(2)}) collective-permute-start(f32[8,8,256]{2,1,0:T(8,128)S(1)} %get-tuple-element.27.jump_ref), channel_id=1, source_target_pairs={{0,24},{8,0},{16,8},{24,16},{1,25},{9,1},{17,9},{25,17},{2,26},{10... | collective-permute-start | bytes 196616 | tf_op jit(solution)/shard_map/ppermute | solution.py:688
  23.3 5.8 %collective-permute-start.8 = (f32[2,6,8,256]{3,2,1,0:T(8,128)S(1)}, f32[2,6,8,256]{3,2,1,0:T(8,128)S(1)}, u32[]{:S(2)}, u32[]{:S(2)}) collective-permute-start(f32[2,6,8,256]{3,2,1,0:T(8,128)S(1)} %get-tuple-element.29), channel_id=1, source_target_pairs={{0,7},{1,2},{2,1},{3,4},{4,3},{5,6},{6,5},{7,0},{8,15},{9,10},{10,... | collective-permute-start | bytes 294920 | tf_op jit(solution)/shard_map/ppermute | solution.py:684
  24.1 5.0 %collective-permute-start.7 = (f32[2,6,8,256]{3,2,1,0:T(8,128)S(1)}, f32[2,6,8,256]{3,2,1,0:T(8,128)S(1)}, u32[]{:S(2)}, u32[]{:S(2)}) collective-permute-start(f32[2,6,8,256]{3,2,1,0:T(8,128)S(1)} %get-tuple-element.30), channel_id=1, source_target_pairs={{0,1},{1,0},{2,3},{3,2},{4,5},{5,4},{6,7},{7,6},{8,9},{9,8},{10,11... | collective-permute-start | bytes 294920 | tf_op jit(solution)/shard_map/ppermute | solution.py:685
  27.0 2.1 %collective-permute-start.5 = (f32[12,8,256]{2,1,0:T(8,128)S(1)}, f32[12,8,256]{2,1,0:T(8,128)S(1)}, u32[]{:S(2)}, u32[]{:S(2)}) collective-permute-start(f32[12,8,256]{2,1,0:T(8,128)S(1)} %pad_maximum_fusion.1), channel_id=1, source_target_pairs={{0,1},{1,0},{2,3},{3,2},{4,5},{5,4},{6,7},{7,6},{8,9},{9,8},{10,11... | collective-permute-start | bytes 294920 | tf_op jit(solution)/shard_map/ppermute | solution.py:699
  27.1 5.5 %collective-permute-start.6 = (f32[12,8,256]{2,1,0:T(8,128)S(1)}, f32[12,8,256]{2,1,0:T(8,128)S(1)}, u32[]{:S(2)}, u32[]{:S(2)}) collective-permute-start(f32[12,8,256]{2,1,0:T(8,128)S(1)} %pad_maximum_fusion.2), channel_id=1, source_target_pairs={{0,7},{1,2},{2,1},{3,4},{4,3},{5,6},{6,5},{7,0},{8,15},{9,10},{10,... | collective-permute-start | bytes 294920 | tf_op jit(solution)/shard_map/ppermute | solution.py:698

commit v3 on v2

--- a/solution.py
+++ b/solution.py
@@ -93,11 +93,10 @@
 
 def split_dot(values, matrix):
     high = values.astype(BF16)
-    rest = values - high.astype(F32)
-    mid = rest.astype(BF16)
-    low = (rest - mid.astype(F32)).astype(BF16)
-    dot = functools.partial(jnp.dot, preferred_element_type=F32)
-    return dot(high, matrix) + (dot(mid, matrix) + dot(low, matrix))
+    low = (values - high.astype(F32)).astype(BF16)
+    both = jnp.dot(jnp.concatenate([high, low], axis=0), matrix, preferred_element_type=F32)
+    rows = values.shape[0]
+    return both[:rows] + both[rows:]
 
 
 def pool_matrix(breadth, value):
@@ -128,7 +127,9 @@
     a_ref[row] = 1.0 + (g - 6.0 * k)
 
 
-def pack_kernel(u_hbm, k_hbm, g_hbm, even_ref, odd_ref, u_nat, k_nat, g_nat, k_wide, g_wide, sems):
+def pack_kernel(
+    u_hbm, k_hbm, g_hbm, odd_ref, even_ref, u_nat, k_nat, g_nat, k_wide, g_wide, state, after, coef_a, coef_b, coef_k, sems
+):
     height, breadth = u_hbm.shape[2:]
     copies = []
     for side, (low, low16) in enumerate(((0, 0), (height - 8, height - 16))):
@@ -138,31 +139,56 @@
     for copy in copies:
         copy.start()
     pool = pool_matrix(breadth, 1.0 / 16.0)
+    edges = masks()
+    zeros = jnp.zeros((8, breadth), F32)
+    state[0] = zeros
+    state[5] = zeros
+    after[0] = zeros
+    after[3] = zeros
     for copy in copies:
         copy.wait()
 
-    def fill(side, ref):
+    def rows_of(side):
         k_wide[side] = k_nat[side].astype(F32)
         g_wide[side] = g_nat[side].astype(F32)
+        low = 12 if side else 0
         u_rows = [u_nat[side, :, i, :] for i in range(8)]
-        low = 12 if side else 0
         k_rows = [k_wide[side, :, low + i, :] for i in range(4)]
         g_rows = [g_wide[side, :, low + i, :] for i in range(4)]
+        sums = [(r[0] + r[1]) + (r[2] + r[3]) for r in (u_rows[:4], u_rows[4:], k_rows, g_rows)]
+        return u_rows, k_rows, g_rows, sums
+
+    def both(first, second):
+        u_rows, k_rows, g_rows, odd_sums = rows_of(first)
+        near = 4 if first else 1
+        step = -1 if first else 1
         for i in range(4):
-            ref[i] = u_rows[(4 if side else 0) + i]
+            state[1 + i] = u_rows[(4 if first else 0) + i]
+            set_coefs(k_rows[i], g_rows[i], coef_a, coef_b, coef_k, 1 + i)
+        odd_ref[0] = state[near]
+        put_tiles(odd_ref, 1, fine_row(state, near, coef_a, coef_b, coef_k, near, breadth, edges))
+        one = fine_row(state, near + step, coef_a, coef_b, coef_k, near + step, breadth, edges)
+        two = fine_row(state, near + 2 * step, coef_a, coef_b, coef_k, near + 2 * step, breadth, edges)
+        put_tiles(odd_ref, 2, one)
+        place = 2 if first else 1
+        put_tiles(after, place, one)
+        put_tiles(after, place + step, two)
+        put_tiles(odd_ref, 3, fine_row(after, place, coef_a, coef_b, coef_k, near + step, breadth, edges))
+        odd_ref[4] = k_rows[near - 1]
+        odd_ref[5] = g_rows[near - 1]
+        odd_ref[6] = k_rows[near - 1 + step]
+        u_rows, k_rows, g_rows, even_sums = rows_of(second)
+        for i in range(4):
+            even_ref[i] = u_rows[(4 if second else 0) + i]
         for i in range(3):
-            ref[4 + i] = k_rows[(1 if side else 0) + i]
-            ref[7 + i] = g_rows[(1 if side else 0) + i]
-        return [(r[0] + r[1]) + (r[2] + r[3]) for r in (u_rows[:4], u_rows[4:], k_rows, g_rows)]
-
-    def both(first, second):
-        sums = fill(first, odd_ref) + fill(second, even_ref)
-        small = split_dot(jnp.concatenate(sums, axis=0), pool)
+            even_ref[4 + i] = k_rows[(1 if second else 0) + i]
+            even_ref[7 + i] = g_rows[(1 if second else 0) + i]
+        small = split_dot(jnp.concatenate(odd_sums + even_sums, axis=0), pool)
         for j, ref in enumerate((odd_ref, even_ref)):
             for i in range(4):
                 scale = 1.0 if i < 2 else 2.0 * DT
                 row = small[32 * j + 8 * i : 32 * j + 8 * i + 8]
-                ref[10, :, i * (breadth // 4) : (i + 1) * (breadth // 4)] = row * scale
+                ref[ref.shape[0] - 1, :, i * (breadth // 4) : (i + 1) * (breadth // 4)] = row * scale
 
     even_device = parity() == 0
 
@@ -177,9 +203,10 @@
 
 def pack(starts, diffusivity, reaction):
     breadth = starts.shape[3]
+    coef = pltpu.VMEM((6, 8, breadth), F32)
     return pl.pallas_call(
         pack_kernel,
-        out_shape=[struct(11, 8, breadth)] * 2,
+        out_shape=[struct(8, 8, breadth), struct(11, 8, breadth)],
         in_specs=[HBM] * 3,
         out_specs=[VMEM] * 2,
         scratch_shapes=[
@@ -188,9 +215,14 @@
             pltpu.VMEM((2, 8, 16, breadth), BF16),
             pltpu.VMEM((2, 8, 16, breadth), F32),
             pltpu.VMEM((2, 8, 16, breadth), F32),
+            coef,
+            pltpu.VMEM((4, 8, breadth), F32),
+            coef,
+            coef,
+            coef,
             pltpu.SemaphoreType.DMA((3, 2)),
         ],
-        compiler_params=params(16),
+        compiler_params=params(53),
         name="pack_rows",
     )(starts, diffusivity, reaction)
 
@@ -300,7 +332,7 @@
                         target[z + level, x, pl.ds(pl.multiple_of(row + shift, 8), 8), :] = out
             return carry
 
-        lax.fori_loop(0, 8, body, 0, unroll=2)
+        lax.fori_loop(0, 8, body, 0, unroll=4)
 
     def keep(step, source):
         def write(row):
@@ -333,25 +365,27 @@
 
     pool = pool_matrix(breadth, 1.0 / 16.0)
 
-    def sums_of(ref, level, start):
+    def sums_of(ref, level, start, part):
         def body(z, carry):
             for x, span in enumerate(spans):
                 parts = [ref[z + level, x, pl.ds(start + i, small, stride=4), :] for i in range(4)]
-                flat[z, :, span] = (parts[0] + parts[1]) + (parts[2] + parts[3])
+                flat[part, z, :, span] = (parts[0] + parts[1]) + (parts[2] + parts[3])
             return carry
 
-        lax.fori_loop(0, 8, body, 0)
-
-    def pooled_into(ref, level, start, target, scale):
-        sums_of(ref, level, start)
-        mean = split_dot(flat[...].reshape(8 * small, breadth), pool) * scale
-        flat[:, :, 0:thin] = mean.reshape(8, small, thin)
-        for r in range(small):
-            target[r] = flat[:, r, 0:thin]
-
-    pooled_into(one, 1, 8 + own, coarse_ref.at[0], 1.0)
-    pooled_into(coef_k, 0, own, coarse_ref.at[1], 2.0)
-    pooled_into(coef_b, 0, own, coarse_ref.at[2], 6.0)
+        lax.fori_loop(0, 8, body, 0, unroll=2)
+
+    def pooled_into(targets, scales):
+        count = len(targets)
+        means = split_dot(flat[0:count].reshape(count * 8 * small, breadth), pool).reshape(count, 8, small, thin)
+        for part in range(count):
+            flat[part, :, :, 0:thin] = means[part] * scales[part]
+            for r in range(small):
+                targets[part][r] = flat[part, :, r, 0:thin]
+
+    sums_of(one, 1, 8 + own, 0)
+    sums_of(coef_k, 0, own, 1)
+    sums_of(coef_b, 0, own, 2)
+    pooled_into([coarse_ref.at[0], coarse_ref.at[1], coarse_ref.at[2]], (1.0, 2.0, 6.0))
     keep(0, one)
     sweep(one, two, 1, None)
     keep(1, two)
@@ -360,7 +394,8 @@
     sweep(one, two, 1, None)
     keep(3, two)
     sweep(two, fine_ref, 0, jnp.where(above, 0, -8))
-    pooled_into(fine_ref, 0, 8, end_ref, 1.0)
+    sums_of(fine_ref, 0, 8, 0)
+    pooled_into([end_ref], (1.0,))
 
 
 def inner(starts, diffusivity, reaction, got):
@@ -384,7 +419,7 @@
         + [
             pltpu.VMEM((8, height, breadth), BF16),
             pltpu.VMEM((8, height, breadth), BF16),
-            pltpu.VMEM((8, small, breadth), F32),
+            pltpu.VMEM((3, 8, small, breadth), F32),
             pltpu.SemaphoreType.DMA((columns + 2,)),
         ],
         compiler_params=params(28),
@@ -420,31 +455,31 @@
     live = alive()
     edges = masks()
     states = (zero, one, two, three, rows_ref)
-    got_u = jnp.where(low_side, 0, 8)
-    got_c = jnp.where(low_side, 1, 8)
+
+    def index(distance):
+        return jnp.where(low_side, 4 + distance, 7 - distance)
+
     for i in range(4):
-        zero[got_u + i] = got_ref[i] * live
         coef_a[4 + i] = coefs_ref[0, i]
         coef_b[4 + i] = coefs_ref[1, i]
         coef_k[4 + i] = coefs_ref[2, i]
-    for i in range(3):
-        set_coefs(got_ref[4 + i], got_ref[7 + i], coef_a, coef_b, coef_k, got_c + i)
+    set_coefs(got_ref[4], got_ref[5], coef_a, coef_b, coef_k, index(-1))
+    zero[index(-1)] = got_ref[0] * live
+    one[index(-2)] = got_ref[2] * live
     for step in range(4):
         at = jnp.where(low_side, 4 + step, 6 - step)
         for i in range(2):
             states[step][at + i] = steps_ref[2 * step + i]
+    toward = jnp.where(low_side, -0.5 * VEL * DT, 0.5 * VEL * DT)
+    one[index(-1)] = (got_ref[1] + (DT * got_ref[4] + toward) * zero[index(0)]) * live
+    two[index(-2)] = (got_ref[3] + (DT * got_ref[6] + toward) * one[index(-1)]) * live
     for step in range(1, 5):
-        at = jnp.where(low_side, step, 8 - step)
-        for i in range(4):
-            tiles = fine_row(states[step - 1], at + i, coef_a, coef_b, coef_k, at + i, breadth, edges)
-            outside = jnp.logical_or(
-                jnp.logical_and(low_side, i < 4 - step), jnp.logical_and(jnp.logical_not(low_side), i >= step)
-            )
-            if step < 4:
-                factor = jnp.where(outside, live, 1.0)
-                put_tiles(states[step], at + i, [t * factor for t in tiles])
-            else:
-                put_tiles(rows_ref, i, tiles)
+        for distance in range(0 if step in (1, 4) else -1, step):
+            at = index(distance)
+            tiles = fine_row(states[step - 1], at, coef_a, coef_b, coef_k, at, breadth, edges)
+            if distance < 0:
+                tiles = [t * live for t in tiles]
+            put_tiles(states[step], at - 4 if step == 4 else at, tiles)
     pool = pool_matrix(breadth, 1.0 / 16.0)
     end_ref[...] = end_in[...]
     end_ref[jnp.where(low_side, 0, small - 1)] = pooled(rows_ref, 0, 1, pool)
@@ -460,11 +495,11 @@
         coarse_g[2 + r] = coarse_ref[2, r]
     for i in range(2):
         span = slice(i * thin, (i + 1) * thin)
-        seen[odd_at + i] = got_ref[10, :, span] * live
+        seen[odd_at + i] = got_ref[7, :, span] * live
         seen[even_at + i] = even_ref[10, :, span]
     for i, ref in ((2, coarse_k), (3, coarse_g)):
         span = slice(i * thin, (i + 1) * thin)
-        ref[near] = got_ref[10, :, span]
+        ref[near] = got_ref[7, :, span]
         ref[far] = even_ref[10, :, span]
     coarse_sweep(seen, half, coarse_k, coarse_g, 1, small + 3, 2, small, low_side, live, edges)
     first = lax.axis_index("tm") == 0
@@ -674,7 +709,7 @@
     low_side = parity() == 0
     high_side = jnp.logical_not(low_side)
 
-    even_rows, odd_rows = pack(starts, diffusivity, reaction)
+    odd_rows, even_rows = pack(starts, diffusivity, reaction)
     odd_got = lax.ppermute(odd_rows, "space", odd)
     even_got = lax.ppermute(even_rows, "space", even)
     fine, steps, coefs, coarse, end = inner(starts, diffusivity, reaction, even_got)

time: 35 us -> 30.4 us (0.87)
  local copies, waits for them, and re-layouts: 3.38 us -> 0.07 us
  Pallas kernels: 12 us -> 11.1 us
    unnamed x12 -> x6, local copies, waits for them, and re-layouts: 3.32 us -> 0.01 us
    pallas_call x1, Pallas kernels: 7.96 us -> 6.15 us  [inner(): pl.pallas_call(inner_kernel, out_shape=[struct(8, columns, height + 16, L...]
    pallas_call x1, Pallas kernels: 0.93 us -> 2.21 us  [pack(): pl.pallas_call(pack_kernel, out_shape=[struct(8, 8, breadth), struct(11,...]
  transfers between devices with their start and end apart: 9 -> 9, of which waited for: 3 -> 2; matrix products, arithmetic and copies ran while one was open for 0% -> 0% of each run, Pallas kernels for 23% -> 20%
where the time goes in v3:
time: 30.4 us; the launch traced here: 30.2 us
  starting transfers between devices  12.7 us (42%)
  Pallas kernels  11.1 us (37%)
  waiting for transfers between devices  6.24 us (21%)
    pallas_call x1, Pallas kernels, inner(): pl.pallas_call(inner_kernel, out_shape=[struct(8, columns, height + 16, L...  6.15 us
    ppermute x3, starting transfers between devices, per_device(): lax.ppermute(jump, 'tm', [(i, (i + k) % slices) for i in range(slices)])  5.75 us
    ppermute x1, starting transfers between devices, per_device(): odd_got = lax.ppermute(odd_rows, 'space', odd)  3.56 us
    ppermute x1, waiting for transfers between devices, per_device(): odd_j = lax.ppermute(outer(low_side), 'space', odd)  3.41 us
    ppermute x3, waiting for transfers between devices, per_device(): lax.ppermute(jump, 'tm', [(i, (i + k) % slices) for i in range(slices)])  2.81 us
    pallas_call x1, Pallas kernels, pack(): pl.pallas_call(pack_kernel, out_shape=[struct(8, 8, breadth), struct(11,...  2.21 us
    pallas_call x1, Pallas kernels, last(): pl.pallas_call(last_kernel, out_shape=struct(1, 8, height, breadth), in_s...  2.12 us
    ppermute x1, starting transfers between devices, per_device(): odd_j = lax.ppermute(outer(low_side), 'space', odd)  1.99 us
  transfers between devices with their start and end apart: 9, of which 2 were waited for; matrix products, arithmetic and copies ran while one was open for 0% of the time, Pallas kernels for 20%

profile of v3, /device:TPU:0, one launch (start us, length us, event | category | flops | bytes accessed | tf_op | source)
XLA Modules:
  0.0 30.2 jit_solution(17652795740723042772)
XLA Ops:
  0.0 0.0 copy-start.2
  0.0 0.0 copy-start.1
  0.0 0.0 copy-start
  0.0 2.2 %pack_rows.1 = (f32[8,8,1024]{2,1,0:T(8,128)S(1)}, f32[11,8,1024]{2,1,0:T(8,128)S(1)}) custom-call(f32[1,8,32,1024]{3,2,1,0:T(8,128)} %u_hbm.3, bf16[8,32,1024]{2,1,0:T(8,128)(2,1)} %k_hbm.3, bf16[8,32,1024]{2,1,0:T(8,128)(2,1)} %g_hbm.3), custom_call_target="tpu_custom_call" | custom-call | tf_op jit(solution)/shard_map/pack_rows/pallas_call | solution.py:207
  2.2 0.5 %collective-permute-start = (f32[11,8,1024]{2,1,0:T(8,128)S(1)}, f32[11,8,1024]{2,1,0:T(8,128)S(1)}, u32[]{:S(2)}, u32[]{:S(2)}) collective-permute-start(f32[11,8,1024]{2,1,0:T(8,128)S(1)} %get-tuple-element.17), channel_id=1, source_target_pairs={{0,1},{1,0},{2,3},{3,2},{4,5},{5,4},{6,7},{7,6},{8,9},{9,8},{10,11... | collective-permute-start | bytes 1081352 | tf_op jit(solution)/shard_map/ppermute | solution.py:714
  2.7 3.6 %collective-permute-start.1 = (f32[8,8,1024]{2,1,0:T(8,128)S(1)}, f32[8,8,1024]{2,1,0:T(8,128)S(1)}, u32[]{:S(2)}, u32[]{:S(2)}) collective-permute-start(f32[8,8,1024]{2,1,0:T(8,128)S(1)} %get-tuple-element.21), channel_id=1, source_target_pairs={{0,7},{1,2},{2,1},{3,4},{4,3},{5,6},{6,5},{7,0},{8,15},{9,10},{10,... | collective-permute-start | bytes 786440 | tf_op jit(solution)/shard_map/ppermute | solution.py:713
  6.3 0.0 collective-permute-done.got_ref.even_ref
  6.3 0.0 copy-done.2
  6.3 0.0 copy-done.1
  6.3 0.0 copy-done
  6.3 6.2 %inner_updates.1 = (f32[8,8,48,128]{3,2,1,0:T(8,128)S(1)}, f32[8,8,1024]{2,1,0:T(8,128)S(1)}, f32[3,4,8,1024]{3,2,1,0:T(8,128)S(1)}, f32[3,8,8,256]{3,2,1,0:T(8,128)S(1)}, f32[8,8,256]{2,1,0:T(8,128)S(1)}) custom-call(f32[1,8,32,1024]{3,2,1,0:T(8,128)S(1)} %copy-done, bf16[8,32,1024]{2,1,0:T(8,128)(2,1)S(1)} %copy-done.1, ...), custom_call_target="tpu_custom_call" | custom-call | flops 30000000 | bytes 4000000 | tf_op jit(solution)/shard_map/inner_updates/pallas_call | solution.py:407
  12.5 0.0 collective-permute-done.1.got_ref
  12.5 0.6 %edge_updates.1 = (f32[4,8,1024]{2,1,0:T(8,128)S(1)}, f32[8,8,256]{2,1,0:T(8,128)S(1)}, f32[8,8,256]{2,1,0:T(8,128)S(1)}) custom-call(f32[8,8,1024]{2,1,0:T(8,128)S(1)} %get-tuple-element.19.steps_ref, f32[3,4,8,1024]{3,2,1,0:T(8,128)S(1)} %get-tuple-element.20.coefs_ref, f32[8,8,1024]{2,1,0:T(8,128)S(1)} %collective-permute-done.1.got_ref, ...), custom_call_target="tpu_custom_call" | custom-call | tf_op jit(solution)/shard_map/edge_updates/pallas_call | solution.py:545
  13.1 1.8 %collective-permute-start.4 = (f32[8,8,256]{2,1,0:T(8,128)S(1)}, f32[8,8,256]{2,1,0:T(8,128)S(1)}, u32[]{:S(2)}, u32[]{:S(2)}) collective-permute-start(f32[8,8,256]{2,1,0:T(8,128)S(1)} %get-tuple-element.27.jump_ref), channel_id=1, source_target_pairs={{0,8},{8,16},{16,24},{24,0},{1,9},{9,17},{17,25},{25,1},{2,10},{10... | collective-permute-start | bytes 196616 | tf_op jit(solution)/shard_map/ppermute | solution.py:723
  14.9 2.6 %collective-permute-start.3 = (f32[8,8,256]{2,1,0:T(8,128)S(1)}, f32[8,8,256]{2,1,0:T(8,128)S(1)}, u32[]{:S(2)}, u32[]{:S(2)}) collective-permute-start(f32[8,8,256]{2,1,0:T(8,128)S(1)} %get-tuple-element.27.jump_ref), channel_id=1, source_target_pairs={{0,16},{8,24},{16,0},{24,8},{1,17},{9,25},{17,1},{25,9},{2,18},{10... | collective-permute-start | bytes 196616 | tf_op jit(solution)/shard_map/ppermute | solution.py:723
  17.5 1.3 %collective-permute-start.2 = (f32[8,8,256]{2,1,0:T(8,128)S(1)}, f32[8,8,256]{2,1,0:T(8,128)S(1)}, u32[]{:S(2)}, u32[]{:S(2)}) collective-permute-start(f32[8,8,256]{2,1,0:T(8,128)S(1)} %get-tuple-element.27.jump_ref), channel_id=1, source_target_pairs={{0,24},{8,0},{16,8},{24,16},{1,25},{9,1},{17,9},{25,17},{2,26},{10... | collective-permute-start | bytes 196616 | tf_op jit(solution)/shard_map/ppermute | solution.py:723
  18.9 0.8 %collective-permute-start.8 = (f32[2,6,8,256]{3,2,1,0:T(8,128)S(1)}, f32[2,6,8,256]{3,2,1,0:T(8,128)S(1)}, u32[]{:S(2)}, u32[]{:S(2)}) collective-permute-start(f32[2,6,8,256]{3,2,1,0:T(8,128)S(1)} %get-tuple-element.29), channel_id=1, source_target_pairs={{0,7},{1,2},{2,1},{3,4},{4,3},{5,6},{6,5},{7,0},{8,15},{9,10},{10,... | collective-permute-start | bytes 294920 | tf_op jit(solution)/shard_map/ppermute | solution.py:719
  19.7 0.0 collective-permute-start.7
  19.7 2.8 %collective-permute-done.2 = f32[8,8,256]{2,1,0:T(8,128)S(1)} collective-permute-done((f32[8,8,256]{2,1,0:T(8,128)S(1)}, f32[8,8,256]{2,1,0:T(8,128)S(1)}, u32[]{:S(2)}, u32[]{:S(2)}) %collective-permute-start.2) | collective-permute-done | bytes 65568 | tf_op jit(solution)/shard_map/ppermute | solution.py:723
  22.5 0.0 collective-permute-done.4
  22.5 0.0 collective-permute-done.3
  22.6 0.1 collective-permute-start.5
  22.7 2.0 %collective-permute-start.6 = (f32[12,8,256]{2,1,0:T(8,128)S(1)}, f32[12,8,256]{2,1,0:T(8,128)S(1)}, u32[]{:S(2)}, u32[]{:S(2)}) collective-permute-start(f32[12,8,256]{2,1,0:T(8,128)S(1)} %pad_maximum_fusion.2), channel_id=1, source_target_pairs={{0,7},{1,2},{2,1},{3,4},{4,3},{5,6},{6,5},{7,0},{8,15},{9,10},{10,... | collective-permute-start | bytes 294920 | tf_op jit(solution)/shard_map/ppermute | solution.py:733
  24.7 0.0 collective-permute-done.8.odd_c
  24.7 0.0 collective-permute-done.7.even_c
  24.7 0.0 collective-permute-done.5.even_j
  24.7 3.4 %collective-permute-done.6.odd_j = f32[12,8,256]{2,1,0:T(8,128)S(1)} collective-permute-done((f32[12,8,256]{2,1,0:T(8,128)S(1)}, f32[12,8,256]{2,1,0:T(8,128)S(1)}, u32[]{:S(2)}, u32[]{:S(2)}) %collective-permute-start.6) | collective-permute-done | bytes 98336 | tf_op jit(solution)/shard_map/ppermute | solution.py:733
  28.1 2.1 %chain_and_spread.1 = f32[1,8,32,1024]{3,2,1,0:T(8,128)} custom-call(f32[8,8,48,128]{3,2,1,0:T(8,128)S(1)} %get-tuple-element.18.fine_hbm, f32[4,8,1024]{2,1,0:T(8,128)S(1)} %get-tuple-element.24.rows_ref, f32[8,8,256]{2,1,0:T(8,128)S(1)} %get-tuple-element.25.end_ref, f32[8,8,256]{2,1,0:T(8,128)S(1)} %get-tuple-element.27.jump_ref, ...), custom_call_target="tpu_custom_call" | custom-call | tf_op jit(solution)/shard_map/chain_and_spread/pallas_call | solution.py:637
  (8 shorter events, 0.1 us)
Async XLA Ops:
  0.0 6.3 %copy-start.2 = (bf16[8,32,1024]{2,1,0:T(8,128)(2,1)S(1)}, bf16[8,32,1024]{2,1,0:T(8,128)(2,1)}, u32[]{:S(2)}) copy-start(bf16[8,32,1024]{2,1,0:T(8,128)(2,1)} %g_hbm.3) | copy-start | bytes 1572868
  0.0 6.3 %copy-start.1 = (bf16[8,32,1024]{2,1,0:T(8,128)(2,1)S(1)}, bf16[8,32,1024]{2,1,0:T(8,128)(2,1)}, u32[]{:S(2)}) copy-start(bf16[8,32,1024]{2,1,0:T(8,128)(2,1)} %k_hbm.3) | copy-start | bytes 1572868
  0.0 6.3 %copy-start = (f32[1,8,32,1024]{3,2,1,0:T(8,128)S(1)}, f32[1,8,32,1024]{3,2,1,0:T(8,128)}, u32[]{:S(2)}) copy-start(f32[1,8,32,1024]{3,2,1,0:T(8,128)} %u_hbm.3) | copy-start | bytes 3145732
  2.2 4.1 %collective-permute-start = (f32[11,8,1024]{2,1,0:T(8,128)S(1)}, f32[11,8,1024]{2,1,0:T(8,128)S(1)}, u32[]{:S(2)}, u32[]{:S(2)}) collective-permute-start(f32[11,8,1024]{2,1,0:T(8,128)S(1)} %get-tuple-element.17), channel_id=1, source_target_pairs={{0,1},{1,0},{2,3},{3,2},{4,5},{5,4},{6,7},{7,6},{8,9},{9,8},{10,11... | collective-permute-start | bytes 1081352 | tf_op jit(solution)/shard_map/ppermute | solution.py:714
  2.7 9.8 %collective-permute-start.1 = (f32[8,8,1024]{2,1,0:T(8,128)S(1)}, f32[8,8,1024]{2,1,0:T(8,128)S(1)}, u32[]{:S(2)}, u32[]{:S(2)}) collective-permute-start(f32[8,8,1024]{2,1,0:T(8,128)S(1)} %get-tuple-element.21), channel_id=1, source_target_pairs={{0,7},{1,2},{2,1},{3,4},{4,3},{5,6},{6,5},{7,0},{8,15},{9,10},{10,... | collective-permute-start | bytes 786440 | tf_op jit(solution)/shard_map/ppermute | solution.py:713
  13.1 9.4 %collective-permute-start.4 = (f32[8,8,256]{2,1,0:T(8,128)S(1)}, f32[8,8,256]{2,1,0:T(8,128)S(1)}, u32[]{:S(2)}, u32[]{:S(2)}) collective-permute-start(f32[8,8,256]{2,1,0:T(8,128)S(1)} %get-tuple-element.27.jump_ref), channel_id=1, source_target_pairs={{0,8},{8,16},{16,24},{24,0},{1,9},{9,17},{17,25},{25,1},{2,10},{10... | collective-permute-start | bytes 196616 | tf_op jit(solution)/shard_map/ppermute | solution.py:723
  14.9 7.6 %collective-permute-start.3 = (f32[8,8,256]{2,1,0:T(8,128)S(1)}, f32[8,8,256]{2,1,0:T(8,128)S(1)}, u32[]{:S(2)}, u32[]{:S(2)}) collective-permute-start(f32[8,8,256]{2,1,0:T(8,128)S(1)} %get-tuple-element.27.jump_ref), channel_id=1, source_target_pairs={{0,16},{8,24},{16,0},{24,8},{1,17},{9,25},{17,1},{25,9},{2,18},{10... | collective-permute-start | bytes 196616 | tf_op jit(solution)/shard_map/ppermute | solution.py:723
  17.5 4.9 %collective-permute-start.2 = (f32[8,8,256]{2,1,0:T(8,128)S(1)}, f32[8,8,256]{2,1,0:T(8,128)S(1)}, u32[]{:S(2)}, u32[]{:S(2)}) collective-permute-start(f32[8,8,256]{2,1,0:T(8,128)S(1)} %get-tuple-element.27.jump_ref), channel_id=1, source_target_pairs={{0,24},{8,0},{16,8},{24,16},{1,25},{9,1},{17,9},{25,17},{2,26},{10... | collective-permute-start | bytes 196616 | tf_op jit(solution)/shard_map/ppermute | solution.py:723
  18.9 5.8 %collective-permute-start.8 = (f32[2,6,8,256]{3,2,1,0:T(8,128)S(1)}, f32[2,6,8,256]{3,2,1,0:T(8,128)S(1)}, u32[]{:S(2)}, u32[]{:S(2)}) collective-permute-start(f32[2,6,8,256]{3,2,1,0:T(8,128)S(1)} %get-tuple-element.29), channel_id=1, source_target_pairs={{0,7},{1,2},{2,1},{3,4},{4,3},{5,6},{6,5},{7,0},{8,15},{9,10},{10,... | collective-permute-start | bytes 294920 | tf_op jit(solution)/shard_map/ppermute | solution.py:719
  19.7 5.0 %collective-permute-start.7 = (f32[2,6,8,256]{3,2,1,0:T(8,128)S(1)}, f32[2,6,8,256]{3,2,1,0:T(8,128)S(1)}, u32[]{:S(2)}, u32[]{:S(2)}) collective-permute-start(f32[2,6,8,256]{3,2,1,0:T(8,128)S(1)} %get-tuple-element.30), channel_id=1, source_target_pairs={{0,1},{1,0},{2,3},{3,2},{4,5},{5,4},{6,7},{7,6},{8,9},{9,8},{10,11... | collective-permute-start | bytes 294920 | tf_op jit(solution)/shard_map/ppermute | solution.py:720
  22.6 2.1 %collective-permute-start.5 = (f32[12,8,256]{2,1,0:T(8,128)S(1)}, f32[12,8,256]{2,1,0:T(8,128)S(1)}, u32[]{:S(2)}, u32[]{:S(2)}) collective-permute-start(f32[12,8,256]{2,1,0:T(8,128)S(1)} %pad_maximum_fusion.1), channel_id=1, source_target_pairs={{0,1},{1,0},{2,3},{3,2},{4,5},{5,4},{6,7},{7,6},{8,9},{9,8},{10,11... | collective-permute-start | bytes 294920 | tf_op jit(solution)/shard_map/ppermute | solution.py:734
  22.7 5.5 %collective-permute-start.6 = (f32[12,8,256]{2,1,0:T(8,128)S(1)}, f32[12,8,256]{2,1,0:T(8,128)S(1)}, u32[]{:S(2)}, u32[]{:S(2)}) collective-permute-start(f32[12,8,256]{2,1,0:T(8,128)S(1)} %pad_maximum_fusion.2), channel_id=1, source_target_pairs={{0,7},{1,2},{2,1},{3,4},{4,3},{5,6},{6,5},{7,0},{8,15},{9,10},{10,... | collective-permute-start | bytes 294920 | tf_op jit(solution)/shard_map/ppermute | solution.py:733

commit v4 on v3

--- a/solution.py
+++ b/solution.py
@@ -14,6 +14,7 @@
 LANES = 128
 F32 = jnp.float32
 BF16 = jnp.bfloat16
+ODD_MIB = 53.4
 
 VMEM = pl.BlockSpec(memory_space=pltpu.VMEM)
 ANY = pl.BlockSpec(memory_space=pl.ANY)
@@ -21,7 +22,7 @@
 
 
 def params(mib):
-    return pltpu.CompilerParams(vmem_limit_bytes=mib * 2**20)
+    return pltpu.CompilerParams(vmem_limit_bytes=int(mib * 2**20))
 
 
 def struct(*shape):
@@ -127,15 +128,30 @@
     a_ref[row] = 1.0 + (g - 6.0 * k)
 
 
-def pack_kernel(
-    u_hbm, k_hbm, g_hbm, odd_ref, even_ref, u_nat, k_nat, g_nat, k_wide, g_wide, state, after, coef_a, coef_b, coef_k, sems
+def put_pooled(ref, sums, pool):
+    thin = ref.shape[2] // 4
+    small = split_dot(jnp.concatenate(sums, axis=0), pool)
+    for i in range(4):
+        row = small[8 * i : 8 * i + 8] * (1.0 if i < 2 else 2.0 * DT)
+        ref[ref.shape[0] - 1, :, i * thin : (i + 1) * thin] = row
+
+
+def sums_of_four(*arrays):
+    return [(r[0] + r[1]) + (r[2] + r[3]) for r in arrays]
+
+
+def odd_kernel(
+    u_hbm, k_hbm, g_hbm, odd_ref, u_nat, k_nat, g_nat, k_wide, g_wide, state, after, coef_a, coef_b, coef_k, sems
 ):
     height, breadth = u_hbm.shape[2:]
-    copies = []
-    for side, (low, low16) in enumerate(((0, 0), (height - 8, height - 16))):
-        copies.append(pltpu.make_async_copy(u_hbm.at[0, :, pl.ds(low, 8), :], u_nat.at[side], sems.at[0, side]))
-        copies.append(pltpu.make_async_copy(k_hbm.at[:, pl.ds(low16, 16), :], k_nat.at[side], sems.at[1, side]))
-        copies.append(pltpu.make_async_copy(g_hbm.at[:, pl.ds(low16, 16), :], g_nat.at[side], sems.at[2, side]))
+    low_side = parity() == 0
+    row8 = pl.multiple_of(jnp.where(low_side, 0, height - 8), 8)
+    row16 = pl.multiple_of(jnp.where(low_side, 0, height - 16), 16)
+    copies = [
+        pltpu.make_async_copy(u_hbm.at[0, :, pl.ds(row8, 8), :], u_nat, sems.at[0]),
+        pltpu.make_async_copy(k_hbm.at[:, pl.ds(row16, 16), :], k_nat, sems.at[1]),
+        pltpu.make_async_copy(g_hbm.at[:, pl.ds(row16, 16), :], g_nat, sems.at[2]),
+    ]
     for copy in copies:
         copy.start()
     pool = pool_matrix(breadth, 1.0 / 16.0)
@@ -147,84 +163,109 @@
     after[3] = zeros
     for copy in copies:
         copy.wait()
-
-    def rows_of(side):
-        k_wide[side] = k_nat[side].astype(F32)
-        g_wide[side] = g_nat[side].astype(F32)
-        low = 12 if side else 0
-        u_rows = [u_nat[side, :, i, :] for i in range(8)]
-        k_rows = [k_wide[side, :, low + i, :] for i in range(4)]
-        g_rows = [g_wide[side, :, low + i, :] for i in range(4)]
-        sums = [(r[0] + r[1]) + (r[2] + r[3]) for r in (u_rows[:4], u_rows[4:], k_rows, g_rows)]
-        return u_rows, k_rows, g_rows, sums
-
-    def both(first, second):
-        u_rows, k_rows, g_rows, odd_sums = rows_of(first)
-        near = 4 if first else 1
-        step = -1 if first else 1
+    k_wide[...] = k_nat[...].astype(F32)
+    g_wide[...] = g_nat[...].astype(F32)
+
+    def fill(high):
+        low = 12 if high else 0
+        u_rows = [u_nat[:, i, :] for i in range(8)]
+        k_rows = [k_wide[:, low + i, :] for i in range(4)]
+        g_rows = [g_wide[:, low + i, :] for i in range(4)]
+        near = 4 if high else 1
+        step = -1 if high else 1
         for i in range(4):
-            state[1 + i] = u_rows[(4 if first else 0) + i]
+            state[1 + i] = u_rows[(4 if high else 0) + i]
             set_coefs(k_rows[i], g_rows[i], coef_a, coef_b, coef_k, 1 + i)
         odd_ref[0] = state[near]
         put_tiles(odd_ref, 1, fine_row(state, near, coef_a, coef_b, coef_k, near, breadth, edges))
         one = fine_row(state, near + step, coef_a, coef_b, coef_k, near + step, breadth, edges)
         two = fine_row(state, near + 2 * step, coef_a, coef_b, coef_k, near + 2 * step, breadth, edges)
         put_tiles(odd_ref, 2, one)
-        place = 2 if first else 1
+        place = 2 if high else 1
         put_tiles(after, place, one)
         put_tiles(after, place + step, two)
         put_tiles(odd_ref, 3, fine_row(after, place, coef_a, coef_b, coef_k, near + step, breadth, edges))
         odd_ref[4] = k_rows[near - 1]
         odd_ref[5] = g_rows[near - 1]
         odd_ref[6] = k_rows[near - 1 + step]
-        u_rows, k_rows, g_rows, even_sums = rows_of(second)
-        for i in range(4):
-            even_ref[i] = u_rows[(4 if second else 0) + i]
-        for i in range(3):
-            even_ref[4 + i] = k_rows[(1 if second else 0) + i]
-            even_ref[7 + i] = g_rows[(1 if second else 0) + i]
-        small = split_dot(jnp.concatenate(odd_sums + even_sums, axis=0), pool)
-        for j, ref in enumerate((odd_ref, even_ref)):
-            for i in range(4):
-                scale = 1.0 if i < 2 else 2.0 * DT
-                row = small[32 * j + 8 * i : 32 * j + 8 * i + 8]
-                ref[ref.shape[0] - 1, :, i * (breadth // 4) : (i + 1) * (breadth // 4)] = row * scale
-
-    even_device = parity() == 0
-
-    @pl.when(even_device)
-    def _():
-        both(0, 1)
-
-    @pl.when(jnp.logical_not(even_device))
-    def _():
-        both(1, 0)
-
-
-def pack(starts, diffusivity, reaction):
+        put_pooled(odd_ref, sums_of_four(u_rows[:4], u_rows[4:], k_rows, g_rows), pool)
+
+    @pl.when(low_side)
+    def _():
+        fill(0)
+
+    @pl.when(jnp.logical_not(low_side))
+    def _():
+        fill(1)
+
+
+def odd_pack(starts, diffusivity, reaction):
     breadth = starts.shape[3]
     coef = pltpu.VMEM((6, 8, breadth), F32)
     return pl.pallas_call(
-        pack_kernel,
-        out_shape=[struct(8, 8, breadth), struct(11, 8, breadth)],
+        odd_kernel,
+        out_shape=struct(8, 8, breadth),
         in_specs=[HBM] * 3,
-        out_specs=[VMEM] * 2,
+        out_specs=VMEM,
         scratch_shapes=[
-            pltpu.VMEM((2, 8, 8, breadth), F32),
-            pltpu.VMEM((2, 8, 16, breadth), BF16),
-            pltpu.VMEM((2, 8, 16, breadth), BF16),
-            pltpu.VMEM((2, 8, 16, breadth), F32),
-            pltpu.VMEM((2, 8, 16, breadth), F32),
+            pltpu.VMEM((8, 8, breadth), F32),
+            pltpu.VMEM((8, 16, breadth), BF16),
+            pltpu.VMEM((8, 16, breadth), BF16),
+            pltpu.VMEM((8, 16, breadth), F32),
+            pltpu.VMEM((8, 16, breadth), F32),
             coef,
             pltpu.VMEM((4, 8, breadth), F32),
             coef,
             coef,
             coef,
-            pltpu.SemaphoreType.DMA((3, 2)),
+            pltpu.SemaphoreType.DMA((3,)),
         ],
-        compiler_params=params(53),
-        name="pack_rows",
+        compiler_params=params(ODD_MIB),
+        name="odd_rows",
     )(starts, diffusivity, reaction)
+
+
+def even_kernel(odd_rows, u_ref, k_ref, g_ref, even_ref, k_wide, g_wide):
+    del odd_rows
+    height, breadth = u_ref.shape[2:]
+    pool = pool_matrix(breadth, 1.0 / 16.0)
+
+    def fill(high):
+        k_wide[...] = k_ref[:, height - 16 if high else 0 : height if high else 16, :].astype(F32)
+        g_wide[...] = g_ref[:, height - 16 if high else 0 : height if high else 16, :].astype(F32)
+        low = 12 if high else 0
+        u_rows = [u_ref[0, :, (height - 8 if high else 0) + i, :] for i in range(8)]
+        k_rows = [k_wide[:, low + i, :] for i in range(4)]
+        g_rows = [g_wide[:, low + i, :] for i in range(4)]
+        for i in range(4):
+            even_ref[i] = u_rows[(4 if high else 0) + i]
+        for i in range(3):
+            even_ref[4 + i] = k_rows[(1 if high else 0) + i]
+            even_ref[7 + i] = g_rows[(1 if high else 0) + i]
+        put_pooled(even_ref, sums_of_four(u_rows[:4], u_rows[4:], k_rows, g_rows), pool)
+
+    above = parity() == 0
+
+    @pl.when(above)
+    def _():
+        fill(1)
+
+    @pl.when(jnp.logical_not(above))
+    def _():
+        fill(0)
+
+
+def even_pack(odd_rows, starts, diffusivity, reaction):
+    breadth = starts.shape[3]
+    return pl.pallas_call(
+        even_kernel,
+        out_shape=struct(11, 8, breadth),
+        in_specs=[ANY] + [VMEM] * 3,
+        out_specs=VMEM,
+        scratch_shapes=[pltpu.VMEM((8, 16, breadth), F32)] * 2,
+        compiler_params=params(16),
+        name="even_rows",
+    )(odd_rows, starts, diffusivity, reaction)
 
 
 def inner_kernel(
@@ -332,7 +373,7 @@
                         target[z + level, x, pl.ds(pl.multiple_of(row + shift, 8), 8), :] = out
             return carry
 
-        lax.fori_loop(0, 8, body, 0, unroll=4)
+        lax.fori_loop(0, 8, body, 0, unroll=8)
 
     def keep(step, source):
         def write(row):
@@ -433,10 +474,25 @@
     return lax.dynamic_slice_in_dim(array, start, reach, axis=1)
 
 
-def exchanges(count):
-    even = [(i, i ^ 1) for i in range(count)]
-    odd = [(i, (i - 1 if i % 2 == 0 else i + 1) % count) for i in range(count)]
-    return even, odd
+def even_pairs():
+    return [(i, i ^ 1) for i in range(lax.axis_size("space"))]
+
+
+def swap_odd(block):
+    places = lax.axis_size("space")
+    slices = lax.axis_size("tm")
+
+    def partner(time, place):
+        if 0 < place < places - 1 or slices % 2:
+            return time, (place - 1 if place % 2 == 0 else place + 1) % places
+        return time ^ 1, place
+
+    pairs = []
+    for time in range(slices):
+        for place in range(places):
+            other, near = partner(time, place)
+            pairs.append((time * places + place, other * places + near))
+    return lax.ppermute(block, ("tm", "space"), pairs)
 
 
 def alive():
@@ -557,11 +613,10 @@
     )(steps, coefs, got, even_got, end, coarse)
 
 
-def last_kernel(
-    fine_hbm, rows_ref, end_ref, jump_ref, before_ref, even_j, odd_j, coarse_ref, even_c, odd_c, out_hbm,
-    fine_ref, out_ref, one, two, coarse_k, coarse_g, added, change, moved, sems,
-):
-    behind = before_ref.shape[0]
+def last_kernel(behind, *refs):
+    before, refs = refs[:behind], refs[behind:]
+    fine_hbm, rows_ref, end_ref, jump_ref, even_j, odd_j, coarse_ref, even_c, odd_c, out_hbm = refs[:10]
+    fine_ref, out_ref, one, two, coarse_k, coarse_g, added, change, moved, sems = refs[10:]
     reach = COARSE * behind
     height, breadth = out_hbm.shape[2:]
     columns = breadth // LANES
@@ -581,7 +636,7 @@
         target = one if j == 0 else added
         base = reach - width
         for r in range(small):
-            target[reach + r] = before_ref[j, r] * ok
+            target[reach + r] = before[j][r] * ok
         odd_at = jnp.where(low_side, base, reach + small)
         even_at = jnp.where(low_side, reach + small, base)
         for i in range(width):
@@ -632,12 +687,12 @@
 def last(fine, rows, end, jump, before, even_j, odd_j, coarse, even_c, odd_c, height):
     breadth = rows.shape[2]
     small = height // 4
-    reach = COARSE * before.shape[0]
+    reach = COARSE * len(before)
     thin = pltpu.VMEM((small + 2 * reach, 8, breadth // 4), F32)
     return pl.pallas_call(
-        last_kernel,
+        functools.partial(last_kernel, len(before)),
         out_shape=struct(1, 8, height, breadth),
-        in_specs=[ANY] + [VMEM] * 9,
+        in_specs=[VMEM] * len(before) + [ANY] + [VMEM] * 8,
         out_specs=HBM,
         scratch_shapes=[pltpu.VMEM(fine.shape, F32), pltpu.VMEM((8, height, breadth), F32)]
         + [thin] * 5
@@ -648,10 +703,10 @@
         ],
         compiler_params=params(16),
         name="chain_and_spread",
-    )(fine, rows, end, jump, before, even_j, odd_j, coarse, even_c, odd_c)
-
-
-def relay(jump, coarse, even_c, odd_c, even, odd):
+    )(*before, fine, rows, end, jump, even_j, odd_j, coarse, even_c, odd_c)
+
+
+def relay(jump, coarse, even_c, odd_c, even):
     low_side = parity() == 0
     live = alive()
     small = jump.shape[0]
@@ -682,7 +737,7 @@
     def advance(values):
         block = values[None]
         even_v = lax.ppermute(rows_for(block, jnp.logical_not(low_side), 2), "space", even)
-        odd_v = lax.ppermute(rows_for(block, low_side, 2), "space", odd)
+        odd_v = swap_odd(rows_for(block, low_side, 2))
         wide = widened(block, even_v, odd_v)[0]
         wide = jnp.where(inside, update(wide, coefs[0, 1:-1], coefs[1, 1:-1]), 0.0)
         return update(wide, coarse[1], coarse[2])
@@ -705,35 +760,34 @@
     behind = slices - 1
     reach = COARSE * behind
     at_once = 0 < behind and reach <= small
-    even, odd = exchanges(lax.axis_size("space"))
+    even = even_pairs()
     low_side = parity() == 0
     high_side = jnp.logical_not(low_side)
 
-    odd_rows, even_rows = pack(starts, diffusivity, reaction)
-    odd_got = lax.ppermute(odd_rows, "space", odd)
-    even_got = lax.ppermute(even_rows, "space", even)
+    odd_rows = odd_pack(starts, diffusivity, reaction)
+    odd_got = swap_odd(odd_rows)
+    even_got = lax.ppermute(even_pack(odd_rows, starts, diffusivity, reaction), "space", even)
     fine, steps, coefs, coarse, end = inner(starts, diffusivity, reaction, even_got)
     rows, end, jump = edge(steps, coefs, odd_got, even_got, end, coarse)
     width = reach if at_once else COARSE
     later, jump = lax.optimization_barrier((coarse[1:], jump))
-    odd_c = lax.ppermute(rows_for(later, low_side, width), "space", odd)
+    odd_c = swap_odd(rows_for(later, low_side, width))
     even_c = lax.ppermute(rows_for(later, high_side, width), "space", even)
     if at_once:
         before = [
             lax.ppermute(jump, "tm", [(i, (i + k) % slices) for i in range(slices)])
             for k in range(behind, 0, -1)
         ]
-        before = jnp.stack(before)
 
         def outer(low):
             return jnp.concatenate(
                 [rows_for(before[j][None], low, reach - COARSE * j)[0] for j in range(behind)], axis=0
             )
 
-        odd_j = lax.ppermute(outer(low_side), "space", odd)
+        odd_j = swap_odd(outer(low_side))
         even_j = lax.ppermute(outer(high_side), "space", even)
         return last(fine, rows, end, jump, before, even_j, odd_j, coarse, even_c, odd_c, height)
-    chained = relay(jump, coarse, even_c, odd_c, even, odd)
+    chained = relay(jump, coarse, even_c, odd_c, even)
     change = jnp.repeat(jnp.repeat(jnp.transpose(chained - end, (1, 0, 2)), 4, axis=1), 4, axis=2)
     fixed = jnp.where(low_side, 0, height - 4)
     fine = jnp.transpose(fine[:, :, 8 : 8 + height], (0, 2, 1, 3)).reshape(8, height, breadth)

time: 30.4 us -> 29.2 us (0.961)
  waiting for transfers between devices: 6.24 us -> 5.65 us
  starting transfers between devices: 12.7 us -> 12.3 us
    ppermute x4, starting transfers between devices: 6.83 us -> 5.67 us  [the longest x3 5.15 us: swap_odd(): return lax.ppermute(block, ('tm', 'space'), pairs)]
    ppermute x1, starting transfers between devices: 0.01 us -> 0.94 us  [per_device(): even_c = lax.ppermute(rows_for(later, high_side, width), 'space', even)]
    ppermute x4, waiting for transfers between devices: 3.42 us -> 2.9 us  [the longest x3 2.9 us: swap_odd(): return lax.ppermute(block, ('tm', 'space'), pairs)]
    pallas_call x1, Pallas kernels: 6.15 us -> 5.84 us  [inner(): pl.pallas_call(inner_kernel, out_shape=[struct(8, columns, height + 16, L...]
    pallas_call x2 -> x3, Pallas kernels: 4.33 us -> 4.36 us  [the longest x1 2.12 us: last(): pl.pallas_call(functools.partial(last_kernel, len(before)), out_shape=str...]
where the time goes in v4:
time: 29.2 us; the launch traced here: 29 us
  starting transfers between devices  12.3 us (42%)
  Pallas kernels  10.8 us (37%)
  waiting for transfers between devices  5.65 us (19%)
    pallas_call x1, Pallas kernels, inner(): pl.pallas_call(inner_kernel, out_shape=[struct(8, columns, height + 16, L...  5.84 us
    ppermute x3, starting transfers between devices, per_device(): lax.ppermute(jump, 'tm', [(i, (i + k) % slices) for i in range(slices)])  5.59 us
    ppermute x3, starting transfers between devices, swap_odd(): return lax.ppermute(block, ('tm', 'space'), pairs)  5.15 us
    ppermute x3, waiting for transfers between devices, swap_odd(): return lax.ppermute(block, ('tm', 'space'), pairs)  2.9 us
    ppermute x3, waiting for transfers between devices, per_device(): lax.ppermute(jump, 'tm', [(i, (i + k) % slices) for i in range(slices)])  2.75 us
    pallas_call x1, Pallas kernels, last(): pl.pallas_call(functools.partial(last_kernel, len(before)), out_shape=str...  2.12 us
    pallas_call x1, Pallas kernels, odd_pack(): pl.pallas_call(odd_kernel, out_shape=struct(8, 8, breadth), in_specs=[HBM...  1.77 us
    ppermute x1, starting transfers between devices, per_device(): even_c = lax.ppermute(rows_for(later, high_side, width), 'space', even)  0.94 us
  transfers between devices with their start and end apart: 9, of which 2 were waited for; matrix products, arithmetic and copies ran while one was open for 0% of the time, Pallas kernels for 20%

profile of v4, /device:TPU:0, one launch (start us, length us, event | category | flops | bytes accessed | tf_op | source)
XLA Modules:
  0.0 29.0 jit_solution(2562122312359571725)
XLA Ops:
  0.0 0.0 copy-start.2
  0.0 0.0 copy-start.1
  0.0 0.0 copy-start
  0.0 1.8 %odd_rows.1 = f32[8,8,1024]{2,1,0:T(8,128)S(1)} custom-call(f32[1,8,32,1024]{3,2,1,0:T(8,128)} %u_hbm.3, bf16[8,32,1024]{2,1,0:T(8,128)(2,1)} %k_hbm.3, bf16[8,32,1024]{2,1,0:T(8,128)(2,1)} %g_hbm.3), custom_call_target="tpu_custom_call" | custom-call | tf_op jit(solution)/shard_map/odd_rows/pallas_call | solution.py:205
  1.8 0.0 copy-done.2
  1.8 0.0 copy-done.1
  1.8 0.0 copy-done
  1.8 0.5 %even_rows.1 = f32[11,8,1024]{2,1,0:T(8,128)S(1)} custom-call(f32[8,8,1024]{2,1,0:T(8,128)S(1)} %odd_rows.1, f32[1,8,32,1024]{3,2,1,0:T(8,128)S(1)} %copy-done, bf16[8,32,1024]{2,1,0:T(8,128)(2,1)S(1)} %copy-done.1, bf16[8,32,1024]{2,1,0:T(8,128)(2,1)S(1)} %copy-done.2), custom_call_target="tpu_custom_call" | custom-call | tf_op jit(solution)/shard_map/even_rows/pallas_call | solution.py:260
  2.3 0.5 %collective-permute-start = (f32[11,8,1024]{2,1,0:T(8,128)S(1)}, f32[11,8,1024]{2,1,0:T(8,128)S(1)}, u32[]{:S(2)}, u32[]{:S(2)}) collective-permute-start(f32[11,8,1024]{2,1,0:T(8,128)S(1)} %even_rows.1), channel_id=1, source_target_pairs={{0,1},{1,0},{2,3},{3,2},{4,5},{5,4},{6,7},{7,6},{8,9},{9,8},{10,11... | collective-permute-start | bytes 1081352 | tf_op jit(solution)/shard_map/ppermute | solution.py:769
  2.8 2.6 %collective-permute-start.1 = (f32[8,8,1024]{2,1,0:T(8,128)S(1)}, f32[8,8,1024]{2,1,0:T(8,128)S(1)}, u32[]{:S(2)}, u32[]{:S(2)}) collective-permute-start(f32[8,8,1024]{2,1,0:T(8,128)S(1)} %odd_rows.1), channel_id=1, source_target_pairs={{0,8},{1,2},{2,1},{3,4},{4,3},{5,6},{6,5},{7,15},{8,0},{9,10},{10,... | collective-permute-start | bytes 786440 | tf_op jit(solution)/shard_map/ppermute | solution.py:495
  5.5 0.0 collective-permute-done.got_ref.even_ref
  5.5 5.8 %inner_updates.1 = (f32[8,8,48,128]{3,2,1,0:T(8,128)S(1)}, f32[8,8,1024]{2,1,0:T(8,128)S(1)}, f32[3,4,8,1024]{3,2,1,0:T(8,128)S(1)}, f32[3,8,8,256]{3,2,1,0:T(8,128)S(1)}, f32[8,8,256]{2,1,0:T(8,128)S(1)}) custom-call(f32[1,8,32,1024]{3,2,1,0:T(8,128)S(1)} %copy-done, bf16[8,32,1024]{2,1,0:T(8,128)(2,1)S(1)} %copy-done.1, ...), custom_call_target="tpu_custom_call" | custom-call | flops 30000000 | bytes 4000000 | tf_op jit(solution)/shard_map/inner_updates/pallas_call | solution.py:448
  11.3 0.0 collective-permute-done.1.got_ref
  11.3 0.6 %edge_updates.1 = (f32[4,8,1024]{2,1,0:T(8,128)S(1)}, f32[8,8,256]{2,1,0:T(8,128)S(1)}, f32[8,8,256]{2,1,0:T(8,128)S(1)}) custom-call(f32[8,8,1024]{2,1,0:T(8,128)S(1)} %get-tuple-element.16.steps_ref, f32[3,4,8,1024]{3,2,1,0:T(8,128)S(1)} %get-tuple-element.17.coefs_ref, f32[8,8,1024]{2,1,0:T(8,128)S(1)} %collective-permute-done.1.got_ref, ...), custom_call_target="tpu_custom_call" | custom-call | tf_op jit(solution)/shard_map/edge_updates/pallas_call | solution.py:601
  12.0 1.6 %collective-permute-start.4 = (f32[8,8,256]{2,1,0:T(8,128)S(1)}, f32[8,8,256]{2,1,0:T(8,128)S(1)}, u32[]{:S(2)}, u32[]{:S(2)}) collective-permute-start(f32[8,8,256]{2,1,0:T(8,128)S(1)} %get-tuple-element.20.refs_6_), channel_id=1, source_target_pairs={{0,8},{8,16},{16,24},{24,0},{1,9},{9,17},{17,25},{25,1},{2,10},{10... | collective-permute-start | bytes 196616 | tf_op jit(solution)/shard_map/ppermute | solution.py:778
  13.6 2.6 %collective-permute-start.3 = (f32[8,8,256]{2,1,0:T(8,128)S(1)}, f32[8,8,256]{2,1,0:T(8,128)S(1)}, u32[]{:S(2)}, u32[]{:S(2)}) collective-permute-start(f32[8,8,256]{2,1,0:T(8,128)S(1)} %get-tuple-element.20.refs_6_), channel_id=1, source_target_pairs={{0,16},{8,24},{16,0},{24,8},{1,17},{9,25},{17,1},{25,9},{2,18},{10... | collective-permute-start | bytes 196616 | tf_op jit(solution)/shard_map/ppermute | solution.py:778
  16.2 1.4 %collective-permute-start.2 = (f32[8,8,256]{2,1,0:T(8,128)S(1)}, f32[8,8,256]{2,1,0:T(8,128)S(1)}, u32[]{:S(2)}, u32[]{:S(2)}) collective-permute-start(f32[8,8,256]{2,1,0:T(8,128)S(1)} %get-tuple-element.20.refs_6_), channel_id=1, source_target_pairs={{0,24},{8,0},{16,8},{24,16},{1,25},{9,1},{17,9},{25,17},{2,26},{10... | collective-permute-start | bytes 196616 | tf_op jit(solution)/shard_map/ppermute | solution.py:778
  17.6 0.7 %collective-permute-start.8 = (f32[2,6,8,256]{3,2,1,0:T(8,128)S(1)}, f32[2,6,8,256]{3,2,1,0:T(8,128)S(1)}, u32[]{:S(2)}, u32[]{:S(2)}) collective-permute-start(f32[2,6,8,256]{3,2,1,0:T(8,128)S(1)} %get-tuple-element.25), channel_id=1, source_target_pairs={{0,8},{1,2},{2,1},{3,4},{4,3},{5,6},{6,5},{7,15},{8,0},{9,10},{10,... | collective-permute-start | bytes 294920 | tf_op jit(solution)/shard_map/ppermute | solution.py:495
  18.3 0.9 %collective-permute-start.7 = (f32[2,6,8,256]{3,2,1,0:T(8,128)S(1)}, f32[2,6,8,256]{3,2,1,0:T(8,128)S(1)}, u32[]{:S(2)}, u32[]{:S(2)}) collective-permute-start(f32[2,6,8,256]{3,2,1,0:T(8,128)S(1)} %get-tuple-element.26), channel_id=1, source_target_pairs={{0,1},{1,0},{2,3},{3,2},{4,5},{5,4},{6,7},{7,6},{8,9},{9,8},{10,11... | collective-permute-start | bytes 294920 | tf_op jit(solution)/shard_map/ppermute | solution.py:775
  19.2 2.7 %collective-permute-done.2.refs_0_ = f32[8,8,256]{2,1,0:T(8,128)S(1)} collective-permute-done((f32[8,8,256]{2,1,0:T(8,128)S(1)}, f32[8,8,256]{2,1,0:T(8,128)S(1)}, u32[]{:S(2)}, u32[]{:S(2)}) %collective-permute-start.2) | collective-permute-done | bytes 65568 | tf_op jit(solution)/shard_map/ppermute | solution.py:778
  22.0 0.0 collective-permute-done.4.refs_2_
  22.0 0.0 collective-permute-done.3.refs_1_
  22.1 0.1 collective-permute-start.5
  22.2 1.8 %collective-permute-start.6 = (f32[12,8,256]{2,1,0:T(8,128)S(1)}, f32[12,8,256]{2,1,0:T(8,128)S(1)}, u32[]{:S(2)}, u32[]{:S(2)}) collective-permute-start(f32[12,8,256]{2,1,0:T(8,128)S(1)} %pad_maximum_fusion.1), channel_id=1, source_target_pairs={{0,8},{1,2},{2,1},{3,4},{4,3},{5,6},{6,5},{7,15},{8,0},{9,10},{10,... | collective-permute-start | bytes 294920 | tf_op jit(solution)/shard_map/ppermute | solution.py:495
  23.9 0.0 collective-permute-done.8.refs_11_
  23.9 0.0 collective-permute-done.7.refs_10_
  24.0 0.0 collective-permute-done.5.refs_7_
  24.0 2.9 %collective-permute-done.6.refs_8_ = f32[12,8,256]{2,1,0:T(8,128)S(1)} collective-permute-done((f32[12,8,256]{2,1,0:T(8,128)S(1)}, f32[12,8,256]{2,1,0:T(8,128)S(1)}, u32[]{:S(2)}, u32[]{:S(2)}) %collective-permute-start.6) | collective-permute-done | bytes 98336 | tf_op jit(solution)/shard_map/ppermute | solution.py:495
  26.9 2.1 %chain_and_spread.1 = f32[1,8,32,1024]{3,2,1,0:T(8,128)} custom-call(f32[8,8,256]{2,1,0:T(8,128)S(1)} %collective-permute-done.2.refs_0_, f32[8,8,256]{2,1,0:T(8,128)S(1)} %collective-permute-done.3.refs_1_, f32[8,8,256]{2,1,0:T(8,128)S(1)} %collective-permute-done.4.refs_2_, f32[8,8,48,128]{3,2,1,0:T(8,128)S(1)} %get-tuple-element.21.refs_3_, ...), custom_call_target="tpu_custom_call" | custom-call | tf_op jit(solution)/shard_map/chain_and_spread/pallas_call | solution.py:692
  (7 shorter events, 0.1 us)
Async XLA Ops:
  0.0 1.8 %copy-start.2 = (bf16[8,32,1024]{2,1,0:T(8,128)(2,1)S(1)}, bf16[8,32,1024]{2,1,0:T(8,128)(2,1)}, u32[]{:S(2)}) copy-start(bf16[8,32,1024]{2,1,0:T(8,128)(2,1)} %g_hbm.3) | copy-start | bytes 1572868
  0.0 1.8 %copy-start.1 = (bf16[8,32,1024]{2,1,0:T(8,128)(2,1)S(1)}, bf16[8,32,1024]{2,1,0:T(8,128)(2,1)}, u32[]{:S(2)}) copy-start(bf16[8,32,1024]{2,1,0:T(8,128)(2,1)} %k_hbm.3) | copy-start | bytes 1572868
  0.0 1.8 %copy-start = (f32[1,8,32,1024]{3,2,1,0:T(8,128)S(1)}, f32[1,8,32,1024]{3,2,1,0:T(8,128)}, u32[]{:S(2)}) copy-start(f32[1,8,32,1024]{3,2,1,0:T(8,128)} %u_hbm.3) | copy-start | bytes 3145732
  2.3 3.2 %collective-permute-start = (f32[11,8,1024]{2,1,0:T(8,128)S(1)}, f32[11,8,1024]{2,1,0:T(8,128)S(1)}, u32[]{:S(2)}, u32[]{:S(2)}) collective-permute-start(f32[11,8,1024]{2,1,0:T(8,128)S(1)} %even_rows.1), channel_id=1, source_target_pairs={{0,1},{1,0},{2,3},{3,2},{4,5},{5,4},{6,7},{7,6},{8,9},{9,8},{10,11... | collective-permute-start | bytes 1081352 | tf_op jit(solution)/shard_map/ppermute | solution.py:769
  2.8 8.5 %collective-permute-start.1 = (f32[8,8,1024]{2,1,0:T(8,128)S(1)}, f32[8,8,1024]{2,1,0:T(8,128)S(1)}, u32[]{:S(2)}, u32[]{:S(2)}) collective-permute-start(f32[8,8,1024]{2,1,0:T(8,128)S(1)} %odd_rows.1), channel_id=1, source_target_pairs={{0,8},{1,2},{2,1},{3,4},{4,3},{5,6},{6,5},{7,15},{8,0},{9,10},{10,... | collective-permute-start | bytes 786440 | tf_op jit(solution)/shard_map/ppermute | solution.py:495
  12.0 10.0 %collective-permute-start.4 = (f32[8,8,256]{2,1,0:T(8,128)S(1)}, f32[8,8,256]{2,1,0:T(8,128)S(1)}, u32[]{:S(2)}, u32[]{:S(2)}) collective-permute-start(f32[8,8,256]{2,1,0:T(8,128)S(1)} %get-tuple-element.20.refs_6_), channel_id=1, source_target_pairs={{0,8},{8,16},{16,24},{24,0},{1,9},{9,17},{17,25},{25,1},{2,10},{10... | collective-permute-start | bytes 196616 | tf_op jit(solution)/shard_map/ppermute | solution.py:778
  13.6 8.4 %collective-permute-start.3 = (f32[8,8,256]{2,1,0:T(8,128)S(1)}, f32[8,8,256]{2,1,0:T(8,128)S(1)}, u32[]{:S(2)}, u32[]{:S(2)}) collective-permute-start(f32[8,8,256]{2,1,0:T(8,128)S(1)} %get-tuple-element.20.refs_6_), channel_id=1, source_target_pairs={{0,16},{8,24},{16,0},{24,8},{1,17},{9,25},{17,1},{25,9},{2,18},{10... | collective-permute-start | bytes 196616 | tf_op jit(solution)/shard_map/ppermute | solution.py:778
  16.2 5.8 %collective-permute-start.2 = (f32[8,8,256]{2,1,0:T(8,128)S(1)}, f32[8,8,256]{2,1,0:T(8,128)S(1)}, u32[]{:S(2)}, u32[]{:S(2)}) collective-permute-start(f32[8,8,256]{2,1,0:T(8,128)S(1)} %get-tuple-element.20.refs_6_), channel_id=1, source_target_pairs={{0,24},{8,0},{16,8},{24,16},{1,25},{9,1},{17,9},{25,17},{2,26},{10... | collective-permute-start | bytes 196616 | tf_op jit(solution)/shard_map/ppermute | solution.py:778
  17.6 6.4 %collective-permute-start.8 = (f32[2,6,8,256]{3,2,1,0:T(8,128)S(1)}, f32[2,6,8,256]{3,2,1,0:T(8,128)S(1)}, u32[]{:S(2)}, u32[]{:S(2)}) collective-permute-start(f32[2,6,8,256]{3,2,1,0:T(8,128)S(1)} %get-tuple-element.25), channel_id=1, source_target_pairs={{0,8},{1,2},{2,1},{3,4},{4,3},{5,6},{6,5},{7,15},{8,0},{9,10},{10,... | collective-permute-start | bytes 294920 | tf_op jit(solution)/shard_map/ppermute | solution.py:495
  18.3 5.7 %collective-permute-start.7 = (f32[2,6,8,256]{3,2,1,0:T(8,128)S(1)}, f32[2,6,8,256]{3,2,1,0:T(8,128)S(1)}, u32[]{:S(2)}, u32[]{:S(2)}) collective-permute-start(f32[2,6,8,256]{3,2,1,0:T(8,128)S(1)} %get-tuple-element.26), channel_id=1, source_target_pairs={{0,1},{1,0},{2,3},{3,2},{4,5},{5,4},{6,7},{7,6},{8,9},{9,8},{10,11... | collective-permute-start | bytes 294920 | tf_op jit(solution)/shard_map/ppermute | solution.py:775
  22.1 1.9 %collective-permute-start.5 = (f32[12,8,256]{2,1,0:T(8,128)S(1)}, f32[12,8,256]{2,1,0:T(8,128)S(1)}, u32[]{:S(2)}, u32[]{:S(2)}) collective-permute-start(f32[12,8,256]{2,1,0:T(8,128)S(1)} %pad_maximum_fusion), channel_id=1, source_target_pairs={{0,1},{1,0},{2,3},{3,2},{4,5},{5,4},{6,7},{7,6},{8,9},{9,8},{10,11... | collective-permute-start | bytes 294920 | tf_op jit(solution)/shard_map/ppermute | solution.py:788
  22.2 4.7 %collective-permute-start.6 = (f32[12,8,256]{2,1,0:T(8,128)S(1)}, f32[12,8,256]{2,1,0:T(8,128)S(1)}, u32[]{:S(2)}, u32[]{:S(2)}) collective-permute-start(f32[12,8,256]{2,1,0:T(8,128)S(1)} %pad_maximum_fusion.1), channel_id=1, source_target_pairs={{0,8},{1,2},{2,1},{3,4},{4,3},{5,6},{6,5},{7,15},{8,0},{9,10},{10,... | collective-permute-start | bytes 294920 | tf_op jit(solution)/shard_map/ppermute | solution.py:495

commit v5 on v4

--- a/solution.py
+++ b/solution.py
@@ -128,16 +128,43 @@
     a_ref[row] = 1.0 + (g - 6.0 * k)
 
 
-def put_pooled(ref, sums, pool):
+def put_pooled(ref, row, sums, pool):
     thin = ref.shape[2] // 4
     small = split_dot(jnp.concatenate(sums, axis=0), pool)
     for i in range(4):
-        row = small[8 * i : 8 * i + 8] * (1.0 if i < 2 else 2.0 * DT)
-        ref[ref.shape[0] - 1, :, i * thin : (i + 1) * thin] = row
+        value = small[8 * i : 8 * i + 8] * (1.0 if i < 2 else 2.0 * DT)
+        ref[row, :, i * thin : (i + 1) * thin] = value
 
 
 def sums_of_four(*arrays):
     return [(r[0] + r[1]) + (r[2] + r[3]) for r in arrays]
+
+
+def message(high, u_rows, k_rows, g_rows, ref, last_ref, last_row, state, after, coefs, pool, edges):
+    breadth = ref.shape[2]
+    near = 4 if high else 1
+    step = -1 if high else 1
+    zeros = jnp.zeros((8, breadth), F32)
+    state[0] = zeros
+    state[5] = zeros
+    after[0] = zeros
+    after[3] = zeros
+    for i in range(4):
+        state[1 + i] = u_rows[(4 if high else 0) + i]
+        set_coefs(k_rows[i], g_rows[i], *coefs, 1 + i)
+    ref[0] = state[near]
+    put_tiles(ref, 1, fine_row(state, near, *coefs, near, breadth, edges))
+    one = fine_row(state, near + step, *coefs, near + step, breadth, edges)
+    two = fine_row(state, near + 2 * step, *coefs, near + 2 * step, breadth, edges)
+    put_tiles(ref, 2, one)
+    place = 2 if high else 1
+    put_tiles(after, place, one)
+    put_tiles(after, place + step, two)
+    put_tiles(ref, 3, fine_row(after, place, *coefs, near + step, breadth, edges))
+    ref[4] = k_rows[near - 1]
+    ref[5] = g_rows[near - 1]
+    ref[6] = k_rows[near - 1 + step]
+    put_pooled(last_ref, last_row, sums_of_four(u_rows[:4], u_rows[4:], k_rows, g_rows), pool)
 
 
 def odd_kernel(
@@ -156,11 +183,6 @@
         copy.start()
     pool = pool_matrix(breadth, 1.0 / 16.0)
     edges = masks()
-    zeros = jnp.zeros((8, breadth), F32)
-    state[0] = zeros
-    state[5] = zeros
-    after[0] = zeros
-    after[3] = zeros
     for copy in copies:
         copy.wait()
     k_wide[...] = k_nat[...].astype(F32)
@@ -171,24 +193,8 @@
         u_rows = [u_nat[:, i, :] for i in range(8)]
         k_rows = [k_wide[:, low + i, :] for i in range(4)]
         g_rows = [g_wide[:, low + i, :] for i in range(4)]
-        near = 4 if high else 1
-        step = -1 if high else 1
-        for i in range(4):
-            state[1 + i] = u_rows[(4 if high else 0) + i]
-            set_coefs(k_rows[i], g_rows[i], coef_a, coef_b, coef_k, 1 + i)
-        odd_ref[0] = state[near]
-        put_tiles(odd_ref, 1, fine_row(state, near, coef_a, coef_b, coef_k, near, breadth, edges))
-        one = fine_row(state, near + step, coef_a, coef_b, coef_k, near + step, breadth, edges)
-        two = fine_row(state, near + 2 * step, coef_a, coef_b, coef_k, near + 2 * step, breadth, edges)
-        put_tiles(odd_ref, 2, one)
-        place = 2 if high else 1
-        put_tiles(after, place, one)
-        put_tiles(after, place + step, two)
-        put_tiles(odd_ref, 3, fine_row(after, place, coef_a, coef_b, coef_k, near + step, breadth, edges))
-        odd_ref[4] = k_rows[near - 1]
-        odd_ref[5] = g_rows[near - 1]
-        odd_ref[6] = k_rows[near - 1 + step]
-        put_pooled(odd_ref, sums_of_four(u_rows[:4], u_rows[4:], k_rows, g_rows), pool)
+        coefs = (coef_a, coef_b, coef_k)
+        message(high, u_rows, k_rows, g_rows, odd_ref, odd_ref, 7, state, after, coefs, pool, edges)
 
     @pl.when(low_side)
     def _():
@@ -225,24 +231,26 @@
     )(starts, diffusivity, reaction)
 
 
-def even_kernel(odd_rows, u_ref, k_ref, g_ref, even_ref, k_wide, g_wide):
+def side_rows(high, u_ref, k_ref, g_ref, k_wide, g_wide):
+    height = u_ref.shape[2]
+    k_wide[...] = k_ref[:, height - 16 if high else 0 : height if high else 16, :].astype(F32)
+    g_wide[...] = g_ref[:, height - 16 if high else 0 : height if high else 16, :].astype(F32)
+    low = 12 if high else 0
+    u_rows = [u_ref[0, :, (height - 8 if high else 0) + i, :] for i in range(8)]
+    k_rows = [k_wide[:, low + i, :] for i in range(4)]
+    g_rows = [g_wide[:, low + i, :] for i in range(4)]
+    return u_rows, k_rows, g_rows
+
+
+def even_kernel(odd_rows, u_ref, k_ref, g_ref, even_ref, rest_ref, k_wide, g_wide, state, after, coef_a, coef_b, coef_k):
     del odd_rows
-    height, breadth = u_ref.shape[2:]
-    pool = pool_matrix(breadth, 1.0 / 16.0)
+    pool = pool_matrix(u_ref.shape[3], 1.0 / 16.0)
+    edges = masks()
 
     def fill(high):
-        k_wide[...] = k_ref[:, height - 16 if high else 0 : height if high else 16, :].astype(F32)
-        g_wide[...] = g_ref[:, height - 16 if high else 0 : height if high else 16, :].astype(F32)
-        low = 12 if high else 0
-        u_rows = [u_ref[0, :, (height - 8 if high else 0) + i, :] for i in range(8)]
-        k_rows = [k_wide[:, low + i, :] for i in range(4)]
-        g_rows = [g_wide[:, low + i, :] for i in range(4)]
-        for i in range(4):
-            even_ref[i] = u_rows[(4 if high else 0) + i]
-        for i in range(3):
-            even_ref[4 + i] = k_rows[(1 if high else 0) + i]
-            even_ref[7 + i] = g_rows[(1 if high else 0) + i]
-        put_pooled(even_ref, sums_of_four(u_rows[:4], u_rows[4:], k_rows, g_rows), pool)
+        coefs = (coef_a, coef_b, coef_k)
+        rows = side_rows(high, u_ref, k_ref, g_ref, k_wide, g_wide)
+        message(high, *rows, even_ref, rest_ref, 0, state, after, coefs, pool, edges)
 
     above = parity() == 0
 
@@ -257,31 +265,69 @@
 
 def even_pack(odd_rows, starts, diffusivity, reaction):
     breadth = starts.shape[3]
+    coef = pltpu.VMEM((6, 8, breadth), F32)
     return pl.pallas_call(
         even_kernel,
-        out_shape=struct(11, 8, breadth),
+        out_shape=[struct(7, 8, breadth), struct(1, 8, breadth)],
         in_specs=[ANY] + [VMEM] * 3,
-        out_specs=VMEM,
-        scratch_shapes=[pltpu.VMEM((8, 16, breadth), F32)] * 2,
+        out_specs=[VMEM] * 2,
+        scratch_shapes=[pltpu.VMEM((8, 16, breadth), F32)] * 2
+        + [coef, pltpu.VMEM((4, 8, breadth), F32), coef, coef, coef],
         compiler_params=params(16),
         name="even_rows",
     )(odd_rows, starts, diffusivity, reaction)
 
 
+def pooled_into(flat, targets, scales, pool):
+    count = len(targets)
+    _, _, small, breadth = flat.shape
+    thin = breadth // 4
+    means = split_dot(flat[0:count].reshape(count * 8 * small, breadth), pool).reshape(count, 8, small, thin)
+    for part in range(count):
+        flat[part, :, :, 0:thin] = means[part] * scales[part]
+        for r in range(small):
+            targets[part][r] = flat[part, :, r, 0:thin]
+
+
+def sums_of(ref, level, start, flat, part):
+    small = flat.shape[2]
+
+    def body(z, carry):
+        for x in range(ref.shape[1]):
+            rows = [ref[z + level, x, pl.ds(start + i, small, stride=4), :] for i in range(4)]
+            flat[part, z, :, x * LANES : (x + 1) * LANES] = (rows[0] + rows[1]) + (rows[2] + rows[3])
+        return carry
+
+    lax.fori_loop(0, 8, body, 0, unroll=2)
+
+
+def clear_ends(ref, top):
+    blank = jnp.zeros((8, LANES), F32)
+    columns = ref.shape[1]
+
+    def clear(z, carry):
+        for x in range(columns):
+            ref[z, x, 0:8, :] = blank
+            ref[z, x, top : top + 8, :] = blank
+        return carry
+
+    lax.fori_loop(0, 10, clear, 0)
+    for z in (0, 9):
+        for x in range(columns):
+            ref[z, x, 8:top, :] = jnp.zeros((top - 8, LANES), F32)
+
+
 def inner_kernel(
-    u_hbm, k_hbm, g_hbm, got_ref, fine_ref, steps_ref, coefs_ref, coarse_ref, end_ref,
+    u_hbm, k_hbm, g_hbm, fine_ref, low_ref, high_ref, coarse_ref, end_ref,
     one, two, coef_a, coef_b, coef_k, k_nat, g_nat, flat, sems,
 ):
     height, breadth = u_hbm.shape[2:]
     columns = breadth // LANES
-    small = height // 4
-    thin = breadth // 4
     spans = [slice(x * LANES, (x + 1) * LANES) for x in range(columns)]
-    above = parity() == 0
-    own = pl.multiple_of(jnp.where(above, 0, 8), 8)
+    top = height + 8
     copies = [
         pltpu.make_async_copy(
-            u_hbm.at[0, :, :, pl.ds(x * LANES, LANES)], one.at[pl.ds(1, 8), x, pl.ds(8 + own, height), :], sems.at[x]
+            u_hbm.at[0, :, :, pl.ds(x * LANES, LANES)], one.at[pl.ds(1, 8), x, pl.ds(8, height), :], sems.at[x]
         )
         for x in range(columns)
     ]
@@ -289,47 +335,9 @@
     g_copy = pltpu.make_async_copy(g_hbm, g_nat, sems.at[columns + 1])
     for copy in [k_copy, g_copy] + copies:
         copy.start()
-    blank = jnp.zeros((8, LANES), F32)
-    top = height + 16
-
-    def clear(z, carry):
-        for ref in (one, two):
-            for x in range(columns):
-                ref[z, x, 0:8, :] = blank
-                ref[z, x, top : top + 8, :] = blank
-        return carry
-
-    lax.fori_loop(0, 10, clear, 0)
-    for ref in (one, two):
-        for z in (0, 9):
-            for x in range(columns):
-                ref[z, x, 8:top, :] = jnp.zeros((height + 8, LANES), F32)
-
-    def place(u_row, c_row, tile):
-        for x in range(columns):
-            for z in range(8):
-                one[1 + z, x, 8 + tile : 16 + tile, :] = blank
-                coef_a[z, x, tile : tile + 8, :] = blank
-                coef_b[z, x, tile : tile + 8, :] = blank
-                coef_k[z, x, tile : tile + 8, :] = blank
-        for x, span in enumerate(spans):
-            for i in range(4):
-                one[1:9, x, u_row + i, :] = got_ref[i, :, span]
-            for i in range(3):
-                k = DT * got_ref[4 + i, :, span]
-                g = DT * got_ref[7 + i, :, span]
-                coef_k[:, x, c_row + i, :] = k
-                coef_b[:, x, c_row + i, :] = g * (1.0 / 3.0)
-                coef_a[:, x, c_row + i, :] = 1.0 + (g - 6.0 * k)
-
-    @pl.when(above)
-    def _():
-        place(8 + height, height, height)
-
-    @pl.when(jnp.logical_not(above))
-    def _():
-        place(12, 5, 0)
-
+    clear_ends(one, top)
+    clear_ends(two, top)
+    pool = pool_matrix(breadth, 1.0 / 16.0)
     k_copy.wait()
     g_copy.wait()
 
@@ -338,18 +346,22 @@
             for r in range(0, height, 16):
                 k = DT * k_nat[z, r : r + 16, span].astype(F32)
                 g = DT * g_nat[z, r : r + 16, span].astype(F32)
-                rows = pl.ds(own + r, 16)
-                coef_k[z, x, rows, :] = k
-                coef_b[z, x, rows, :] = g * (1.0 / 3.0)
-                coef_a[z, x, rows, :] = 1.0 + (g - 6.0 * k)
+                coef_k[z, x, r : r + 16, :] = k
+                coef_b[z, x, r : r + 16, :] = g * (1.0 / 3.0)
+                coef_a[z, x, r : r + 16, :] = 1.0 + (g - 6.0 * k)
         return carry
 
     lax.fori_loop(0, 8, widen, 0)
     for copy in copies:
         copy.wait()
+    sums_of(one, 1, 8, flat, 0)
+    sums_of(coef_k, 0, 0, flat, 1)
+    sums_of(coef_b, 0, 0, flat, 2)
+    pooled_into(flat, [coarse_ref.at[0], coarse_ref.at[1], coarse_ref.at[2]], (1.0, 2.0, 6.0), pool)
 
     lane = lax.broadcasted_iota(jnp.int32, (8, LANES), 1)
     first, final = lane == 0, lane == LANES - 1
+    blank = jnp.zeros((8, LANES), F32)
 
     def sweep(source, target, level, shift):
         def body(z, carry):
@@ -367,94 +379,44 @@
                     own_part = u * (coef_a[z, x, rows, :] - coef_b[z, x, rows, :] * (u * u))
                     spread = coef_k[z, x, rows, :] * ((plus + minus) + levels)
                     out = (own_part + spread) - (0.5 * VEL * DT) * (plus - minus)
-                    if shift is None:
-                        target[z + level, x, row : row + 8, :] = out
-                    else:
-                        target[z + level, x, pl.ds(pl.multiple_of(row + shift, 8), 8), :] = out
+                    target[z + level, x, row + shift : row + shift + 8, :] = out
             return carry
 
         lax.fori_loop(0, 8, body, 0, unroll=8)
 
     def keep(step, source):
-        def write(row):
-            for x, span in enumerate(spans):
-                for i in range(2):
-                    steps_ref[2 * step + i, :, span] = source[1:9, x, row + i, :]
-
-        @pl.when(above)
-        def _():
-            write(8 + step)
-
-        @pl.when(jnp.logical_not(above))
-        def _():
-            write(16 + height - 2 - step)
-
-    def keep_coefs(row):
         for x, span in enumerate(spans):
-            for i in range(4):
-                coefs_ref[0, i, :, span] = coef_a[:, x, row + i, :]
-                coefs_ref[1, i, :, span] = coef_b[:, x, row + i, :]
-                coefs_ref[2, i, :, span] = coef_k[:, x, row + i, :]
-
-    @pl.when(above)
-    def _():
-        keep_coefs(0)
-
-    @pl.when(jnp.logical_not(above))
-    def _():
-        keep_coefs(8 + height - 4)
-
-    pool = pool_matrix(breadth, 1.0 / 16.0)
-
-    def sums_of(ref, level, start, part):
-        def body(z, carry):
-            for x, span in enumerate(spans):
-                parts = [ref[z + level, x, pl.ds(start + i, small, stride=4), :] for i in range(4)]
-                flat[part, z, :, span] = (parts[0] + parts[1]) + (parts[2] + parts[3])
-            return carry
-
-        lax.fori_loop(0, 8, body, 0, unroll=2)
-
-    def pooled_into(targets, scales):
-        count = len(targets)
-        means = split_dot(flat[0:count].reshape(count * 8 * small, breadth), pool).reshape(count, 8, small, thin)
-        for part in range(count):
-            flat[part, :, :, 0:thin] = means[part] * scales[part]
-            for r in range(small):
-                targets[part][r] = flat[part, :, r, 0:thin]
-
-    sums_of(one, 1, 8 + own, 0)
-    sums_of(coef_k, 0, own, 1)
-    sums_of(coef_b, 0, own, 2)
-    pooled_into([coarse_ref.at[0], coarse_ref.at[1], coarse_ref.at[2]], (1.0, 2.0, 6.0))
-    keep(0, one)
-    sweep(one, two, 1, None)
+            for i in range(2):
+                low_ref[2 * step - 2 + i, :, span] = source[1:9, x, 8 + step + i, :]
+                high_ref[2 * step - 2 + i, :, span] = source[1:9, x, top - 2 - step + i, :]
+
+    sweep(one, two, 1, 0)
     keep(1, two)
-    sweep(two, one, 1, None)
+    sweep(two, one, 1, 0)
     keep(2, one)
-    sweep(one, two, 1, None)
+    sweep(one, two, 1, 0)
     keep(3, two)
-    sweep(two, fine_ref, 0, jnp.where(above, 0, -8))
-    sums_of(fine_ref, 0, 8, 0)
-    pooled_into([end_ref], (1.0,))
-
-
-def inner(starts, diffusivity, reaction, got):
+    sweep(two, fine_ref, 0, -8)
+    sums_of(fine_ref, 0, 0, flat, 0)
+    pooled_into(flat, [end_ref], (1.0,), pool)
+
+
+def inner(starts, diffusivity, reaction):
     height, breadth = starts.shape[2:]
     small = height // 4
     columns = breadth // LANES
-    wide = pltpu.VMEM((10, columns, height + 24, LANES), F32)
-    coef = pltpu.VMEM((8, columns, height + 8, LANES), F32)
+    wide = pltpu.VMEM((10, columns, height + 16, LANES), F32)
+    coef = pltpu.VMEM((8, columns, height, LANES), F32)
     return pl.pallas_call(
         inner_kernel,
         out_shape=[
-            struct(8, columns, height + 16, LANES),
-            struct(8, 8, breadth),
-            struct(3, 4, 8, breadth),
+            struct(8, columns, height, LANES),
+            struct(6, 8, breadth),
+            struct(6, 8, breadth),
             struct(3, small, 8, breadth // 4),
             struct(small, 8, breadth // 4),
         ],
-        in_specs=[ANY] * 3 + [VMEM],
+        in_specs=[ANY] * 3,
         out_specs=[VMEM] * 5,
         scratch_shapes=[wide, wide, coef, coef, coef]
         + [
@@ -463,10 +425,10 @@
             pltpu.VMEM((3, 8, small, breadth), F32),
             pltpu.SemaphoreType.DMA((columns + 2,)),
         ],
-        compiler_params=params(28),
+        compiler_params=params(24),
         cost_estimate=pl.CostEstimate(flops=30_000_000, bytes_accessed=4_000_000, transcendentals=0),
         name="inner_updates",
-    )(starts, diffusivity, reaction, got)
+    )(starts, diffusivity, reaction)
 
 
 def rows_for(array, low_side, reach):
@@ -501,32 +463,39 @@
     return jnp.where(jnp.logical_or(place == 0, place == last), 0.0, 1.0).astype(F32)
 
 
-def edge_kernel(
-    steps_ref, coefs_ref, got_ref, even_ref, end_in, coarse_ref, rows_ref, end_ref, jump_ref,
-    zero, one, two, three, coef_a, coef_b, coef_k, seen, half, coarse_k, coarse_g,
-):
+def mend(low, live, outer, low_ref, high_ref, got_ref, rows_ref, buffers, edges):
+    outer_ref, outer_a, outer_b, outer_k = outer
+    zero, one, two, three, coef_a, coef_b, coef_k = buffers
     breadth = got_ref.shape[2]
-    small = end_ref.shape[0]
-    low_side = parity() == 0
-    live = alive()
-    edges = masks()
     states = (zero, one, two, three, rows_ref)
 
     def index(distance):
-        return jnp.where(low_side, 4 + distance, 7 - distance)
+        return jnp.where(low, 4 + distance, 7 - distance)
 
     for i in range(4):
-        coef_a[4 + i] = coefs_ref[0, i]
-        coef_b[4 + i] = coefs_ref[1, i]
-        coef_k[4 + i] = coefs_ref[2, i]
+        coef_a[4 + i] = outer_a[1 + i]
+        coef_b[4 + i] = outer_b[1 + i]
+        coef_k[4 + i] = outer_k[1 + i]
     set_coefs(got_ref[4], got_ref[5], coef_a, coef_b, coef_k, index(-1))
     zero[index(-1)] = got_ref[0] * live
     one[index(-2)] = got_ref[2] * live
-    for step in range(4):
-        at = jnp.where(low_side, 4 + step, 6 - step)
-        for i in range(2):
-            states[step][at + i] = steps_ref[2 * step + i]
-    toward = jnp.where(low_side, -0.5 * VEL * DT, 0.5 * VEL * DT)
+    at = jnp.where(low, 4, 6)
+    for i in range(2):
+        zero[at + i] = outer_ref[jnp.where(low, 1, 3) + i]
+
+    @pl.when(low)
+    def _():
+        for step in range(1, 4):
+            for i in range(2):
+                states[step][4 + step + i] = low_ref[2 * step - 2 + i]
+
+    @pl.when(jnp.logical_not(low))
+    def _():
+        for step in range(1, 4):
+            for i in range(2):
+                states[step][6 - step + i] = high_ref[2 * step - 2 + i]
+
+    toward = jnp.where(low, -0.5 * VEL * DT, 0.5 * VEL * DT)
     one[index(-1)] = (got_ref[1] + (DT * got_ref[4] + toward) * zero[index(0)]) * live
     two[index(-2)] = (got_ref[3] + (DT * got_ref[6] + toward) * one[index(-1)]) * live
     for step in range(1, 5):
@@ -536,6 +505,67 @@
             if distance < 0:
                 tiles = [t * live for t in tiles]
             put_tiles(states[step], at - 4 if step == 4 else at, tiles)
+
+
+def even_edge_kernel(
+    u_ref, k_ref, g_ref, low_ref, high_ref, got_ref, end_in, rows_ref, end_ref, odd_own, odd_a, odd_b, odd_k,
+    k_wide, g_wide, even_own, even_a, even_b, even_k, *buffers
+):
+    breadth = got_ref.shape[2]
+    small = end_ref.shape[0]
+    low = parity() == 1
+
+    def fill(high):
+        for side, own, coefs in ((high, even_own, (even_a, even_b, even_k)), (1 - high, odd_own, (odd_a, odd_b, odd_k))):
+            u_rows, k_rows, g_rows = side_rows(side, u_ref, k_ref, g_ref, k_wide, g_wide)
+            for i in range(4):
+                own[1 + i] = u_rows[(4 if side else 0) + i]
+                set_coefs(k_rows[i], g_rows[i], *coefs, 1 + i)
+
+    @pl.when(low)
+    def _():
+        fill(0)
+
+    @pl.when(jnp.logical_not(low))
+    def _():
+        fill(1)
+
+    outer = (even_own, even_a, even_b, even_k)
+    mend(low, 1.0, outer, low_ref, high_ref, got_ref, rows_ref, buffers, masks())
+    end_ref[...] = end_in[...]
+    pool = pool_matrix(breadth, 1.0 / 16.0)
+    end_ref[jnp.where(low, 0, small - 1)] = pooled(rows_ref, 0, 1, pool)
+
+
+def even_edge(starts, diffusivity, reaction, low, high, got, end):
+    breadth = got.shape[2]
+    side = struct(5, 8, breadth)
+    outs = pl.pallas_call(
+        even_edge_kernel,
+        out_shape=[struct(4, 8, breadth), struct(*end.shape), side, side, side, side],
+        in_specs=[VMEM] * 7,
+        out_specs=[VMEM] * 6,
+        scratch_shapes=[pltpu.VMEM((8, 16, breadth), F32)] * 2
+        + [pltpu.VMEM((5, 8, breadth), F32)] * 4
+        + [pltpu.VMEM((12, 8, breadth), F32)] * 7,
+        compiler_params=params(16),
+        name="even_edge",
+    )(starts, diffusivity, reaction, low, high, got, end)
+    return outs[0], outs[1], outs[2:]
+
+
+def edge_kernel(
+    outer_ref, outer_a, outer_b, outer_k, low_ref, high_ref, got_ref, even_ref, end_in, coarse_ref,
+    rows_ref, end_ref, jump_ref, zero, one, two, three, coef_a, coef_b, coef_k, seen, half, coarse_k, coarse_g,
+):
+    breadth = got_ref.shape[2]
+    small = end_ref.shape[0]
+    low_side = parity() == 0
+    live = alive()
+    edges = masks()
+    outer = (outer_ref, outer_a, outer_b, outer_k)
+    buffers = (zero, one, two, three, coef_a, coef_b, coef_k)
+    mend(low_side, live, outer, low_ref, high_ref, got_ref, rows_ref, buffers, edges)
     pool = pool_matrix(breadth, 1.0 / 16.0)
     end_ref[...] = end_in[...]
     end_ref[jnp.where(low_side, 0, small - 1)] = pooled(rows_ref, 0, 1, pool)
@@ -552,11 +582,11 @@
     for i in range(2):
         span = slice(i * thin, (i + 1) * thin)
         seen[odd_at + i] = got_ref[7, :, span] * live
-        seen[even_at + i] = even_ref[10, :, span]
+        seen[even_at + i] = even_ref[0, :, span]
     for i, ref in ((2, coarse_k), (3, coarse_g)):
         span = slice(i * thin, (i + 1) * thin)
         ref[near] = got_ref[7, :, span]
-        ref[far] = even_ref[10, :, span]
+        ref[far] = even_ref[0, :, span]
     coarse_sweep(seen, half, coarse_k, coarse_g, 1, small + 3, 2, small, low_side, live, edges)
     first = lax.axis_index("tm") == 0
     for r in range(small):
@@ -593,7 +623,7 @@
         put_tiles(target, row, tiles)
 
 
-def edge(steps, coefs, got, even_got, end, coarse):
+def edge(outer, low, high, got, even_got, end, coarse):
     breadth = got.shape[2]
     small = end.shape[0]
     wide = pltpu.VMEM((12, 8, breadth), F32)
@@ -605,18 +635,18 @@
             struct(small, 8, breadth // 4),
             struct(small, 8, breadth // 4),
         ],
-        in_specs=[VMEM] * 6,
+        in_specs=[VMEM] * 10,
         out_specs=[VMEM] * 3,
         scratch_shapes=[wide] * 7 + [thin] * 4,
         compiler_params=params(16),
         name="edge_updates",
-    )(steps, coefs, got, even_got, end, coarse)
+    )(*outer, low, high, got, even_got, end, coarse)
 
 
 def last_kernel(behind, *refs):
     before, refs = refs[:behind], refs[behind:]
-    fine_hbm, rows_ref, end_ref, jump_ref, even_j, odd_j, coarse_ref, even_c, odd_c, out_hbm = refs[:10]
-    fine_ref, out_ref, one, two, coarse_k, coarse_g, added, change, moved, sems = refs[10:]
+    fine_hbm, odd_rows, even_rows, end_ref, jump_ref, even_j, odd_j, coarse_ref, even_c, odd_c, out_hbm = refs[:11]
+    fine_ref, out_ref, one, two, coarse_k, coarse_g, added, change, moved, sems = refs[11:]
     reach = COARSE * behind
     height, breadth = out_hbm.shape[2:]
     columns = breadth // LANES
@@ -654,18 +684,19 @@
     moved[...] = split_dot(change[...].reshape(8 * small, breadth // 4), spread).reshape(8, small, breadth)
     fetch.wait()
 
-    def fix(row):
+    def fix(low_ref, high_ref):
         for x in range(columns):
             for i in range(4):
-                fine_ref[:, x, row + i, :] = rows_ref[i, :, x * LANES : (x + 1) * LANES]
+                fine_ref[:, x, i, :] = low_ref[i, :, x * LANES : (x + 1) * LANES]
+                fine_ref[:, x, height - 4 + i, :] = high_ref[i, :, x * LANES : (x + 1) * LANES]
 
     @pl.when(low_side)
     def _():
-        fix(8)
+        fix(odd_rows, even_rows)
 
     @pl.when(jnp.logical_not(low_side))
     def _():
-        fix(8 + height - 4)
+        fix(even_rows, odd_rows)
 
     lower = lax.broadcasted_iota(jnp.int32, (8, LANES), 0) < 4
 
@@ -675,7 +706,7 @@
             for row in range(0, height, 8):
                 c = row // 4
                 step = jnp.where(lower, moved[z, c : c + 1, span], moved[z, c + 1 : c + 2, span])
-                out_ref[z, row : row + 8, span] = fine_ref[z, x, 8 + row : 16 + row, :] + step
+                out_ref[z, row : row + 8, span] = fine_ref[z, x, row : row + 8, :] + step
         pltpu.make_async_copy(out_ref.at[z], out_hbm.at[0, z], sems.at[z]).start()
         return carry
 
@@ -684,7 +715,7 @@
         pltpu.make_async_copy(out_ref.at[z], out_hbm.at[0, z], sems.at[z]).wait()
 
 
-def last(fine, rows, end, jump, before, even_j, odd_j, coarse, even_c, odd_c, height):
+def last(fine, rows, even_rows, end, jump, before, even_j, odd_j, coarse, even_c, odd_c, height):
     breadth = rows.shape[2]
     small = height // 4
     reach = COARSE * len(before)
@@ -692,7 +723,7 @@
     return pl.pallas_call(
         functools.partial(last_kernel, len(before)),
         out_shape=struct(1, 8, height, breadth),
-        in_specs=[VMEM] * len(before) + [ANY] + [VMEM] * 8,
+        in_specs=[VMEM] * len(before) + [ANY] + [VMEM] * 9,
         out_specs=HBM,
         scratch_shapes=[pltpu.VMEM(fine.shape, F32), pltpu.VMEM((8, height, breadth), F32)]
         + [thin] * 5
@@ -703,7 +734,7 @@
         ],
         compiler_params=params(16),
         name="chain_and_spread",
-    )(*before, fine, rows, end, jump, even_j, odd_j, coarse, even_c, odd_c)
+    )(*before, fine, rows, even_rows, end, jump, even_j, odd_j, coarse, even_c, odd_c)
 
 
 def relay(jump, coarse, even_c, odd_c, even):
@@ -766,9 +797,12 @@
 
     odd_rows = odd_pack(starts, diffusivity, reaction)
     odd_got = swap_odd(odd_rows)
-    even_got = lax.ppermute(even_pack(odd_rows, starts, diffusivity, reaction), "space", even)
-    fine, steps, coefs, coarse, end = inner(starts, diffusivity, reaction, even_got)
-    rows, end, jump = edge(steps, coefs, odd_got, even_got, end, coarse)
+    even_rows, even_rest = even_pack(odd_rows, starts, diffusivity, reaction)
+    even_got = lax.ppermute(even_rows, "space", even)
+    even_got_rest = lax.ppermute(even_rest, "space", even)
+    fine, low_steps, high_steps, coarse, end = inner(starts, diffusivity, reaction)
+    mended, end, odd_outer = even_edge(starts, diffusivity, reaction, low_steps, high_steps, even_got, end)
+    rows, end, jump = edge(odd_outer, low_steps, high_steps, odd_got, even_got_rest, end, coarse)
     width = reach if at_once else COARSE
     later, jump = lax.optimization_barrier((coarse[1:], jump))
     odd_c = swap_odd(rows_for(later, low_side, width))
@@ -779,19 +813,20 @@
             for k in range(behind, 0, -1)
         ]
 
-        def outer(low):
+        def halo(low):
             return jnp.concatenate(
                 [rows_for(before[j][None], low, reach - COARSE * j)[0] for j in range(behind)], axis=0
             )
 
-        odd_j = swap_odd(outer(low_side))
-        even_j = lax.ppermute(outer(high_side), "space", even)
-        return last(fine, rows, end, jump, before, even_j, odd_j, coarse, even_c, odd_c, height)
+        odd_j = swap_odd(halo(low_side))
+        even_j = lax.ppermute(halo(high_side), "space", even)
+        return last(fine, rows, mended, end, jump, before, even_j, odd_j, coarse, even_c, odd_c, height)
     chained = relay(jump, coarse, even_c, odd_c, even)
     change = jnp.repeat(jnp.repeat(jnp.transpose(chained - end, (1, 0, 2)), 4, axis=1), 4, axis=2)
     fixed = jnp.where(low_side, 0, height - 4)
-    fine = jnp.transpose(fine[:, :, 8 : 8 + height], (0, 2, 1, 3)).reshape(8, height, breadth)
+    fine = jnp.transpose(fine, (0, 2, 1, 3)).reshape(8, height, breadth)
     fine = lax.dynamic_update_slice_in_dim(fine, jnp.transpose(rows, (1, 0, 2)), fixed, axis=1)
+    fine = lax.dynamic_update_slice_in_dim(fine, jnp.transpose(mended, (1, 0, 2)), height - 4 - fixed, axis=1)
     return (fine + change)[None]
 
 

time: 29.2 us -> 29 us (level)
  waiting for transfers between devices: 5.65 us -> 5.01 us
    ppermute x3, waiting for transfers between devices: 2.75 us -> 2.12 us  [per_device(): lax.ppermute(jump, 'tm', [(i, (i + k) % slices) for i in range(slices)])]
    ppermute x2 -> x3, starting transfers between devices: 0.59 us -> 0.65 us  [the longest x1 0.47 us: per_device(): even_got_rest = lax.ppermute(even_rest, 'space', even)]
    pallas_call x2 -> x3, Pallas kernels: 6.31 us -> 6.31 us  [the longest x1 4.72 us: inner(): pl.pallas_call(inner_kernel, out_shape=[struct(8, columns, height, LANES)...]
  transfers between devices with their start and end apart: 9 -> 10, of which waited for: 2 -> 2; matrix products, arithmetic and copies ran while one was open for 0% -> 0% of each run, Pallas kernels for 20% -> 22%
where the time goes in v5:
time: 29 us; the launch traced here: 28.5 us
  starting transfers between devices  12.4 us (43%)
  Pallas kernels  10.9 us (38%)
  waiting for transfers between devices  5.01 us (17%)
    ppermute x3, starting transfers between devices, per_device(): lax.ppermute(jump, 'tm', [(i, (i + k) % slices) for i in range(slices)])  5.56 us
    ppermute x3, starting transfers between devices, swap_odd(): return lax.ppermute(block, ('tm', 'space'), pairs)  5.25 us
    pallas_call x1, Pallas kernels, inner(): pl.pallas_call(inner_kernel, out_shape=[struct(8, columns, height, LANES)...  4.72 us
    ppermute x3, waiting for transfers between devices, swap_odd(): return lax.ppermute(block, ('tm', 'space'), pairs)  2.86 us
    pallas_call x1, Pallas kernels, last(): pl.pallas_call(functools.partial(last_kernel, len(before)), out_shape=str...  2.15 us
    ppermute x3, waiting for transfers between devices, per_device(): lax.ppermute(jump, 'tm', [(i, (i + k) % slices) for i in range(slices)])  2.12 us
    pallas_call x1, Pallas kernels, odd_pack(): pl.pallas_call(odd_kernel, out_shape=struct(8, 8, breadth), in_specs=[HBM...  1.77 us
    pallas_call x1, Pallas kernels, even_edge(): pl.pallas_call(even_edge_kernel, out_shape=[struct(4, 8, breadth), struct...  1.05 us
  transfers between devices with their start and end apart: 10, of which 2 were waited for; matrix products, arithmetic and copies ran while one was open for 0% of the time, Pallas kernels for 22%

profile of v5, /device:TPU:0, one launch (start us, length us, event | category | flops | bytes accessed | tf_op | source)
XLA Modules:
  0.0 28.5 jit_solution(5719379014644270815)
XLA Ops:
  0.0 0.0 copy-start.2
  0.0 0.0 copy-start.1
  0.0 0.0 copy-start
  0.0 1.8 %odd_rows.1 = f32[8,8,1024]{2,1,0:T(8,128)S(1)} custom-call(f32[1,8,32,1024]{3,2,1,0:T(8,128)} %u_ref.3, bf16[8,32,1024]{2,1,0:T(8,128)(2,1)} %k_ref.3, bf16[8,32,1024]{2,1,0:T(8,128)(2,1)} %g_ref.3), custom_call_target="tpu_custom_call" | custom-call | tf_op jit(solution)/shard_map/odd_rows/pallas_call | solution.py:211
  1.8 3.1 %collective-permute-start.1 = (f32[8,8,1024]{2,1,0:T(8,128)S(1)}, f32[8,8,1024]{2,1,0:T(8,128)S(1)}, u32[]{:S(2)}, u32[]{:S(2)}) collective-permute-start(f32[8,8,1024]{2,1,0:T(8,128)S(1)} %odd_rows.1), channel_id=1, source_target_pairs={{0,8},{1,2},{2,1},{3,4},{4,3},{5,6},{6,5},{7,15},{8,0},{9,10},{10,... | collective-permute-start | bytes 786440 | tf_op jit(solution)/shard_map/ppermute | solution.py:457
  4.9 0.0 copy-done.2
  4.9 0.0 copy-done.1
  4.9 0.0 copy-done
  4.9 0.5 %even_rows.1 = (f32[7,8,1024]{2,1,0:T(8,128)S(1)}, f32[1,8,1024]{2,1,0:T(8,128)S(1)}) custom-call(f32[8,8,1024]{2,1,0:T(8,128)S(1)} %odd_rows.1, f32[1,8,32,1024]{3,2,1,0:T(8,128)S(1)} %copy-done, bf16[8,32,1024]{2,1,0:T(8,128)(2,1)S(1)} %copy-done.1, bf16[8,32,1024]{2,1,0:T(8,128)(2,1)S(1)} %copy-done.2), custom_call_target="tpu_custom_call" | custom-call | tf_op jit(solution)/shard_map/even_rows/pallas_call | solution.py:269
  5.4 0.1 collective-permute-start
  5.5 0.5 %collective-permute-start.2 = (f32[1,8,1024]{2,1,0:T(8,128)S(1)}, f32[1,8,1024]{2,1,0:T(8,128)S(1)}, u32[]{:S(2)}, u32[]{:S(2)}) collective-permute-start(f32[1,8,1024]{2,1,0:T(8,128)S(1)} %get-tuple-element.32), channel_id=1, source_target_pairs={{0,1},{1,0},{2,3},{3,2},{4,5},{5,4},{6,7},{7,6},{8,9},{9,8},{10,11... | collective-permute-start | bytes 98312 | tf_op jit(solution)/shard_map/ppermute | solution.py:802
  6.0 4.7 %inner_updates.1 = (f32[8,8,32,128]{3,2,1,0:T(8,128)S(1)}, f32[6,8,1024]{2,1,0:T(8,128)S(1)}, f32[6,8,1024]{2,1,0:T(8,128)S(1)}, f32[3,8,8,256]{3,2,1,0:T(8,128)S(1)}, f32[8,8,256]{2,1,0:T(8,128)S(1)}) custom-call(f32[1,8,32,1024]{3,2,1,0:T(8,128)S(1)} %copy-done, bf16[8,32,1024]{2,1,0:T(8,128)(2,1)S(1)} %copy-done.1, bf16[8,32,1024]{2,1,0:T(8,128)(2,1)S(1)} %copy-done.2), custom_call_target="tpu_custom_call" | custom-call | flops 30000000 | bytes 4000000 | tf_op jit(solution)/shard_map/inner_updates/pallas_call | solution.py:410
  10.8 0.0 collective-permute-done.got_ref
  10.8 1.0 %even_edge.1 = (f32[4,8,1024]{2,1,0:T(8,128)S(1)}, f32[8,8,256]{2,1,0:T(8,128)S(1)}, f32[5,8,1024]{2,1,0:T(8,128)S(1)}, f32[5,8,1024]{2,1,0:T(8,128)S(1)}, f32[5...) custom-call(f32[1,8,32,1024]{3,2,1,0:T(8,128)S(1)} %copy-done, bf16[8,32,1024]{2,1,0:T(8,128)(2,1)S(1)} %copy-done.1, ...), custom_call_target="tpu_custom_call" | custom-call | tf_op jit(solution)/shard_map/even_edge/pallas_call | solution.py:543
  11.8 0.0 collective-permute-done.2.even_ref
  11.8 0.0 collective-permute-done.1.got_ref
  11.9 0.7 %edge_updates.1 = (f32[4,8,1024]{2,1,0:T(8,128)S(1)}, f32[8,8,256]{2,1,0:T(8,128)S(1)}, f32[8,8,256]{2,1,0:T(8,128)S(1)}) custom-call(f32[5,8,1024]{2,1,0:T(8,128)S(1)} %get-tuple-element.28.outer_ref, f32[5,8,1024]{2,1,0:T(8,128)S(1)} %get-tuple-element.29.outer_a, f32[5,8,1024]{2,1,0:T(8,128)S(1)} %get-tuple-element.30.outer_b, ...), custom_call_target="tpu_custom_call" | custom-call | tf_op jit(solution)/shard_map/edge_updates/pallas_call | solution.py:631
  12.5 1.2 %collective-permute-start.5 = (f32[8,8,256]{2,1,0:T(8,128)S(1)}, f32[8,8,256]{2,1,0:T(8,128)S(1)}, u32[]{:S(2)}, u32[]{:S(2)}) collective-permute-start(f32[8,8,256]{2,1,0:T(8,128)S(1)} %get-tuple-element.35.refs_7_), channel_id=1, source_target_pairs={{0,8},{8,16},{16,24},{24,0},{1,9},{9,17},{17,25},{25,1},{2,10},{10... | collective-permute-start | bytes 196616 | tf_op jit(solution)/shard_map/ppermute | solution.py:812
  13.7 2.6 %collective-permute-start.4 = (f32[8,8,256]{2,1,0:T(8,128)S(1)}, f32[8,8,256]{2,1,0:T(8,128)S(1)}, u32[]{:S(2)}, u32[]{:S(2)}) collective-permute-start(f32[8,8,256]{2,1,0:T(8,128)S(1)} %get-tuple-element.35.refs_7_), channel_id=1, source_target_pairs={{0,16},{8,24},{16,0},{24,8},{1,17},{9,25},{17,1},{25,9},{2,18},{10... | collective-permute-start | bytes 196616 | tf_op jit(solution)/shard_map/ppermute | solution.py:812
  16.3 1.7 %collective-permute-start.3 = (f32[8,8,256]{2,1,0:T(8,128)S(1)}, f32[8,8,256]{2,1,0:T(8,128)S(1)}, u32[]{:S(2)}, u32[]{:S(2)}) collective-permute-start(f32[8,8,256]{2,1,0:T(8,128)S(1)} %get-tuple-element.35.refs_7_), channel_id=1, source_target_pairs={{0,24},{8,0},{16,8},{24,16},{1,25},{9,1},{17,9},{25,17},{2,26},{10... | collective-permute-start | bytes 196616 | tf_op jit(solution)/shard_map/ppermute | solution.py:812
  18.1 0.4 %collective-permute-start.9 = (f32[2,6,8,256]{3,2,1,0:T(8,128)S(1)}, f32[2,6,8,256]{3,2,1,0:T(8,128)S(1)}, u32[]{:S(2)}, u32[]{:S(2)}) collective-permute-start(f32[2,6,8,256]{3,2,1,0:T(8,128)S(1)} %get-tuple-element.41), channel_id=1, source_target_pairs={{0,8},{1,2},{2,1},{3,4},{4,3},{5,6},{6,5},{7,15},{8,0},{9,10},{10,... | collective-permute-start | bytes 294920 | tf_op jit(solution)/shard_map/ppermute | solution.py:457
  18.4 0.9 %collective-permute-start.8 = (f32[2,6,8,256]{3,2,1,0:T(8,128)S(1)}, f32[2,6,8,256]{3,2,1,0:T(8,128)S(1)}, u32[]{:S(2)}, u32[]{:S(2)}) collective-permute-start(f32[2,6,8,256]{3,2,1,0:T(8,128)S(1)} %get-tuple-element.42), channel_id=1, source_target_pairs={{0,1},{1,0},{2,3},{3,2},{4,5},{5,4},{6,7},{7,6},{8,9},{9,8},{10,11... | collective-permute-start | bytes 294920 | tf_op jit(solution)/shard_map/ppermute | solution.py:809
  19.4 2.1 %collective-permute-done.3.refs_0_ = f32[8,8,256]{2,1,0:T(8,128)S(1)} collective-permute-done((f32[8,8,256]{2,1,0:T(8,128)S(1)}, f32[8,8,256]{2,1,0:T(8,128)S(1)}, u32[]{:S(2)}, u32[]{:S(2)}) %collective-permute-start.3) | collective-permute-done | bytes 65568 | tf_op jit(solution)/shard_map/ppermute | solution.py:812
  21.5 0.0 collective-permute-done.5.refs_2_
  21.5 0.0 collective-permute-done.4.refs_1_
  21.6 0.1 collective-permute-start.6
  21.7 1.8 %collective-permute-start.7 = (f32[12,8,256]{2,1,0:T(8,128)S(1)}, f32[12,8,256]{2,1,0:T(8,128)S(1)}, u32[]{:S(2)}, u32[]{:S(2)}) collective-permute-start(f32[12,8,256]{2,1,0:T(8,128)S(1)} %pad_maximum_fusion.1), channel_id=1, source_target_pairs={{0,8},{1,2},{2,1},{3,4},{4,3},{5,6},{6,5},{7,15},{8,0},{9,10},{10,... | collective-permute-start | bytes 294920 | tf_op jit(solution)/shard_map/ppermute | solution.py:457
  23.5 0.0 collective-permute-done.9.refs_12_
  23.5 0.0 collective-permute-done.8.refs_11_
  23.5 0.0 collective-permute-done.6.refs_8_
  23.5 2.9 %collective-permute-done.7.refs_9_ = f32[12,8,256]{2,1,0:T(8,128)S(1)} collective-permute-done((f32[12,8,256]{2,1,0:T(8,128)S(1)}, f32[12,8,256]{2,1,0:T(8,128)S(1)}, u32[]{:S(2)}, u32[]{:S(2)}) %collective-permute-start.7) | collective-permute-done | bytes 98336 | tf_op jit(solution)/shard_map/ppermute | solution.py:457
  26.4 2.2 %chain_and_spread.1 = f32[1,8,32,1024]{3,2,1,0:T(8,128)} custom-call(f32[8,8,256]{2,1,0:T(8,128)S(1)} %collective-permute-done.3.refs_0_, f32[8,8,256]{2,1,0:T(8,128)S(1)} %collective-permute-done.4.refs_1_, f32[8,8,256]{2,1,0:T(8,128)S(1)} %collective-permute-done.5.refs_2_, f32[8,8,32,128]{3,2,1,0:T(8,128)S(1)} %get-tuple-element.36.refs_3_, ...), custom_call_target="tpu_custom_call" | custom-call | tf_op jit(solution)/shard_map/chain_and_spread/pallas_call | solution.py:723
  (7 shorter events, 0.1 us)
Async XLA Ops:
  0.0 4.9 %copy-start.2 = (bf16[8,32,1024]{2,1,0:T(8,128)(2,1)S(1)}, bf16[8,32,1024]{2,1,0:T(8,128)(2,1)}, u32[]{:S(2)}) copy-start(bf16[8,32,1024]{2,1,0:T(8,128)(2,1)} %g_ref.3) | copy-start | bytes 1572868
  0.0 4.9 %copy-start.1 = (bf16[8,32,1024]{2,1,0:T(8,128)(2,1)S(1)}, bf16[8,32,1024]{2,1,0:T(8,128)(2,1)}, u32[]{:S(2)}) copy-start(bf16[8,32,1024]{2,1,0:T(8,128)(2,1)} %k_ref.3) | copy-start | bytes 1572868
  0.0 4.9 %copy-start = (f32[1,8,32,1024]{3,2,1,0:T(8,128)S(1)}, f32[1,8,32,1024]{3,2,1,0:T(8,128)}, u32[]{:S(2)}) copy-start(f32[1,8,32,1024]{3,2,1,0:T(8,128)} %u_ref.3) | copy-start | bytes 3145732
  1.8 10.1 %collective-permute-start.1 = (f32[8,8,1024]{2,1,0:T(8,128)S(1)}, f32[8,8,1024]{2,1,0:T(8,128)S(1)}, u32[]{:S(2)}, u32[]{:S(2)}) collective-permute-start(f32[8,8,1024]{2,1,0:T(8,128)S(1)} %odd_rows.1), channel_id=1, source_target_pairs={{0,8},{1,2},{2,1},{3,4},{4,3},{5,6},{6,5},{7,15},{8,0},{9,10},{10,... | collective-permute-start | bytes 786440 | tf_op jit(solution)/shard_map/ppermute | solution.py:457
  5.4 5.3 %collective-permute-start = (f32[7,8,1024]{2,1,0:T(8,128)S(1)}, f32[7,8,1024]{2,1,0:T(8,128)S(1)}, u32[]{:S(2)}, u32[]{:S(2)}) collective-permute-start(f32[7,8,1024]{2,1,0:T(8,128)S(1)} %get-tuple-element.26), channel_id=1, source_target_pairs={{0,1},{1,0},{2,3},{3,2},{4,5},{5,4},{6,7},{7,6},{8,9},{9,8},{10,11... | collective-permute-start | bytes 688136 | tf_op jit(solution)/shard_map/ppermute | solution.py:801
  5.5 6.3 %collective-permute-start.2 = (f32[1,8,1024]{2,1,0:T(8,128)S(1)}, f32[1,8,1024]{2,1,0:T(8,128)S(1)}, u32[]{:S(2)}, u32[]{:S(2)}) collective-permute-start(f32[1,8,1024]{2,1,0:T(8,128)S(1)} %get-tuple-element.32), channel_id=1, source_target_pairs={{0,1},{1,0},{2,3},{3,2},{4,5},{5,4},{6,7},{7,6},{8,9},{9,8},{10,11... | collective-permute-start | bytes 98312 | tf_op jit(solution)/shard_map/ppermute | solution.py:802
  12.5 9.0 %collective-permute-start.5 = (f32[8,8,256]{2,1,0:T(8,128)S(1)}, f32[8,8,256]{2,1,0:T(8,128)S(1)}, u32[]{:S(2)}, u32[]{:S(2)}) collective-permute-start(f32[8,8,256]{2,1,0:T(8,128)S(1)} %get-tuple-element.35.refs_7_), channel_id=1, source_target_pairs={{0,8},{8,16},{16,24},{24,0},{1,9},{9,17},{17,25},{25,1},{2,10},{10... | collective-permute-start | bytes 196616 | tf_op jit(solution)/shard_map/ppermute | solution.py:812
  13.7 7.8 %collective-permute-start.4 = (f32[8,8,256]{2,1,0:T(8,128)S(1)}, f32[8,8,256]{2,1,0:T(8,128)S(1)}, u32[]{:S(2)}, u32[]{:S(2)}) collective-permute-start(f32[8,8,256]{2,1,0:T(8,128)S(1)} %get-tuple-element.35.refs_7_), channel_id=1, source_target_pairs={{0,16},{8,24},{16,0},{24,8},{1,17},{9,25},{17,1},{25,9},{2,18},{10... | collective-permute-start | bytes 196616 | tf_op jit(solution)/shard_map/ppermute | solution.py:812
  16.3 5.2 %collective-permute-start.3 = (f32[8,8,256]{2,1,0:T(8,128)S(1)}, f32[8,8,256]{2,1,0:T(8,128)S(1)}, u32[]{:S(2)}, u32[]{:S(2)}) collective-permute-start(f32[8,8,256]{2,1,0:T(8,128)S(1)} %get-tuple-element.35.refs_7_), channel_id=1, source_target_pairs={{0,24},{8,0},{16,8},{24,16},{1,25},{9,1},{17,9},{25,17},{2,26},{10... | collective-permute-start | bytes 196616 | tf_op jit(solution)/shard_map/ppermute | solution.py:812
  18.1 5.4 %collective-permute-start.9 = (f32[2,6,8,256]{3,2,1,0:T(8,128)S(1)}, f32[2,6,8,256]{3,2,1,0:T(8,128)S(1)}, u32[]{:S(2)}, u32[]{:S(2)}) collective-permute-start(f32[2,6,8,256]{3,2,1,0:T(8,128)S(1)} %get-tuple-element.41), channel_id=1, source_target_pairs={{0,8},{1,2},{2,1},{3,4},{4,3},{5,6},{6,5},{7,15},{8,0},{9,10},{10,... | collective-permute-start | bytes 294920 | tf_op jit(solution)/shard_map/ppermute | solution.py:457
  18.4 5.1 %collective-permute-start.8 = (f32[2,6,8,256]{3,2,1,0:T(8,128)S(1)}, f32[2,6,8,256]{3,2,1,0:T(8,128)S(1)}, u32[]{:S(2)}, u32[]{:S(2)}) collective-permute-start(f32[2,6,8,256]{3,2,1,0:T(8,128)S(1)} %get-tuple-element.42), channel_id=1, source_target_pairs={{0,1},{1,0},{2,3},{3,2},{4,5},{5,4},{6,7},{7,6},{8,9},{9,8},{10,11... | collective-permute-start | bytes 294920 | tf_op jit(solution)/shard_map/ppermute | solution.py:809
  21.6 1.9 %collective-permute-start.6 = (f32[12,8,256]{2,1,0:T(8,128)S(1)}, f32[12,8,256]{2,1,0:T(8,128)S(1)}, u32[]{:S(2)}, u32[]{:S(2)}) collective-permute-start(f32[12,8,256]{2,1,0:T(8,128)S(1)} %pad_maximum_fusion), channel_id=1, source_target_pairs={{0,1},{1,0},{2,3},{3,2},{4,5},{5,4},{6,7},{7,6},{8,9},{9,8},{10,11... | collective-permute-start | bytes 294920 | tf_op jit(solution)/shard_map/ppermute | solution.py:822
  21.7 4.7 %collective-permute-start.7 = (f32[12,8,256]{2,1,0:T(8,128)S(1)}, f32[12,8,256]{2,1,0:T(8,128)S(1)}, u32[]{:S(2)}, u32[]{:S(2)}) collective-permute-start(f32[12,8,256]{2,1,0:T(8,128)S(1)} %pad_maximum_fusion.1), channel_id=1, source_target_pairs={{0,8},{1,2},{2,1},{3,4},{4,3},{5,6},{6,5},{7,15},{8,0},{9,10},{10,... | collective-permute-start | bytes 294920 | tf_op jit(solution)/shard_map/ppermute | solution.py:457

commit v6 on v5

--- a/solution.py
+++ b/solution.py
@@ -643,22 +643,72 @@
     )(*outer, low, high, got, even_got, end, coarse)
 
 
+def ready_kernel(
+    odd_rows, even_rows, end_ref, jump_ref, coarse_ref, even_c, odd_c, fine_hbm,
+    fine_ref, gap_ref, coarse_k, coarse_g, spread_ref, sem,
+):
+    columns, height = fine_ref.shape[1:3]
+    reach = even_c.shape[1]
+    small = end_ref.shape[0]
+    fetch = pltpu.make_async_copy(fine_hbm, fine_ref, sem)
+    fetch.start()
+    low_side = parity() == 0
+    live = alive()
+    fill_coarse(coarse_k, coarse_ref.at[1], even_c.at[0], odd_c.at[0], reach, low_side, live)
+    fill_coarse(coarse_g, coarse_ref.at[2], even_c.at[1], odd_c.at[1], reach, low_side, live)
+    for r in range(small):
+        gap_ref[r] = jump_ref[r] - end_ref[r]
+    spread_ref[...] = spread_matrix(columns * LANES)
+    fetch.wait()
+
+    def fix(low_ref, high_ref):
+        for x in range(columns):
+            for i in range(4):
+                fine_ref[:, x, i, :] = low_ref[i, :, x * LANES : (x + 1) * LANES]
+                fine_ref[:, x, height - 4 + i, :] = high_ref[i, :, x * LANES : (x + 1) * LANES]
+
+    @pl.when(low_side)
+    def _():
+        fix(odd_rows, even_rows)
+
+    @pl.when(jnp.logical_not(low_side))
+    def _():
+        fix(even_rows, odd_rows)
+
+
+def ready(fine, rows, even_rows, end, jump, coarse, even_c, odd_c):
+    breadth = rows.shape[2]
+    small = end.shape[0]
+    thin = struct(small + 2 * even_c.shape[1], 8, breadth // 4)
+    return pl.pallas_call(
+        ready_kernel,
+        out_shape=[
+            struct(*fine.shape),
+            struct(*end.shape),
+            thin,
+            thin,
+            jax.ShapeDtypeStruct((breadth // 4, breadth), BF16),
+        ],
+        in_specs=[VMEM] * 7 + [ANY],
+        out_specs=[VMEM] * 5,
+        scratch_shapes=[pltpu.SemaphoreType.DMA(())],
+        compiler_params=params(16),
+        name="ready_arrays",
+    )(rows, even_rows, end, jump, coarse, even_c, odd_c, fine)
+
+
 def last_kernel(behind, *refs):
-    before, refs = refs[:behind], refs[behind:]
-    fine_hbm, odd_rows, even_rows, end_ref, jump_ref, even_j, odd_j, coarse_ref, even_c, odd_c, out_hbm = refs[:11]
-    fine_ref, out_ref, one, two, coarse_k, coarse_g, added, change, moved, sems = refs[11:]
+    before, refs = refs[:behind][::-1], refs[behind:]
+    fine_ref, gap_ref, even_j, odd_j, coarse_k, coarse_g, spread_ref, out_hbm = refs[:8]
+    out_ref, one, two, added, change, moved, sems = refs[8:]
     reach = COARSE * behind
     height, breadth = out_hbm.shape[2:]
     columns = breadth // LANES
     small = height // 4
-    fetch = pltpu.make_async_copy(fine_hbm, fine_ref, sems.at[8])
-    fetch.start()
     low_side = parity() == 0
     live = alive()
     edges = masks()
     slice_id = lax.axis_index("tm")
-    fill_coarse(coarse_k, coarse_ref.at[1], even_c.at[0], odd_c.at[0], reach, low_side, live)
-    fill_coarse(coarse_g, coarse_ref.at[2], even_c.at[1], odd_c.at[1], reach, low_side, live)
     at = 0
     for j in range(behind):
         width = reach - COARSE * j
@@ -679,25 +729,8 @@
         coarse_sweep(one, two, coarse_k, coarse_g, base + 1, reach + small + width - 1, reach, small, low_side, live, edges)
         coarse_sweep(two, one, coarse_k, coarse_g, base + 2, reach + small + width - 2, reach, small, low_side, live, edges)
     for r in range(small):
-        change[:, r, :] = (one[reach + r] + jump_ref[r]) - end_ref[r]
-    spread = spread_matrix(breadth)
-    moved[...] = split_dot(change[...].reshape(8 * small, breadth // 4), spread).reshape(8, small, breadth)
-    fetch.wait()
-
-    def fix(low_ref, high_ref):
-        for x in range(columns):
-            for i in range(4):
-                fine_ref[:, x, i, :] = low_ref[i, :, x * LANES : (x + 1) * LANES]
-                fine_ref[:, x, height - 4 + i, :] = high_ref[i, :, x * LANES : (x + 1) * LANES]
-
-    @pl.when(low_side)
-    def _():
-        fix(odd_rows, even_rows)
-
-    @pl.when(jnp.logical_not(low_side))
-    def _():
-        fix(even_rows, odd_rows)
-
+        change[:, r, :] = one[reach + r] + gap_ref[r]
+    moved[...] = split_dot(change[...].reshape(8 * small, breadth // 4), spread_ref[...]).reshape(8, small, breadth)
     lower = lax.broadcasted_iota(jnp.int32, (8, LANES), 0) < 4
 
     def body(z, carry):
@@ -715,26 +748,28 @@
         pltpu.make_async_copy(out_ref.at[z], out_hbm.at[0, z], sems.at[z]).wait()
 
 
-def last(fine, rows, even_rows, end, jump, before, even_j, odd_j, coarse, even_c, odd_c, height):
-    breadth = rows.shape[2]
+def last(before, even_j, odd_j, fine, gap, coarse_k, coarse_g, spread):
+    _, columns, height, _ = fine.shape
+    breadth = columns * LANES
     small = height // 4
-    reach = COARSE * len(before)
-    thin = pltpu.VMEM((small + 2 * reach, 8, breadth // 4), F32)
+    thin = pltpu.VMEM(coarse_k.shape, F32)
     return pl.pallas_call(
         functools.partial(last_kernel, len(before)),
         out_shape=struct(1, 8, height, breadth),
-        in_specs=[VMEM] * len(before) + [ANY] + [VMEM] * 9,
+        in_specs=[VMEM] * (len(before) + 7),
         out_specs=HBM,
-        scratch_shapes=[pltpu.VMEM(fine.shape, F32), pltpu.VMEM((8, height, breadth), F32)]
-        + [thin] * 5
-        + [
+        scratch_shapes=[
+            pltpu.VMEM((8, height, breadth), F32),
+            thin,
+            thin,
+            thin,
             pltpu.VMEM((8, small, breadth // 4), F32),
             pltpu.VMEM((8, small, breadth), F32),
-            pltpu.SemaphoreType.DMA((9,)),
+            pltpu.SemaphoreType.DMA((8,)),
         ],
         compiler_params=params(16),
         name="chain_and_spread",
-    )(*before, fine, rows, even_rows, end, jump, even_j, odd_j, coarse, even_c, odd_c)
+    )(*before[::-1], fine, gap, even_j, odd_j, coarse_k, coarse_g, spread)
 
 
 def relay(jump, coarse, even_c, odd_c, even):
@@ -820,7 +855,7 @@
 
         odd_j = swap_odd(halo(low_side))
         even_j = lax.ppermute(halo(high_side), "space", even)
-        return last(fine, rows, mended, end, jump, before, even_j, odd_j, coarse, even_c, odd_c, height)
+        return last(before, even_j, odd_j, *ready(fine, rows, mended, end, jump, coarse, even_c, odd_c))
     chained = relay(jump, coarse, even_c, odd_c, even)
     change = jnp.repeat(jnp.repeat(jnp.transpose(chained - end, (1, 0, 2)), 4, axis=1), 4, axis=2)
     fixed = jnp.where(low_side, 0, height - 4)

time: 29 us -> 28.7 us (0.990)
  starting transfers between devices: 12.4 us -> 11.5 us
  waiting for transfers between devices: 5.01 us -> 5.55 us
    ppermute x1, starting transfers between devices: 0.93 us -> 0.07 us  [per_device(): even_c = lax.ppermute(rows_for(later, high_side, width), 'space', even)]
    ppermute x3, waiting for transfers between devices: 2.12 us -> 2.97 us  [per_device(): lax.ppermute(jump, 'tm', [(i, (i + k) % slices) for i in range(slices)])]
    ppermute x3, waiting for transfers between devices: 2.86 us -> 2.55 us  [swap_odd(): return lax.ppermute(block, ('tm', 'space'), pairs)]
    pallas_call x0 -> x1, Pallas kernels: none -> 0.3 us  [ready(): pl.pallas_call(ready_kernel, out_shape=[struct(*fine.shape), struct(*end....]
  transfers between devices with their start and end apart: 10 -> 10, of which waited for: 2 -> 2; matrix products, arithmetic and copies ran while one was open for 0% -> 0% of each run, Pallas kernels for 22% -> 23%
where the time goes in v6:
time: 28.7 us; the launch traced here: 28.3 us
  starting transfers between devices  11.5 us (40%)
  Pallas kernels  10.9 us (38%)
  waiting for transfers between devices  5.55 us (19%)
    ppermute x3, starting transfers between devices, per_device(): lax.ppermute(jump, 'tm', [(i, (i + k) % slices) for i in range(slices)])  5.56 us
    ppermute x3, starting transfers between devices, swap_odd(): return lax.ppermute(block, ('tm', 'space'), pairs)  5.25 us
    pallas_call x1, Pallas kernels, inner(): pl.pallas_call(inner_kernel, out_shape=[struct(8, columns, height, LANES)...  4.72 us
    ppermute x3, waiting for transfers between devices, per_device(): lax.ppermute(jump, 'tm', [(i, (i + k) % slices) for i in range(slices)])  2.97 us
    ppermute x3, waiting for transfers between devices, swap_odd(): return lax.ppermute(block, ('tm', 'space'), pairs)  2.55 us
    pallas_call x1, Pallas kernels, last(): pl.pallas_call(functools.partial(last_kernel, len(before)), out_shape=str...  1.91 us
    pallas_call x1, Pallas kernels, odd_pack(): pl.pallas_call(odd_kernel, out_shape=struct(8, 8, breadth), in_specs=[HBM...  1.77 us
    pallas_call x1, Pallas kernels, even_edge(): pl.pallas_call(even_edge_kernel, out_shape=[struct(4, 8, breadth), struct...  1.05 us
  transfers between devices with their start and end apart: 10, of which 2 were waited for; matrix products, arithmetic and copies ran while one was open for 0% of the time, Pallas kernels for 23%

profile of v6, /device:TPU:0, one launch (start us, length us, event | category | flops | bytes accessed | tf_op | source)
XLA Modules:
  0.0 28.3 jit_solution(15170890496030927321)
XLA Ops:
  0.0 0.0 copy-start
  0.0 0.0 copy-start.1
  0.0 0.0 copy-start.2
  0.0 1.8 %odd_rows.1 = f32[8,8,1024]{2,1,0:T(8,128)S(1)} custom-call(f32[1,8,32,1024]{3,2,1,0:T(8,128)} %u_ref.3, bf16[8,32,1024]{2,1,0:T(8,128)(2,1)} %k_ref.3, bf16[8,32,1024]{2,1,0:T(8,128)(2,1)} %g_ref.3), custom_call_target="tpu_custom_call" | custom-call | tf_op jit(solution)/shard_map/odd_rows/pallas_call | solution.py:211
  1.8 3.1 %collective-permute-start.1 = (f32[8,8,1024]{2,1,0:T(8,128)S(1)}, f32[8,8,1024]{2,1,0:T(8,128)S(1)}, u32[]{:S(2)}, u32[]{:S(2)}) collective-permute-start(f32[8,8,1024]{2,1,0:T(8,128)S(1)} %odd_rows.1), channel_id=1, source_target_pairs={{0,8},{1,2},{2,1},{3,4},{4,3},{5,6},{6,5},{7,15},{8,0},{9,10},{10,... | collective-permute-start | bytes 786440 | tf_op jit(solution)/shard_map/ppermute | solution.py:457
  4.9 0.0 copy-done
  4.9 0.0 copy-done.1
  4.9 0.0 copy-done.2
  4.9 0.5 %even_rows.1 = (f32[7,8,1024]{2,1,0:T(8,128)S(1)}, f32[1,8,1024]{2,1,0:T(8,128)S(1)}) custom-call(f32[8,8,1024]{2,1,0:T(8,128)S(1)} %odd_rows.1, f32[1,8,32,1024]{3,2,1,0:T(8,128)S(1)} %copy-done, bf16[8,32,1024]{2,1,0:T(8,128)(2,1)S(1)} %copy-done.1, bf16[8,32,1024]{2,1,0:T(8,128)(2,1)S(1)} %copy-done.2), custom_call_target="tpu_custom_call" | custom-call | tf_op jit(solution)/shard_map/even_rows/pallas_call | solution.py:269
  5.4 0.1 collective-permute-start
  5.5 0.5 %collective-permute-start.2 = (f32[1,8,1024]{2,1,0:T(8,128)S(1)}, f32[1,8,1024]{2,1,0:T(8,128)S(1)}, u32[]{:S(2)}, u32[]{:S(2)}) collective-permute-start(f32[1,8,1024]{2,1,0:T(8,128)S(1)} %get-tuple-element.37), channel_id=1, source_target_pairs={{0,1},{1,0},{2,3},{3,2},{4,5},{5,4},{6,7},{7,6},{8,9},{9,8},{10,11... | collective-permute-start | bytes 98312 | tf_op jit(solution)/shard_map/ppermute | solution.py:837
  6.0 4.7 %inner_updates.1 = (f32[8,8,32,128]{3,2,1,0:T(8,128)S(1)}, f32[6,8,1024]{2,1,0:T(8,128)S(1)}, f32[6,8,1024]{2,1,0:T(8,128)S(1)}, f32[3,8,8,256]{3,2,1,0:T(8,128)S(1)}, f32[8,8,256]{2,1,0:T(8,128)S(1)}) custom-call(f32[1,8,32,1024]{3,2,1,0:T(8,128)S(1)} %copy-done, bf16[8,32,1024]{2,1,0:T(8,128)(2,1)S(1)} %copy-done.1, bf16[8,32,1024]{2,1,0:T(8,128)(2,1)S(1)} %copy-done.2), custom_call_target="tpu_custom_call" | custom-call | flops 30000000 | bytes 4000000 | tf_op jit(solution)/shard_map/inner_updates/pallas_call | solution.py:410
  10.8 0.0 collective-permute-done.got_ref
  10.8 1.0 %even_edge.1 = (f32[4,8,1024]{2,1,0:T(8,128)S(1)}, f32[8,8,256]{2,1,0:T(8,128)S(1)}, f32[5,8,1024]{2,1,0:T(8,128)S(1)}, f32[5,8,1024]{2,1,0:T(8,128)S(1)}, f32[5...) custom-call(f32[1,8,32,1024]{3,2,1,0:T(8,128)S(1)} %copy-done, bf16[8,32,1024]{2,1,0:T(8,128)(2,1)S(1)} %copy-done.1, ...), custom_call_target="tpu_custom_call" | custom-call | tf_op jit(solution)/shard_map/even_edge/pallas_call | solution.py:543
  11.8 0.0 collective-permute-done.2.even_ref
  11.8 0.0 collective-permute-done.1.got_ref
  11.9 0.7 %edge_updates.1 = (f32[4,8,1024]{2,1,0:T(8,128)S(1)}, f32[8,8,256]{2,1,0:T(8,128)S(1)}, f32[8,8,256]{2,1,0:T(8,128)S(1)}) custom-call(f32[5,8,1024]{2,1,0:T(8,128)S(1)} %get-tuple-element.33.outer_ref, f32[5,8,1024]{2,1,0:T(8,128)S(1)} %get-tuple-element.34.outer_a, f32[5,8,1024]{2,1,0:T(8,128)S(1)} %get-tuple-element.35.outer_b, ...), custom_call_target="tpu_custom_call" | custom-call | tf_op jit(solution)/shard_map/edge_updates/pallas_call | solution.py:631
  12.5 1.2 %collective-permute-start.3 = (f32[8,8,256]{2,1,0:T(8,128)S(1)}, f32[8,8,256]{2,1,0:T(8,128)S(1)}, u32[]{:S(2)}, u32[]{:S(2)}) collective-permute-start(f32[8,8,256]{2,1,0:T(8,128)S(1)} %get-tuple-element.40.jump_ref), channel_id=1, source_target_pairs={{0,8},{8,16},{16,24},{24,0},{1,9},{9,17},{17,25},{25,1},{2,10},{10... | collective-permute-start | bytes 196616 | tf_op jit(solution)/shard_map/ppermute | solution.py:847
  13.7 2.6 %collective-permute-start.4 = (f32[8,8,256]{2,1,0:T(8,128)S(1)}, f32[8,8,256]{2,1,0:T(8,128)S(1)}, u32[]{:S(2)}, u32[]{:S(2)}) collective-permute-start(f32[8,8,256]{2,1,0:T(8,128)S(1)} %get-tuple-element.40.jump_ref), channel_id=1, source_target_pairs={{0,16},{8,24},{16,0},{24,8},{1,17},{9,25},{17,1},{25,9},{2,18},{10... | collective-permute-start | bytes 196616 | tf_op jit(solution)/shard_map/ppermute | solution.py:847
  16.3 1.7 %collective-permute-start.5 = (f32[8,8,256]{2,1,0:T(8,128)S(1)}, f32[8,8,256]{2,1,0:T(8,128)S(1)}, u32[]{:S(2)}, u32[]{:S(2)}) collective-permute-start(f32[8,8,256]{2,1,0:T(8,128)S(1)} %get-tuple-element.40.jump_ref), channel_id=1, source_target_pairs={{0,24},{8,0},{16,8},{24,16},{1,25},{9,1},{17,9},{25,17},{2,26},{10... | collective-permute-start | bytes 196616 | tf_op jit(solution)/shard_map/ppermute | solution.py:847
  18.1 0.1 collective-permute-start.6
  18.2 0.4 %collective-permute-start.7 = (f32[2,6,8,256]{3,2,1,0:T(8,128)S(1)}, f32[2,6,8,256]{3,2,1,0:T(8,128)S(1)}, u32[]{:S(2)}, u32[]{:S(2)}) collective-permute-start(f32[2,6,8,256]{3,2,1,0:T(8,128)S(1)} %get-tuple-element.51), channel_id=1, source_target_pairs={{0,8},{1,2},{2,1},{3,4},{4,3},{5,6},{6,5},{7,15},{8,0},{9,10},{10,... | collective-permute-start | bytes 294920 | tf_op jit(solution)/shard_map/ppermute | solution.py:457
  18.5 3.0 %collective-permute-done.5.refs_2_ = f32[8,8,256]{2,1,0:T(8,128)S(1)} collective-permute-done((f32[8,8,256]{2,1,0:T(8,128)S(1)}, f32[8,8,256]{2,1,0:T(8,128)S(1)}, u32[]{:S(2)}, u32[]{:S(2)}) %collective-permute-start.5) | collective-permute-done | bytes 65568 | tf_op jit(solution)/shard_map/ppermute | solution.py:847
  21.5 0.0 collective-permute-done.3.refs_0_
  21.5 0.0 collective-permute-done.4.refs_1_
  21.6 0.1 collective-permute-start.8
  21.7 1.8 %collective-permute-start.9 = (f32[12,8,256]{2,1,0:T(8,128)S(1)}, f32[12,8,256]{2,1,0:T(8,128)S(1)}, u32[]{:S(2)}, u32[]{:S(2)}) collective-permute-start(f32[12,8,256]{2,1,0:T(8,128)S(1)} %pad_maximum_fusion.1), channel_id=1, source_target_pairs={{0,8},{1,2},{2,1},{3,4},{4,3},{5,6},{6,5},{7,15},{8,0},{9,10},{10,... | collective-permute-start | bytes 294920 | tf_op jit(solution)/shard_map/ppermute | solution.py:457
  23.5 0.0 collective-permute-done.6.even_c
  23.5 0.0 collective-permute-done.7.odd_c
  23.5 0.3 %ready_arrays.1 = (f32[8,8,32,128]{3,2,1,0:T(8,128)S(1)}, f32[8,8,256]{2,1,0:T(8,128)S(1)}, f32[20,8,256]{2,1,0:T(8,128)S(1)}, f32[20,8,256]{2,1,0:T(8,128)S(1)}, bf16[256,1024]{1,0:T(8,128)(2,1)S(1)}) custom-call(f32[4,8,1024]{2,1,0:T(8,128)S(1)} %get-tuple-element.41.odd_rows, f32[4,8,1024]{2,1,0:T(8,128)S(1)} %get-tuple-element.42.even_rows, ...), custom_call_target="tpu_custom_call" | custom-call | tf_op jit(solution)/shard_map/ready_arrays/pallas_call | solution.py:683
  23.8 0.0 collective-permute-done.8.refs_5_
  23.8 2.5 %collective-permute-done.9.refs_6_ = f32[12,8,256]{2,1,0:T(8,128)S(1)} collective-permute-done((f32[12,8,256]{2,1,0:T(8,128)S(1)}, f32[12,8,256]{2,1,0:T(8,128)S(1)}, u32[]{:S(2)}, u32[]{:S(2)}) %collective-permute-start.9) | collective-permute-done | bytes 98336 | tf_op jit(solution)/shard_map/ppermute | solution.py:457
  26.4 1.9 %chain_and_spread.1 = f32[1,8,32,1024]{3,2,1,0:T(8,128)} custom-call(f32[8,8,256]{2,1,0:T(8,128)S(1)} %collective-permute-done.3.refs_0_, f32[8,8,256]{2,1,0:T(8,128)S(1)} %collective-permute-done.4.refs_1_, f32[8,8,256]{2,1,0:T(8,128)S(1)} %collective-permute-done.5.refs_2_, f32[8,8,32,128]{3,2,1,0:T(8,128)S(1)} %get-tuple-element.46.refs_3_, ...), custom_call_target="tpu_custom_call" | custom-call | tf_op jit(solution)/shard_map/chain_and_spread/pallas_call | solution.py:756
  (7 shorter events, 0.1 us)
Async XLA Ops:
  0.0 4.9 %copy-start = (f32[1,8,32,1024]{3,2,1,0:T(8,128)S(1)}, f32[1,8,32,1024]{3,2,1,0:T(8,128)}, u32[]{:S(2)}) copy-start(f32[1,8,32,1024]{3,2,1,0:T(8,128)} %u_ref.3) | copy-start | bytes 3145732
  0.0 4.9 %copy-start.1 = (bf16[8,32,1024]{2,1,0:T(8,128)(2,1)S(1)}, bf16[8,32,1024]{2,1,0:T(8,128)(2,1)}, u32[]{:S(2)}) copy-start(bf16[8,32,1024]{2,1,0:T(8,128)(2,1)} %k_ref.3) | copy-start | bytes 1572868
  0.0 4.9 %copy-start.2 = (bf16[8,32,1024]{2,1,0:T(8,128)(2,1)S(1)}, bf16[8,32,1024]{2,1,0:T(8,128)(2,1)}, u32[]{:S(2)}) copy-start(bf16[8,32,1024]{2,1,0:T(8,128)(2,1)} %g_ref.3) | copy-start | bytes 1572868
  1.8 10.1 %collective-permute-start.1 = (f32[8,8,1024]{2,1,0:T(8,128)S(1)}, f32[8,8,1024]{2,1,0:T(8,128)S(1)}, u32[]{:S(2)}, u32[]{:S(2)}) collective-permute-start(f32[8,8,1024]{2,1,0:T(8,128)S(1)} %odd_rows.1), channel_id=1, source_target_pairs={{0,8},{1,2},{2,1},{3,4},{4,3},{5,6},{6,5},{7,15},{8,0},{9,10},{10,... | collective-permute-start | bytes 786440 | tf_op jit(solution)/shard_map/ppermute | solution.py:457
  5.4 5.3 %collective-permute-start = (f32[7,8,1024]{2,1,0:T(8,128)S(1)}, f32[7,8,1024]{2,1,0:T(8,128)S(1)}, u32[]{:S(2)}, u32[]{:S(2)}) collective-permute-start(f32[7,8,1024]{2,1,0:T(8,128)S(1)} %get-tuple-element.31), channel_id=1, source_target_pairs={{0,1},{1,0},{2,3},{3,2},{4,5},{5,4},{6,7},{7,6},{8,9},{9,8},{10,11... | collective-permute-start | bytes 688136 | tf_op jit(solution)/shard_map/ppermute | solution.py:836
  5.5 6.3 %collective-permute-start.2 = (f32[1,8,1024]{2,1,0:T(8,128)S(1)}, f32[1,8,1024]{2,1,0:T(8,128)S(1)}, u32[]{:S(2)}, u32[]{:S(2)}) collective-permute-start(f32[1,8,1024]{2,1,0:T(8,128)S(1)} %get-tuple-element.37), channel_id=1, source_target_pairs={{0,1},{1,0},{2,3},{3,2},{4,5},{5,4},{6,7},{7,6},{8,9},{9,8},{10,11... | collective-permute-start | bytes 98312 | tf_op jit(solution)/shard_map/ppermute | solution.py:837
  12.5 9.0 %collective-permute-start.3 = (f32[8,8,256]{2,1,0:T(8,128)S(1)}, f32[8,8,256]{2,1,0:T(8,128)S(1)}, u32[]{:S(2)}, u32[]{:S(2)}) collective-permute-start(f32[8,8,256]{2,1,0:T(8,128)S(1)} %get-tuple-element.40.jump_ref), channel_id=1, source_target_pairs={{0,8},{8,16},{16,24},{24,0},{1,9},{9,17},{17,25},{25,1},{2,10},{10... | collective-permute-start | bytes 196616 | tf_op jit(solution)/shard_map/ppermute | solution.py:847
  13.7 7.8 %collective-permute-start.4 = (f32[8,8,256]{2,1,0:T(8,128)S(1)}, f32[8,8,256]{2,1,0:T(8,128)S(1)}, u32[]{:S(2)}, u32[]{:S(2)}) collective-permute-start(f32[8,8,256]{2,1,0:T(8,128)S(1)} %get-tuple-element.40.jump_ref), channel_id=1, source_target_pairs={{0,16},{8,24},{16,0},{24,8},{1,17},{9,25},{17,1},{25,9},{2,18},{10... | collective-permute-start | bytes 196616 | tf_op jit(solution)/shard_map/ppermute | solution.py:847
  16.3 5.2 %collective-permute-start.5 = (f32[8,8,256]{2,1,0:T(8,128)S(1)}, f32[8,8,256]{2,1,0:T(8,128)S(1)}, u32[]{:S(2)}, u32[]{:S(2)}) collective-permute-start(f32[8,8,256]{2,1,0:T(8,128)S(1)} %get-tuple-element.40.jump_ref), channel_id=1, source_target_pairs={{0,24},{8,0},{16,8},{24,16},{1,25},{9,1},{17,9},{25,17},{2,26},{10... | collective-permute-start | bytes 196616 | tf_op jit(solution)/shard_map/ppermute | solution.py:847
  18.1 5.4 %collective-permute-start.6 = (f32[2,6,8,256]{3,2,1,0:T(8,128)S(1)}, f32[2,6,8,256]{3,2,1,0:T(8,128)S(1)}, u32[]{:S(2)}, u32[]{:S(2)}) collective-permute-start(f32[2,6,8,256]{3,2,1,0:T(8,128)S(1)} %get-tuple-element.52), channel_id=1, source_target_pairs={{0,1},{1,0},{2,3},{3,2},{4,5},{5,4},{6,7},{7,6},{8,9},{9,8},{10,11... | collective-permute-start | bytes 294920 | tf_op jit(solution)/shard_map/ppermute | solution.py:844
  18.2 5.3 %collective-permute-start.7 = (f32[2,6,8,256]{3,2,1,0:T(8,128)S(1)}, f32[2,6,8,256]{3,2,1,0:T(8,128)S(1)}, u32[]{:S(2)}, u32[]{:S(2)}) collective-permute-start(f32[2,6,8,256]{3,2,1,0:T(8,128)S(1)} %get-tuple-element.51), channel_id=1, source_target_pairs={{0,8},{1,2},{2,1},{3,4},{4,3},{5,6},{6,5},{7,15},{8,0},{9,10},{10,... | collective-permute-start | bytes 294920 | tf_op jit(solution)/shard_map/ppermute | solution.py:457
  21.6 2.2 %collective-permute-start.8 = (f32[12,8,256]{2,1,0:T(8,128)S(1)}, f32[12,8,256]{2,1,0:T(8,128)S(1)}, u32[]{:S(2)}, u32[]{:S(2)}) collective-permute-start(f32[12,8,256]{2,1,0:T(8,128)S(1)} %pad_maximum_fusion), channel_id=1, source_target_pairs={{0,1},{1,0},{2,3},{3,2},{4,5},{5,4},{6,7},{7,6},{8,9},{9,8},{10,11... | collective-permute-start | bytes 294920 | tf_op jit(solution)/shard_map/ppermute | solution.py:857
  21.7 4.7 %collective-permute-start.9 = (f32[12,8,256]{2,1,0:T(8,128)S(1)}, f32[12,8,256]{2,1,0:T(8,128)S(1)}, u32[]{:S(2)}, u32[]{:S(2)}) collective-permute-start(f32[12,8,256]{2,1,0:T(8,128)S(1)} %pad_maximum_fusion.1), channel_id=1, source_target_pairs={{0,8},{1,2},{2,1},{3,4},{4,3},{5,6},{6,5},{7,15},{8,0},{9,10},{10,... | collective-permute-start | bytes 294920 | tf_op jit(solution)/shard_map/ppermute | solution.py:457
